TPU v7x, 128 devices: a whole 4x4x4 slice. The times are simulated.
128 devices in a mesh: dp: 4 (over y), shard: 32 (over z, x, core).
Axes of the slice: x: 4, y: 4, z: 4, core: 2. Of those that a mesh axis runs over, the one named last changes fastest.
Arguments:
- grads: bfloat16 [4, 64, 1024, 1024], P('dp', None, 'shard'), may hold values from -6 to 6
- params: bfloat16 [64, 1024, 1024], P(None, 'shard'), may hold values from -6 to 6
- stats: float32 [4, 32, 1024, 1024], P('dp', 'shard'), may hold values from -1 to 17, as said below
- roots: float32 [4, 32, 1024, 1024], P('dp', 'shard'), may hold values from -1 to 2, as said below
- table: int32 [4, 16], replicated, may hold values from 0 to 15, each once within a row
Outputs:
- new_params: bfloat16 [64, 1024, 1024], P(None, 'shard')
- new_stats: float32 [4, 32, 1024, 1024], P('dp', 'shard')
Inputs may be any that keep to these rules, and one draw needn't show every extreme that they name: Each row of table names each of the 16 blocks of its group once. Every matrix stats[d, s] is symmetric. Every matrix roots[d, s] is symmetric.
All inputs are finite; a program needn't handle non-finite values.
Results may differ from a plain program's by a relative error of at most 0.0085.
Values may be sent and summed in bfloat16 or wider, within the bound.
No kernel may reach another device: no remote copies, remote signals or barrier semaphores. Data moves between devices by JAX's collectives and lax.ppermute only.
A program may use at most 128 MiB of HBM per device.

v0:
```python
import jax
import jax.numpy as jnp
from jax import lax
from jax.sharding import PartitionSpec as P

keep_rate = 0.75
step_size = 0.25


def swapped(block, axis, stride):
    count = lax.axis_size(axis)
    route = []
    for low in range(count):
        high = low | 1 << stride
        if high != low and high < count:
            route += [(low, high), (high, low)]
    return lax.ppermute(block, axis, route)


def on_device(grads, params, stats, roots, table):
    shards = lax.axis_size("shard")
    replicas = lax.axis_size("dp")
    blocks = grads.shape[1]
    row_blocks = blocks // replicas
    block_size = grads.shape[3]
    row_slice = grads.shape[2]
    halfway = block_size // 2
    replica = lax.axis_index("dp")
    position = lax.axis_index("shard")
    parity = position % 2
    owned_blocks = lax.dynamic_index_in_dim(table, replica, 0, keepdims=False)
    summed = lax.psum_scatter(
        grads[0].astype(jnp.float32).astype(jnp.bfloat16), "dp", scatter_dimension=0, tiled=True
    )
    targets = jnp.repeat(owned_blocks, 2)
    outgoing = jnp.take(summed, targets, axis=0)
    arrived = lax.all_to_all(outgoing, "shard", split_axis=0, concat_axis=1, tiled=True)
    gradient = arrived[0]
    oriented = jnp.where(parity == 0, gradient, gradient.T)
    outer_product = jnp.dot(oriented, oriented.T, preferred_element_type=jnp.float32)
    new_stat = keep_rate * stats[0, 0] + (1.0 - keep_rate) / block_size * outer_product
    inverse_root = roots[0, 0]
    first = jnp.dot(inverse_root, oriented.astype(jnp.float32), precision=lax.Precision.HIGHEST)
    partner_first = swapped(first.astype(jnp.bfloat16), "shard", 0).astype(first.dtype)
    complete = jnp.dot(inverse_root, partner_first.T, precision=lax.Precision.HIGHEST)
    update = jnp.where(parity == 0, complete, complete.T)
    my_part = lax.dynamic_slice_in_dim(update, parity * halfway, halfway, 1)
    returned = lax.all_to_all(
        my_part.reshape(shards, row_slice, halfway).astype(jnp.bfloat16),
        "shard",
        split_axis=0,
        concat_axis=0,
        tiled=True,
    ).astype(jnp.float32)
    pieces = (
        returned.reshape(shards // 2, 2, row_slice, halfway)
        .transpose(0, 2, 1, 3)
        .reshape(shards // 2, row_slice, block_size)
    )
    placement_order = jnp.argsort(owned_blocks)
    block_updates = jnp.take(pieces, placement_order, axis=0)
    my_params = lax.dynamic_slice_in_dim(params, replica * row_blocks, row_blocks, 0)
    updated = (my_params.astype(jnp.float32) - step_size * block_updates).astype(jnp.bfloat16)
    new_params = lax.all_gather(updated, "dp", axis=0, tiled=True)
    return (new_params, new_stat[None, None])


def solution(mesh):
    placed = (
        P("dp", None, "shard", None),
        P(None, "shard", None),
        P("dp", "shard", None, None),
        P("dp", "shard", None, None),
        P(),
    )
    return jax.shard_map(
        on_device,
        mesh=mesh,
        in_specs=placed,
        out_specs=(P(None, "shard", None), P("dp", "shard", None, None)),
        check_vma=False,
    )
```

profile of v0, /device:TPU:1, one launch (start us, length us, event | category | flops | bytes accessed | tf_op | source)
XLA Modules:
  0.0 220.1 jit_solution(6480385388320295420)
XLA Ops:
  7.2 0.0 copy-start
  7.2 0.0 reduce-scatter.2.cloned.1.call-start
  7.2 0.7 reduce-scatter.2.cloned.1.call-update
  7.9 0.0 copy-done
  7.9 0.1 broadcast_in_dim.29
  8.0 0.1 reshape.67
  8.1 0.1 reshape.66
  8.2 52.3 %reduce-scatter.2.cloned.1.call-done = bf16[16,32,1024]{2,1,0:T(8,128)(2,1)} async-done(((bf16[64,32,1024]{2,1,0:T(8,128)(2,1)}), bf16[16,32,1024]{2,1,0:T(8,128)(2,1)}) %reduce-scatter.2.cloned.1.call-update) | async-done | bytes 1048592 | tf_op jit(solution)/shard_map/reduce_scatter | solution.py:32
  60.5 1.9 gather_fusion
  62.4 1.6 broadcast_select_fusion
  64.0 7.6 %all-to-all-start = ((bf16[32,32,1024]{2,1,0:T(8,128)(2,1)}), bf16[32,32,1024]{2,1,0:T(8,128)(2,1)S(1)}, u32[]{:S(2)}, u32[]{:S(2)}) async-start(bf16[32,32,1024]{2,1,0:T(8,128)(2,1)} %broadcast_select_fusion), calls=%async_computation.1 | async-start | bytes 4194304 | tf_op jit(solution)/shard_map/all_to_all | solution.py:37
  71.7 27.8 %all-to-all-done = bf16[32,32,1024]{2,1,0:T(8,128)(2,1)S(1)} async-done(((bf16[32,32,1024]{2,1,0:T(8,128)(2,1)}), bf16[32,32,1024]{2,1,0:T(8,128)(2,1)S(1)}, u32[]{:S(2)}, u32[]{:S(2)}) %all-to-all-start) | async-done | bytes 2097184 | tf_op jit(solution)/shard_map/all_to_all | solution.py:37
  99.5 2.6 %copy.15 = bf16[1024,1024]{0,1:T(8,128)(2,1)} copy(bf16[1024,1024]{1,0:T(8,128)(2,1)S(1)} %bitcast.34) | data formatting | bytes 4194304 | tf_op jit(solution)/shard_map/squeeze | solution.py:38
  102.1 0.0 copy-done.1
  102.1 11.5 %convert_bitcast_fusion.1 = bf16[1024,1024]{0,1:T(8,128)(2,1)} fusion(f32[1,1,1024,1024]{3,2,1,0:T(8,128)} %param.8, bf16[1024,1024]{1,0:T(8,128)(2,1)S(1)} %bitcast.35, bf16[1024,1024]{0,1:T(8,128)(2,1)} %copy.15, pred[]{:T(512)S(6)} %eq.6), kind=kOutput, calls=%fused_computation.13 | convolution fusion | flops 12886999040 | bytes 10485761 | tf_op jit(solution)/shard_map/dot_general | solution.py:43
  113.7 2.4 %collective-permute-start = (bf16[1024,1024]{0,1:T(8,128)(2,1)}, bf16[1024,1024]{0,1:T(8,128)(2,1)}, u32[]{:S(2)}, u32[]{:S(2)}) collective-permute-start(bf16[1024,1024]{0,1:T(8,128)(2,1)} %convert_bitcast_fusion.1), channel_id=1, source_target_pairs={{0,1},{1,0},{2,3},{3,2},{4,5},{5,4},{6,7},{7,6},{8,9},{9,8},{10,11... | collective-permute-start | bytes 6291464 | tf_op jit(solution)/shard_map/ppermute | solution.py:17
  116.0 4.1 %collective-permute-done = bf16[1024,1024]{0,1:T(8,128)(2,1)} collective-permute-done((bf16[1024,1024]{0,1:T(8,128)(2,1)}, bf16[1024,1024]{0,1:T(8,128)(2,1)}, u32[]{:S(2)}, u32[]{:S(2)}) %collective-permute-start) | collective-permute-done | bytes 2097184 | tf_op jit(solution)/shard_map/ppermute | solution.py:17
  120.2 10.4 %fusion.1 = bf16[1024,1024]{1,0:T(8,128)(2,1)S(1)} fusion(bf16[1024,1024]{0,1:T(8,128)(2,1)} %collective-permute-done, f32[1,1,1024,1024]{3,2,1,0:T(8,128)} %param.8), kind=kOutput, calls=%fused_computation.4 | convolution fusion | flops 12884901888 | bytes 8388608 | tf_op jit(solution)/shard_map/dot_general | solution.py:45
  130.6 2.6 %copy.16 = bf16[1024,1024]{0,1:T(8,128)(2,1)} copy(bf16[1024,1024]{1,0:T(8,128)(2,1)S(1)} %fusion.1) | data formatting | bytes 4194304 | tf_op jit(solution)/shard_map/dot_general | solution.py:45
  133.2 2.6 %fusion.5 = bf16[1024,512]{1,0:T(8,128)(2,1)} fusion(bf16[1024,1024]{1,0:T(8,128)(2,1)S(1)} %fusion.1, s32[]{:T(128)S(6)} %select_n.70, bf16[1024,1024]{1,0:T(8,128)(2,1)} %bitcast.38, pred[]{:T(512)S(6)} %eq.6), kind=kLoop, calls=%fused_computation.9 | loop fusion | flops 524288 | bytes 3145733 | tf_op jit(solution)/shard_map/convert_element_type | solution.py:49
  135.8 4.1 %all-to-all-start.1 = ((bf16[32,32,512]{2,1,0:T(8,128)(2,1)}), bf16[32,32,512]{2,1,0:T(8,128)(2,1)S(1)}, u32[]{:S(2)}, u32[]{:S(2)}) async-start(bf16[32,32,512]{2,1,0:T(8,128)(2,1)} %bitcast.8), calls=%async_computation.2 | async-start | bytes 2097152 | tf_op jit(solution)/shard_map/all_to_all | solution.py:48
  139.9 0.0 all-gather.2.cloned.1.call-start
  140.0 1.2 sort.17
  141.2 16.0 %all-to-all-done.1 = bf16[32,32,512]{2,1,0:T(8,128)(2,1)S(1)} async-done(((bf16[32,32,512]{2,1,0:T(8,128)(2,1)}), bf16[32,32,512]{2,1,0:T(8,128)(2,1)S(1)}, u32[]{:S(2)}, u32[]{:S(2)}) %all-to-all-start.1) | async-done | bytes 1048608 | tf_op jit(solution)/shard_map/all_to_all | solution.py:48
  157.2 0.3 convert_bitcast_fusion
  157.5 1.5 copy.18
  159.0 2.3 %gather_fusion.1 = f32[16,32,1024]{2,1,0:T(8,128)S(1)} fusion(f32[16,32,1024]{2,1,0:T(8,128)} %bitcast.37, s32[1024]{0:T(1024)S(1)} %pad_clamp_fusion), kind=kCustom, calls=%fused_computation.1 | custom fusion | bytes 4194368 | tf_op jit(solution)/shard_map/jit(_take)/gather | solution.py:61
  161.3 2.7 %subtract_convert_fusion = bf16[16,32,1024]{2,1,0:T(8,128)(2,1)} fusion(f32[16,32,1024]{2,1,0:T(8,128)S(1)} %gather_fusion.1, bf16[64,32,1024]{2,1,0:T(8,128)(2,1)} %param.6, s32[]{:T(128)S(6)} %select_n.60, pred[16]{0:T(512)(128)(4,1)S(1)} %compare_and_fusion.1), kind=kLoop, calls=%fused_computation.12 | loop fusion | flops 2621440 | bytes 4194324 | tf_op jit(solution)/shard_map/convert_element_type | solution.py:63
  164.0 0.0 all-gather.2.cloned.1.call-update
  164.0 7.9 %fusion = f32[1,1,1024,1024]{3,2,1,0:T(8,128)} fusion(f32[1,1,1024,1024]{3,2,1,0:T(8,128)} %param.7, bf16[1024,1024]{1,0:T(8,128)(2,1)} %bitcast.36, bf16[1024,1024]{0,1:T(8,128)(2,1)} %copy.15, pred[]{:T(512)S(6)} %eq.6), kind=kOutput, calls=%fused_computation.3 | convolution fusion | flops 2151677952 | bytes 12582913 | tf_op jit(solution)/shard_map/dot_general | solution.py:40
  171.9 36.3 %all-gather.2.cloned.1.call-done = bf16[64,32,1024]{2,1,0:T(8,128)(2,1)} async-done(((bf16[16,32,1024]{2,1,0:T(8,128)(2,1)}), bf16[64,32,1024]{2,1,0:T(8,128)(2,1)}) %all-gather.2.cloned.1.call-update) | async-done | bytes 4194320 | tf_op jit(solution)/shard_map/all_gather | solution.py:64
  208.2 5.0 %copy.20 = bf16[64,32,1024]{2,1,0:T(8,128)(2,1)} copy(bf16[64,32,1024]{2,1,0:T(8,128)(2,1)} %all-gather.2.cloned.1.call-done) | data formatting | bytes 8388608
  (9 shorter events, 0.1 us)
Async XLA Ops:
  7.2 0.8 copy-start
  7.2 53.4 %reduce-scatter.2.cloned.1.call-start = ((), (), s32[]{:S(2)}) async-start(), calls=%async_computation.3 | async-start | bytes 5242880 | tf_op jit(solution)/shard_map/reduce_scatter | solution.py:32
  64.0 35.5 %all-to-all-start = ((bf16[32,32,1024]{2,1,0:T(8,128)(2,1)}), bf16[32,32,1024]{2,1,0:T(8,128)(2,1)S(1)}, u32[]{:S(2)}, u32[]{:S(2)}) async-start(bf16[32,32,1024]{2,1,0:T(8,128)(2,1)} %broadcast_select_fusion), calls=%async_computation.1 | async-start | bytes 4194304 | tf_op jit(solution)/shard_map/all_to_all | solution.py:37
  99.5 2.6 %copy-start.1 = (bf16[32,32,1024]{2,1,0:T(8,128)(2,1)}, bf16[32,32,1024]{2,1,0:T(8,128)(2,1)S(1)}, u32[]{:S(2)}) copy-start(bf16[32,32,1024]{2,1,0:T(8,128)(2,1)S(1)} %all-to-all-done) | copy-start | bytes 6291460
  113.7 6.5 %collective-permute-start = (bf16[1024,1024]{0,1:T(8,128)(2,1)}, bf16[1024,1024]{0,1:T(8,128)(2,1)}, u32[]{:S(2)}, u32[]{:S(2)}) collective-permute-start(bf16[1024,1024]{0,1:T(8,128)(2,1)} %convert_bitcast_fusion.1), channel_id=1, source_target_pairs={{0,1},{1,0},{2,3},{3,2},{4,5},{5,4},{6,7},{7,6},{8,9},{9,8},{10,11... | collective-permute-start | bytes 6291464 | tf_op jit(solution)/shard_map/ppermute | solution.py:17
  135.8 21.4 %all-to-all-start.1 = ((bf16[32,32,512]{2,1,0:T(8,128)(2,1)}), bf16[32,32,512]{2,1,0:T(8,128)(2,1)S(1)}, u32[]{:S(2)}, u32[]{:S(2)}) async-start(bf16[32,32,512]{2,1,0:T(8,128)(2,1)} %bitcast.8), calls=%async_computation.2 | async-start | bytes 2097152 | tf_op jit(solution)/shard_map/all_to_all | solution.py:48
  139.9 68.3 %all-gather.2.cloned.1.call-start = ((), (), s32[]{:S(2)}) async-start(), calls=%async_computation.4 | async-start | bytes 5242880 | tf_op jit(solution)/shard_map/all_gather | solution.py:64
Sparse Core Ops, SparseCore 0:
  10.4 50.0 reduce-scatter.1
  164.1 44.0 all-gather.1
where the time goes:
time: 221 us; the launch traced here: 220 us
  waiting for transfers between devices  137 us (62%)
  matrix products  29.8 us (13%)
  local copies, waits for them, and re-layouts  16.2 us (7%)
  starting transfers between devices  14.2 us (6%)
  between operations  14.2 us (6%)
  other arithmetic  8.43 us (4%)
    reduce_scatter x1, waiting for transfers between devices, on_device(): lax.psum_scatter(grads[0].astype(jnp.float32).astype(jnp.bfloat16), 'dp',...  52.3 us
    all_gather x1, waiting for transfers between devices, on_device(): new_params = lax.all_gather(updated, 'dp', axis=0, tiled=True)  36.3 us
    all_to_all x1, waiting for transfers between devices, on_device(): lax.all_to_all(outgoing, 'shard', split_axis=0, concat_axis=1, tiled=True)  27.8 us
    all_to_all x1, waiting for transfers between devices, on_device(): lax.all_to_all(my_part.reshape(shards, row_slice, halfway).astype(jnp.bfl...  16 us
    dot_general x1, matrix products, on_device(): jnp.dot(inverse_root, oriented.astype(jnp.float32), precision=lax.Precisi...  11.5 us
    dot_general x1, matrix products, on_device(): jnp.dot(inverse_root, partner_first.T, precision=lax.Precision.HIGHEST)  10.4 us
    dot_general x1, matrix products, on_device(): jnp.dot(oriented, oriented.T, preferred_element_type=jnp.float32)  7.86 us
    all_to_all x1, starting transfers between devices, on_device(): lax.all_to_all(outgoing, 'shard', split_axis=0, concat_axis=1, tiled=True)  7.62 us
  transfers between devices with their start and end apart: 5, of which 5 were waited for; matrix products, arithmetic and copies ran while one was open for 4% of the time, Pallas kernels for 0%

commit v1 on v0

v1 whole, which is shorter than its diff:
```python
import jax
import jax.numpy as jnp
from jax import lax
from jax.sharding import PartitionSpec as P

keep_rate = 0.75
step_size = 0.25
f32 = jnp.float32
bf16 = jnp.bfloat16


def shifted(block, axis, offset):
    count = lax.axis_size(axis)
    return lax.ppermute(block, axis, [(i, (i + offset) % count) for i in range(count)])


def other_core(block):
    count = lax.axis_size("shard")
    return lax.ppermute(block, "shard", [(i, i ^ 1) for i in range(count)])


def exchanged(blocks):
    return lax.all_to_all(blocks, "shard", split_axis=0, concat_axis=0, tiled=True)


def picked(array, index):
    return array.at[index].get(mode="promise_in_bounds")


def added(*terms):
    total = terms[0].astype(f32)
    for term in terms[1:]:
        total = total + term.astype(f32)
    return total.astype(bf16)


def in_order(values, after):
    held = lax.optimization_barrier(tuple(values) + tuple(after))
    return held[: len(values)]


def on_device(grads, params, stats, roots, table):
    shards = lax.axis_size("shard")
    replicas = lax.axis_size("dp")
    blocks = grads.shape[1]
    group = blocks // replicas
    rows = grads.shape[2]
    size = grads.shape[3]
    half_rows = rows // 2
    half = group // 2
    replica = lax.axis_index("dp")
    core = lax.axis_index("shard") % 2
    own_order = lax.dynamic_index_in_dim(table, replica, 0, keepdims=False)
    places = jnp.arange(group, dtype=table.dtype)
    own_inverse = jnp.sum(
        jnp.where(own_order[None, :] == places[:, None], places[None, :], 0), axis=1
    )
    mine = grads[0]

    def piece(step, which):
        start = (replica + step) % replicas * group + which * half
        return lax.dynamic_slice_in_dim(mine, start, half, 0)

    far = (piece(2, 0), piece(2, 1))
    near = in_order((piece(1, 1), piece(3, 0)), far)
    far_up = shifted(far[0], "dp", 1)
    far_down = shifted(far[1], "dp", -1)
    near_up = shifted(near[0], "dp", 1)
    near_down = shifted(near[1], "dp", -1)

    root = in_order((roots[0, 0],), near)[0].astype(bf16)
    partner_root = other_core(root)
    tall = (shards, 2, half_rows, size)
    left_rows = jnp.where(
        core == 0, root.reshape(tall)[:, 0], partner_root.reshape(tall)[:, 1]
    ).reshape(size // 2, size)
    right = jnp.where(core == 0, partner_root, root)

    sums = (added(piece(1, 0), far_up), added(piece(3, 1), far_down))
    sum_up = shifted(sums[0], "dp", 1)
    sum_down = shifted(sums[1], "dp", -1)
    low = added(piece(0, 0), near_down, sum_up)
    high = added(piece(0, 1), near_up, sum_down)
    whole = picked(jnp.concatenate([low, high]), own_order)
    whole, left_rows, right = lax.optimization_barrier((whole, left_rows, right))

    own_rows = exchanged(whole.reshape(shards, half_rows, size))
    other_rows = other_core(own_rows)
    gradient = jnp.zeros((shards, 2, half_rows, size), bf16)
    gradient = lax.dynamic_update_slice(gradient, own_rows[:, None], (0, core, 0, 0))
    gradient = lax.dynamic_update_slice(gradient, other_rows[:, None], (0, 1 - core, 0, 0))
    gradient = gradient.reshape(size, size)
    first = jnp.dot(left_rows, gradient, preferred_element_type=f32).astype(bf16)
    update = jnp.dot(first, right, preferred_element_type=f32).astype(bf16)
    update = exchanged(update.reshape(shards, half_rows, size))

    oriented = jnp.where(core == 0, gradient, gradient.T)
    outer_product = jnp.dot(oriented, oriented.T, preferred_element_type=f32)
    new_stat = keep_rate * stats[0, 0] + (1.0 - keep_rate) / size * outer_product
    out = jnp.zeros(params.shape, bf16)
    update, new_stat, out = lax.optimization_barrier((update, new_stat, out))

    update = update.reshape(group, rows, size)
    own_params = lax.dynamic_slice_in_dim(params, replica * group, group, 0)

    def fresh(which):
        these = slice(which * half, (which + 1) * half)
        moved = picked(update, own_inverse[these]).astype(f32)
        return (own_params[these].astype(f32) - step_size * moved).astype(bf16)

    def placed(out, block, step, which):
        start = (replica + step) % replicas * group + which * half
        return lax.dynamic_update_slice_in_dim(out, block, start, 0)

    low, high = fresh(0), fresh(1)
    low_below = shifted(low, "dp", 1)
    high_above = shifted(high, "dp", -1)
    high_below = shifted(high, "dp", 1)
    low_above = shifted(low, "dp", -1)
    low_far = shifted(low_below, "dp", 1)
    high_far = shifted(high_above, "dp", -1)
    out = placed(out, low, 0, 0)
    out = placed(out, high, 0, 1)
    out = placed(out, low_below, 3, 0)
    out = placed(out, high_above, 1, 1)
    out = placed(out, high_below, 3, 1)
    out = placed(out, low_above, 1, 0)
    out = placed(out, low_far, 2, 0)
    out = placed(out, high_far, 2, 1)
    return (out, new_stat[None, None])


def solution(mesh):
    placed = (
        P("dp", None, "shard", None),
        P(None, "shard", None),
        P("dp", "shard", None, None),
        P("dp", "shard", None, None),
        P(),
    )
    return jax.shard_map(
        on_device,
        mesh=mesh,
        in_specs=placed,
        out_specs=(P(None, "shard", None), P("dp", "shard", None, None)),
        check_vma=False,
    )
```

time: 221 us -> 161 us (0.73)
  waiting for transfers between devices: 137 us -> 65 us
  blocking collectives: 0 us -> 29.7 us
  matrix products: 29.8 us -> 13.1 us
  between operations: 14.2 us -> 0.9 us
  starting transfers between devices: 14.2 us -> 22.5 us
  other arithmetic: 8.43 us -> 16.1 us
  local copies, waits for them, and re-layouts: 16.2 us -> 12.7 us
    ppermute x1 -> x14, waiting for transfers between devices: 4.13 us -> 58.2 us  [the longest x12 56.3 us: shifted(): lax.ppermute(block, axis, [(i, (i + offset) % count) for i in range(count)])]
    reduce_scatter x1 -> x0, waiting for transfers between devices: 52.3 us -> none  [on_device(): lax.psum_scatter(grads[0].astype(jnp.float32).astype(jnp.bfloat16), 'dp',...]
    all_to_all x2 -> x1, waiting for transfers between devices: 43.8 us -> 6.79 us  [exchanged(): lax.all_to_all(blocks, 'shard', split_axis=0, concat_axis=0, tiled=True)]
    all_gather x1 -> x0, waiting for transfers between devices: 36.3 us -> none  [on_device(): new_params = lax.all_gather(updated, 'dp', axis=0, tiled=True)]
    all_to_all x0 -> x1, blocking collectives: none -> 29.7 us  [exchanged(): lax.all_to_all(blocks, 'shard', split_axis=0, concat_axis=0, tiled=True)]
    dot_general x3 -> x2, matrix products: 29.8 us -> 13.1 us  [the longest x1 7.84 us: on_device(): outer_product = jnp.dot(oriented, oriented.T, preferred_element_type=f32)]
    ppermute x1 -> x14, starting transfers between devices: 2.38 us -> 18.5 us  [the longest x12 17.1 us: shifted(): lax.ppermute(block, axis, [(i, (i + offset) % count) for i in range(count)])]
    all_to_all x2 -> x1, starting transfers between devices: 11.8 us -> 3.95 us  [exchanged(): lax.all_to_all(blocks, 'shard', split_axis=0, concat_axis=0, tiled=True)]
  transfers between devices with their start and end apart: 5 -> 15, of which waited for: 5 -> 13; matrix products, arithmetic and copies ran while one was open for 4% -> 13% of each run, Pallas kernels for 0% -> 0%
where the time goes in v1:
time: 161 us; the launch traced here: 160 us
  waiting for transfers between devices  65 us (40%)
  blocking collectives  29.7 us (18%)
  starting transfers between devices  22.5 us (14%)
  other arithmetic  16.1 us (10%)
  matrix products  13.1 us (8%)
  local copies, waits for them, and re-layouts  12.7 us (8%)
    ppermute x12, waiting for transfers between devices, shifted(): lax.ppermute(block, axis, [(i, (i + offset) % count) for i in range(count)])  56.3 us
    all_to_all x1, blocking collectives, exchanged(): lax.all_to_all(blocks, 'shard', split_axis=0, concat_axis=0, tiled=True)  29.7 us
    ppermute x12, starting transfers between devices, shifted(): lax.ppermute(block, axis, [(i, (i + offset) % count) for i in range(count)])  17.1 us
    dot_general x1, matrix products, on_device(): outer_product = jnp.dot(oriented, oriented.T, preferred_element_type=f32)  7.84 us
    all_to_all x1, waiting for transfers between devices, exchanged(): lax.all_to_all(blocks, 'shard', split_axis=0, concat_axis=0, tiled=True)  6.79 us
    convert_element_type x3, other arithmetic, added(): return total.astype(bf16)  5.7 us
    dot_general x1, matrix products, on_device(): update = jnp.dot(first, right, preferred_element_type=f32).astype(bf16)  5.26 us
    all_to_all x1, starting transfers between devices, exchanged(): lax.all_to_all(blocks, 'shard', split_axis=0, concat_axis=0, tiled=True)  3.95 us
  transfers between devices with their start and end apart: 15, of which 13 were waited for; matrix products, arithmetic and copies ran while one was open for 13% of the time, Pallas kernels for 0%

profile of v1, /device:TPU:1, one launch (start us, length us, event | category | flops | bytes accessed | tf_op | source)
XLA Modules:
  0.0 160.0 jit_solution(376899000388786924)
XLA Ops:
  0.7 2.8 %dynamic-slice_bitcast_fusion.1 = (bf16[8,32,1024]{2,1,0:T(8,128)(2,1)S(1)}, bf16[8,32,1024]{2,1,0:T(8,128)(2,1)}, bf16[8,32,1024]{2,1,0:T(8,128)(2,1)}, bf16[8,32,1024]{2,1,0:T(8,128)(2,1)}) fusion(bf16[1,64,32,1024]{3,2,1,0:T(8,128)(2,1)} %param.5, s32[]{:T(128)S(6)} %select_n.143, s32[]{:T(128)S(6)} %select_n.144, s32[]{:T(128)S(6)} %select_n.141, ...), kind=kLoop, calls=%fused_computation.26 | loop fusion | bytes 4194320 | tf_op jit(solution)/shard_map/dynamic_slice | solution.py:62
  3.5 2.1 %collective-permute-start.1 = (bf16[8,32,1024]{2,1,0:T(8,128)(2,1)S(1)}, bf16[8,32,1024]{2,1,0:T(8,128)(2,1)S(1)}, u32[]{:S(2)}, u32[]{:S(2)}) collective-permute-start(bf16[8,32,1024]{2,1,0:T(8,128)(2,1)S(1)} %get-tuple-element.26), channel_id=1, source_target_pairs={{0,32},{32,64},{64,96},{96,0},{1,33},{33,65},{65,97},{97,1},{2,34}... | collective-permute-start | bytes 1572872 | tf_op jit(solution)/shard_map/ppermute | solution.py:14
  7.1 1.5 collective-permute-start
  8.6 1.4 collective-permute-start.4
  10.0 8.6 %collective-permute-done.1 = bf16[8,32,1024]{2,1,0:T(8,128)(2,1)S(1)} collective-permute-done((bf16[8,32,1024]{2,1,0:T(8,128)(2,1)S(1)}, bf16[8,32,1024]{2,1,0:T(8,128)(2,1)S(1)}, u32[]{:S(2)}, u32[]{:S(2)}) %collective-permute-start.1) | collective-permute-done | bytes 524320 | tf_op jit(solution)/shard_map/ppermute | solution.py:14
  19.9 1.2 collective-permute-start.3
  21.2 10.9 %collective-permute-done.4 = bf16[8,32,1024]{2,1,0:T(8,128)(2,1)} collective-permute-done((bf16[8,32,1024]{2,1,0:T(8,128)(2,1)}, bf16[8,32,1024]{2,1,0:T(8,128)(2,1)}, u32[]{:S(2)}, u32[]{:S(2)}) %collective-permute-start.4) | collective-permute-done | bytes 524320 | tf_op jit(solution)/shard_map/ppermute | solution.py:14
  33.3 3.2 %fusion.6 = (bf16[8,32,1024]{2,1,0:T(8,128)(2,1)}, bf16[8,32,1024]{2,1,0:T(8,128)(2,1)}) fusion(bf16[8,32,1024]{2,1,0:T(8,128)(2,1)} %collective-permute-done.2, bf16[8,32,1024]{2,1,0:T(8,128)(2,1)} %collective-permute-done, bf16[1,64,32,1024]{3,2,1,0:T(8,128)(2,1)} %param.5, s32[]{:T(128)S(6)} %select_n.137, ...), kind=kLoop, calls=%fused_computation.22 | loop fusion | flops 2621440 | bytes 3670024 | tf_op jit(solution)/shard_map/convert_element_type | solution.py:34
  36.4 1.5 collective-permute-start.5
  38.0 6.4 %collective-permute-done.3 = bf16[8,32,1024]{2,1,0:T(8,128)(2,1)S(1)} collective-permute-done((bf16[8,32,1024]{2,1,0:T(8,128)(2,1)}, bf16[8,32,1024]{2,1,0:T(8,128)(2,1)S(1)}, u32[]{:S(2)}, u32[]{:S(2)}) %collective-permute-start.3) | collective-permute-done | bytes 524320 | tf_op jit(solution)/shard_map/ppermute | solution.py:14
  44.4 2.2 %collective-permute-done.5 = bf16[8,32,1024]{2,1,0:T(8,128)(2,1)S(1)} collective-permute-done((bf16[8,32,1024]{2,1,0:T(8,128)(2,1)}, bf16[8,32,1024]{2,1,0:T(8,128)(2,1)S(1)}, u32[]{:S(2)}, u32[]{:S(2)}) %collective-permute-start.5) | collective-permute-done | bytes 524320 | tf_op jit(solution)/shard_map/ppermute | solution.py:14
  46.6 1.3 fusion.3
  49.0 1.6 gather_fusion
  50.6 2.3 %slice_select_fusion = bf16[32,1,16,1024]{3,2,1,0:T(8,128)(2,1)} fusion(bf16[32,2,16,1024]{3,2,1,0:T(8,128)(2,1)} %bitcast.12, bf16[32,2,16,1024]{3,2,1,0:T(8,128)(2,1)S(1)} %bitcast.56, pred[]{:T(512)S(6)} %eq.38), kind=kLoop, calls=%fused_computation.9 | loop fusion | flops 524288 | bytes 3145729 | tf_op jit(solution)/shard_map/jit(_where)/select_n | solution.py:74
  52.9 3.9 %broadcast_select_fusion = bf16[1024,1024]{1,0:T(8,128)(2,1)} fusion(bf16[1024,1024]{1,0:T(8,128)(2,1)} %collective-permute-done.6, pred[]{:T(512)S(6)} %eq.38, f32[1024,1024]{1,0:T(8,128)} %bitcast.51), kind=kLoop, calls=%fused_computation.6 | loop fusion | flops 2097152 | bytes 8388609 | tf_op jit(solution)/shard_map/jit(_where)/select_n | solution.py:77
  56.8 29.7 %all_to_all.10 = bf16[32,16,1024]{2,1,0:T(8,128)(2,1)S(1)} all-to-all(bf16[32,16,1024]{2,1,0:T(8,128)(2,1)S(1)} %bitcast.57), channel_id=1, replica_groups=mesh['dp'=4,'shard'=32] {'shard'}, dimensions={0} | all-to-all | bytes 2097152 | tf_op jit(solution)/shard_map/all_to_all | solution.py:23
  87.5 1.9 %collective-permute-done.7 = bf16[32,16,1024]{2,1,0:T(8,128)(2,1)} collective-permute-done((bf16[32,16,1024]{2,1,0:T(8,128)(2,1)S(1)}, bf16[32,16,1024]{2,1,0:T(8,128)(2,1)}, u32[]{:S(2)}, u32[]{:S(2)}) %collective-permute-start.7) | collective-permute-done | bytes 1048608 | tf_op jit(solution)/shard_map/ppermute | solution.py:19
  89.4 1.3 bitcast_dynamic-update-slice_fusion
  90.7 5.3 %convolution_convert_fusion = bf16[512,1024]{1,0:T(8,128)(2,1)} fusion(bf16[1024,1024]{1,0:T(8,128)(2,1)} %broadcast_select_fusion, bf16[512,1024]{1,0:T(8,128)(2,1)} %bitcast.60, bf16[1024,1024]{1,0:T(8,128)(2,1)S(1)} %bitcast.53), kind=kOutput, calls=%fused_computation.7 | convolution fusion | flops 2148532224 | bytes 6291456 | tf_op jit(solution)/shard_map/dot_general | solution.py:94
  96.0 4.0 %all-to-all-start.1 = ((bf16[32,16,1024]{2,1,0:T(8,128)(2,1)}), bf16[32,16,1024]{2,1,0:T(8,128)(2,1)S(1)}, u32[]{:S(2)}, u32[]{:S(2)}) async-start(bf16[32,16,1024]{2,1,0:T(8,128)(2,1)} %bitcast.61), calls=%async_computation.1 | async-start | bytes 2097152 | tf_op jit(solution)/shard_map/all_to_all | solution.py:23
  100.0 2.6 %copy.15 = bf16[1024,1024]{0,1:T(8,128)(2,1)} copy(bf16[1024,1024]{1,0:T(8,128)(2,1)S(1)} %bitcast.54) | data formatting | bytes 4194304 | tf_op jit(solution)/shard_map/reshape | solution.py:92
  102.6 7.8 %bitcast_add_fusion = f32[1024,1024]{1,0:T(8,128)} fusion(f32[1,1,1024,1024]{3,2,1,0:T(8,128)} %param.7, bf16[1024,1024]{1,0:T(8,128)(2,1)S(1)} %bitcast.55, bf16[1024,1024]{0,1:T(8,128)(2,1)} %copy.15, pred[]{:T(512)S(6)} %eq.38), kind=kOutput, calls=%fused_computation.3 | convolution fusion | flops 2151677952 | bytes 12582913 | tf_op jit(solution)/shard_map/dot_general | solution.py:98
  110.4 6.8 %all-to-all-done.1 = bf16[32,16,1024]{2,1,0:T(8,128)(2,1)S(1)} async-done(((bf16[32,16,1024]{2,1,0:T(8,128)(2,1)}), bf16[32,16,1024]{2,1,0:T(8,128)(2,1)S(1)}, u32[]{:S(2)}, u32[]{:S(2)}) %all-to-all-start.1) | async-done | bytes 1048608 | tf_op jit(solution)/shard_map/all_to_all | solution.py:23
  118.9 1.3 constant_dynamic-update-slice_fusion.7
  120.6 1.3 constant_dynamic-update-slice_fusion.6
  121.8 2.7 %collective-permute-start.9 = (bf16[8,32,1024]{2,1,0:T(8,128)(2,1)S(1)}, bf16[8,32,1024]{2,1,0:T(8,128)(2,1)S(1)}, u32[]{:S(2)}, u32[]{:S(2)}) collective-permute-start(bf16[8,32,1024]{2,1,0:T(8,128)(2,1)S(1)} %get-tuple-element.21), channel_id=1, source_target_pairs={{0,96},{32,0},{64,32},{96,64},{1,97},{33,1},{65,33},{97,65},{2,98}... | collective-permute-start | bytes 1572872 | tf_op jit(solution)/shard_map/ppermute | solution.py:14
  124.6 2.7 %collective-permute-start.11 = (bf16[8,32,1024]{2,1,0:T(8,128)(2,1)S(1)}, bf16[8,32,1024]{2,1,0:T(8,128)(2,1)S(1)}, u32[]{:S(2)}, u32[]{:S(2)}) collective-permute-start(bf16[8,32,1024]{2,1,0:T(8,128)(2,1)S(1)} %get-tuple-element.23), channel_id=1, source_target_pairs={{0,96},{32,0},{64,32},{96,64},{1,97},{33,1},{65,33},{97,65},{2,98}... | collective-permute-start | bytes 1572872 | tf_op jit(solution)/shard_map/ppermute | solution.py:14
  127.2 7.9 %collective-permute-done.8 = bf16[8,32,1024]{2,1,0:T(8,128)(2,1)S(1)} collective-permute-done((bf16[8,32,1024]{2,1,0:T(8,128)(2,1)S(1)}, bf16[8,32,1024]{2,1,0:T(8,128)(2,1)S(1)}, u32[]{:S(2)}, u32[]{:S(2)}) %collective-permute-start.8) | collective-permute-done | bytes 524320 | tf_op jit(solution)/shard_map/ppermute | solution.py:14
  135.5 3.4 %collective-permute-start.13 = (bf16[8,32,1024]{2,1,0:T(8,128)(2,1)S(1)}, bf16[8,32,1024]{2,1,0:T(8,128)(2,1)S(1)}, u32[]{:S(2)}, u32[]{:S(2)}) collective-permute-start(bf16[8,32,1024]{2,1,0:T(8,128)(2,1)S(1)} %collective-permute-done.9), channel_id=1, source_target_pairs={{0,96},{32,0},{64,32},{96,64},{1,97},{33,1},{65,33},{97,65},{2,98}... | collective-permute-start | bytes 1572872 | tf_op jit(solution)/shard_map/ppermute | solution.py:14
  139.0 7.4 %collective-permute-done.10 = bf16[8,32,1024]{2,1,0:T(8,128)(2,1)S(1)} collective-permute-done((bf16[8,32,1024]{2,1,0:T(8,128)(2,1)S(1)}, bf16[8,32,1024]{2,1,0:T(8,128)(2,1)S(1)}, u32[]{:S(2)}, u32[]{:S(2)}) %collective-permute-start.10) | collective-permute-done | bytes 524320 | tf_op jit(solution)/shard_map/ppermute | solution.py:14
  146.7 10.9 %collective-permute-done.12 = bf16[8,32,1024]{2,1,0:T(8,128)(2,1)S(1)} collective-permute-done((bf16[8,32,1024]{2,1,0:T(8,128)(2,1)S(1)}, bf16[8,32,1024]{2,1,0:T(8,128)(2,1)S(1)}, u32[]{:S(2)}, u32[]{:S(2)}) %collective-permute-start.12) | collective-permute-done | bytes 524320 | tf_op jit(solution)/shard_map/ppermute | solution.py:14
  158.0 2.0 %copy-done.2 = bf16[64,32,1024]{2,1,0:T(8,128)(2,1)} copy-done((bf16[64,32,1024]{2,1,0:T(8,128)(2,1)}, bf16[64,32,1024]{2,1,0:T(8,128)(2,1)S(1)}, u32[]{:S(2)}) %copy-start.2) | copy-done | bytes 4194328
  (40 shorter events, 9.2 us)
Async XLA Ops:
  0.7 5.0 %copy-start = (f32[1,1,1024,1024]{3,2,1,0:T(8,128)S(1)}, f32[1,1,1024,1024]{3,2,1,0:T(8,128)}, u32[]{:S(2)}) copy-start(f32[1,1,1024,1024]{3,2,1,0:T(8,128)} %param.8) | copy-start | bytes 12582916
  3.5 15.1 %collective-permute-start.1 = (bf16[8,32,1024]{2,1,0:T(8,128)(2,1)S(1)}, bf16[8,32,1024]{2,1,0:T(8,128)(2,1)S(1)}, u32[]{:S(2)}, u32[]{:S(2)}) collective-permute-start(bf16[8,32,1024]{2,1,0:T(8,128)(2,1)S(1)} %get-tuple-element.26), channel_id=1, source_target_pairs={{0,32},{32,64},{64,96},{96,0},{1,33},{33,65},{65,97},{97,1},{2,34}... | collective-permute-start | bytes 1572872 | tf_op jit(solution)/shard_map/ppermute | solution.py:14
  6.0 32.0 %copy-start.3 = (s32[4,16]{1,0:T(4,128)S(1)}, s32[4,16]{1,0:T(4,128)}, u32[]{:S(2)}) copy-start(s32[4,16]{1,0:T(4,128)} %param.9) | copy-start | bytes 772
  6.0 44.6 %collective-permute-start.6 = (bf16[1024,1024]{1,0:T(8,128)(2,1)S(1)}, bf16[1024,1024]{1,0:T(8,128)(2,1)}, u32[]{:S(2)}, u32[]{:S(2)}) collective-permute-start(bf16[1024,1024]{1,0:T(8,128)(2,1)S(1)} %convert_element_type.99), channel_id=1, source_target_pairs={{0,1},{1,0},{2,3},{3,2},{4,5},{5,4},{6,7},{7,6},{8,9},{9,8},{10,11... | collective-permute-start | bytes 6291464 | tf_op jit(solution)/shard_map/ppermute | solution.py:19
  7.1 14.1 %collective-permute-start = (bf16[8,32,1024]{2,1,0:T(8,128)(2,1)}, bf16[8,32,1024]{2,1,0:T(8,128)(2,1)}, u32[]{:S(2)}, u32[]{:S(2)}) collective-permute-start(bf16[8,32,1024]{2,1,0:T(8,128)(2,1)} %get-tuple-element.11), channel_id=1, source_target_pairs={{0,96},{32,0},{64,32},{96,64},{1,97},{33,1},{65,33},{97,65},{2,98}... | collective-permute-start | bytes 1572872 | tf_op jit(solution)/shard_map/ppermute | solution.py:14
  8.6 23.5 %collective-permute-start.4 = (bf16[8,32,1024]{2,1,0:T(8,128)(2,1)}, bf16[8,32,1024]{2,1,0:T(8,128)(2,1)}, u32[]{:S(2)}, u32[]{:S(2)}) collective-permute-start(bf16[8,32,1024]{2,1,0:T(8,128)(2,1)} %get-tuple-element.27), channel_id=1, source_target_pairs={{0,96},{32,0},{64,32},{96,64},{1,97},{33,1},{65,33},{97,65},{2,98}... | collective-permute-start | bytes 1572872 | tf_op jit(solution)/shard_map/ppermute | solution.py:14
  19.8 13.4 %collective-permute-start.2 = (bf16[8,32,1024]{2,1,0:T(8,128)(2,1)S(1)}, bf16[8,32,1024]{2,1,0:T(8,128)(2,1)}, u32[]{:S(2)}, u32[]{:S(2)}) collective-permute-start(bf16[8,32,1024]{2,1,0:T(8,128)(2,1)S(1)} %fusion.4), channel_id=1, source_target_pairs={{0,32},{32,64},{64,96},{96,0},{1,33},{33,65},{65,97},{97,1},{2,34}... | collective-permute-start | bytes 1572872 | tf_op jit(solution)/shard_map/ppermute | solution.py:14
  19.9 24.5 %collective-permute-start.3 = (bf16[8,32,1024]{2,1,0:T(8,128)(2,1)}, bf16[8,32,1024]{2,1,0:T(8,128)(2,1)S(1)}, u32[]{:S(2)}, u32[]{:S(2)}) collective-permute-start(bf16[8,32,1024]{2,1,0:T(8,128)(2,1)} %get-tuple-element.12), channel_id=1, source_target_pairs={{0,32},{32,64},{64,96},{96,0},{1,33},{33,65},{65,97},{97,1},{2,34}... | collective-permute-start | bytes 1572872 | tf_op jit(solution)/shard_map/ppermute | solution.py:14
  36.4 10.1 %collective-permute-start.5 = (bf16[8,32,1024]{2,1,0:T(8,128)(2,1)}, bf16[8,32,1024]{2,1,0:T(8,128)(2,1)S(1)}, u32[]{:S(2)}, u32[]{:S(2)}) collective-permute-start(bf16[8,32,1024]{2,1,0:T(8,128)(2,1)} %get-tuple-element.25), channel_id=1, source_target_pairs={{0,96},{32,0},{64,32},{96,64},{1,97},{33,1},{65,33},{97,65},{2,98}... | collective-permute-start | bytes 1572872 | tf_op jit(solution)/shard_map/ppermute | solution.py:14
  52.9 3.9 %copy-start.1 = (bf16[16,32,1024]{2,1,0:T(8,128)(2,1)S(1)}, bf16[16,32,1024]{2,1,0:T(8,128)(2,1)}, u32[]{:S(2)}) copy-start(bf16[16,32,1024]{2,1,0:T(8,128)(2,1)} %gather_fusion) | copy-start | bytes 3145732
  86.5 2.8 %collective-permute-start.7 = (bf16[32,16,1024]{2,1,0:T(8,128)(2,1)S(1)}, bf16[32,16,1024]{2,1,0:T(8,128)(2,1)}, u32[]{:S(2)}, u32[]{:S(2)}) collective-permute-start(bf16[32,16,1024]{2,1,0:T(8,128)(2,1)S(1)} %all_to_all.10), channel_id=1, source_target_pairs={{0,1},{1,0},{2,3},{3,2},{4,5},{5,4},{6,7},{7,6},{8,9},{9,8},{10,11... | collective-permute-start | bytes 3145736 | tf_op jit(solution)/shard_map/ppermute | solution.py:19
  96.0 21.2 %all-to-all-start.1 = ((bf16[32,16,1024]{2,1,0:T(8,128)(2,1)}), bf16[32,16,1024]{2,1,0:T(8,128)(2,1)S(1)}, u32[]{:S(2)}, u32[]{:S(2)}) async-start(bf16[32,16,1024]{2,1,0:T(8,128)(2,1)} %bitcast.61), calls=%async_computation.1 | async-start | bytes 2097152 | tf_op jit(solution)/shard_map/all_to_all | solution.py:23
  120.2 15.0 %collective-permute-start.8 = (bf16[8,32,1024]{2,1,0:T(8,128)(2,1)S(1)}, bf16[8,32,1024]{2,1,0:T(8,128)(2,1)S(1)}, u32[]{:S(2)}, u32[]{:S(2)}) collective-permute-start(bf16[8,32,1024]{2,1,0:T(8,128)(2,1)S(1)} %get-tuple-element.23), channel_id=1, source_target_pairs={{0,32},{32,64},{64,96},{96,0},{1,33},{33,65},{65,97},{97,1},{2,34}... | collective-permute-start | bytes 1572872 | tf_op jit(solution)/shard_map/ppermute | solution.py:14
  121.8 13.6 %collective-permute-start.9 = (bf16[8,32,1024]{2,1,0:T(8,128)(2,1)S(1)}, bf16[8,32,1024]{2,1,0:T(8,128)(2,1)S(1)}, u32[]{:S(2)}, u32[]{:S(2)}) collective-permute-start(bf16[8,32,1024]{2,1,0:T(8,128)(2,1)S(1)} %get-tuple-element.21), channel_id=1, source_target_pairs={{0,96},{32,0},{64,32},{96,64},{1,97},{33,1},{65,33},{97,65},{2,98}... | collective-permute-start | bytes 1572872 | tf_op jit(solution)/shard_map/ppermute | solution.py:14
  124.6 21.8 %collective-permute-start.10 = (bf16[8,32,1024]{2,1,0:T(8,128)(2,1)S(1)}, bf16[8,32,1024]{2,1,0:T(8,128)(2,1)S(1)}, u32[]{:S(2)}, u32[]{:S(2)}) collective-permute-start(bf16[8,32,1024]{2,1,0:T(8,128)(2,1)S(1)} %get-tuple-element.21), channel_id=1, source_target_pairs={{0,32},{32,64},{64,96},{96,0},{1,33},{33,65},{65,97},{97,1},{2,34}... | collective-permute-start | bytes 1572872 | tf_op jit(solution)/shard_map/ppermute | solution.py:14
  124.6 22.1 %collective-permute-start.11 = (bf16[8,32,1024]{2,1,0:T(8,128)(2,1)S(1)}, bf16[8,32,1024]{2,1,0:T(8,128)(2,1)S(1)}, u32[]{:S(2)}, u32[]{:S(2)}) collective-permute-start(bf16[8,32,1024]{2,1,0:T(8,128)(2,1)S(1)} %get-tuple-element.23), channel_id=1, source_target_pairs={{0,96},{32,0},{64,32},{96,64},{1,97},{33,1},{65,33},{97,65},{2,98}... | collective-permute-start | bytes 1572872 | tf_op jit(solution)/shard_map/ppermute | solution.py:14
  135.1 22.5 %collective-permute-start.12 = (bf16[8,32,1024]{2,1,0:T(8,128)(2,1)S(1)}, bf16[8,32,1024]{2,1,0:T(8,128)(2,1)S(1)}, u32[]{:S(2)}, u32[]{:S(2)}) collective-permute-start(bf16[8,32,1024]{2,1,0:T(8,128)(2,1)S(1)} %collective-permute-done.8), channel_id=1, source_target_pairs={{0,32},{32,64},{64,96},{96,0},{1,33},{33,65},{65,97},{97,1},{2,34}... | collective-permute-start | bytes 1572872 | tf_op jit(solution)/shard_map/ppermute | solution.py:14
  135.5 22.5 %collective-permute-start.13 = (bf16[8,32,1024]{2,1,0:T(8,128)(2,1)S(1)}, bf16[8,32,1024]{2,1,0:T(8,128)(2,1)S(1)}, u32[]{:S(2)}, u32[]{:S(2)}) collective-permute-start(bf16[8,32,1024]{2,1,0:T(8,128)(2,1)S(1)} %collective-permute-done.9), channel_id=1, source_target_pairs={{0,96},{32,0},{64,32},{96,64},{1,97},{33,1},{65,33},{97,65},{2,98}... | collective-permute-start | bytes 1572872 | tf_op jit(solution)/shard_map/ppermute | solution.py:14
  158.0 2.0 %copy-start.2 = (bf16[64,32,1024]{2,1,0:T(8,128)(2,1)}, bf16[64,32,1024]{2,1,0:T(8,128)(2,1)S(1)}, u32[]{:S(2)}) copy-start(bf16[64,32,1024]{2,1,0:T(8,128)(2,1)S(1)} %constant_dynamic-update-slice_fusion) | copy-start | bytes 12582916

commit v2 on v1

v2 whole, which is shorter than its diff:
```python
import functools

import jax
import jax.numpy as jnp
from jax import lax
from jax.experimental import pallas as pl
from jax.experimental.pallas import tpu as pltpu
from jax.sharding import PartitionSpec as P

keep_rate = 0.75
step_size = 0.25
f32 = jnp.float32
bf16 = jnp.bfloat16


def shifted(block, axis, offset):
    count = lax.axis_size(axis)
    return lax.ppermute(block, axis, [(i, (i + offset) % count) for i in range(count)])


def other_core(block):
    count = lax.axis_size("shard")
    return lax.ppermute(block, "shard", [(i, i ^ 1) for i in range(count)])


def exchanged(blocks):
    return lax.all_to_all(blocks, "shard", split_axis=0, concat_axis=0, tiled=True)


def added(*terms):
    total = terms[0].astype(f32)
    for term in terms[1:]:
        total = total + term.astype(f32)
    return total.astype(bf16)


def in_order(values, after):
    held = lax.optimization_barrier(tuple(values) + tuple(after))
    return held[: len(values)]


def whole_in(space):
    return pl.BlockSpec(memory_space=space)


def finish_sum_kernel(order, low, high, sum_low, sum_high, out):
    half = low.shape[0]

    def step(place, carry):
        block = order[place]

        @pl.when(block < half)
        def _():
            out[place] = added(low[block], sum_low[block])

        @pl.when(block >= half)
        def _():
            out[place] = added(high[block - half], sum_high[block - half])

        return carry

    lax.fori_loop(0, out.shape[0], step, 0)


def finish_sum(order, *terms):
    shape = (order.shape[0],) + terms[0].shape[1:]
    size = terms[0].size * 2
    return pl.pallas_call(
        finish_sum_kernel,
        out_shape=jax.ShapeDtypeStruct(shape, bf16),
        in_specs=[whole_in(pltpu.SMEM)] + [whole_in(pltpu.VMEM)] * 4,
        out_specs=whole_in(pltpu.VMEM),
        compiler_params=pltpu.CompilerParams(vmem_limit_bytes=16 << 20),
        cost_estimate=pl.CostEstimate(flops=size, bytes_accessed=6 * size, transcendentals=0),
        name="finish_sum",
    )(order, *terms)


def interleaved(core, own, other, gradient):
    half_rows = own.shape[1]

    def place(shard, carry):
        start = shard * 2 * half_rows
        here = pl.multiple_of(start + core * half_rows, half_rows)
        there = pl.multiple_of(start + (1 - core) * half_rows, half_rows)
        gradient[pl.ds(here, half_rows), :] = own[shard]
        gradient[pl.ds(there, half_rows), :] = other[shard]
        return carry

    lax.fori_loop(0, own.shape[0], place, 0, unroll=4)


def orient_kernel(core, root, partner, left, right, rows, moved):
    shards, _, half_rows, size = root.shape
    half = size // 2

    def rows_of(shard):
        return pl.ds(pl.multiple_of(shard * half_rows, half_rows), half_rows)

    def place_from(source, which):
        def place(shard, carry):
            rows[rows_of(shard), :] = source[shard, which]
            return carry

        lax.fori_loop(0, shards, place, 0)

    @pl.when(core[0] == 0)
    def _():
        right[...] = partner[...].reshape(size, size)
        place_from(root, 0)

    @pl.when(core[0] == 1)
    def _():
        right[...] = root[...].reshape(size, size)
        place_from(partner, 1)

    for side in range(2):
        place = lax.broadcasted_iota(jnp.int32, (size, half), 1)
        which = core[0] if side == 0 else 1 - core[0]
        source = 2 * half_rows * (place // half_rows) + which * half_rows + place % half_rows
        chosen = lax.broadcasted_iota(jnp.int32, (size, half), 0) == source
        moved[...] = jnp.where(chosen, 1.0, 0.0).astype(bf16)
        left[side] = jnp.dot(rows[...], moved[...], preferred_element_type=f32).astype(bf16)


def oriented(core, root, partner):
    shards, _, half_rows, size = root.shape
    half = size // 2
    return pl.pallas_call(
        orient_kernel,
        out_shape=[
            jax.ShapeDtypeStruct((2, half, half), bf16),
            jax.ShapeDtypeStruct((size, size), bf16),
        ],
        in_specs=[whole_in(pltpu.SMEM)] + [whole_in(pltpu.VMEM)] * 2,
        out_specs=[whole_in(pltpu.VMEM)] * 2,
        scratch_shapes=[pltpu.VMEM((half, size), bf16), pltpu.VMEM((size, half), bf16)],
        compiler_params=pltpu.CompilerParams(vmem_limit_bytes=24 << 20),
        cost_estimate=pl.CostEstimate(flops=size**3, bytes_accessed=12 * size**2, transcendentals=0),
        name="orient",
    )(core, root, partner)


def begin_kernel(left, rows, part):
    half, size = part.shape
    width = size // 4
    for low in range(0, size, width):
        columns = slice(low, low + width)
        part[:, columns] = jnp.dot(
            left[0], rows[:, :, columns].reshape(half, width), preferred_element_type=f32
        )


def begun(left, rows):
    half, size = left.shape[1], rows.shape[2]
    return pl.pallas_call(
        begin_kernel,
        out_shape=jax.ShapeDtypeStruct((half, size), f32),
        in_specs=[whole_in(pltpu.VMEM)] * 2,
        out_specs=whole_in(pltpu.VMEM),
        compiler_params=pltpu.CompilerParams(vmem_limit_bytes=16 << 20),
        cost_estimate=pl.CostEstimate(flops=size**3 // 2, bytes_accessed=4 * size**2, transcendentals=0),
        name="begin",
    )(left, rows)


def complete_kernel(part, left, rows, right, update, first):
    half, size = part.shape
    width = size // 4
    for low in range(0, size, width):
        columns = slice(low, low + width)
        product = jnp.dot(
            left[1], rows[:, :, columns].reshape(half, width), preferred_element_type=f32
        )
        first[:, columns] = (part[:, columns] + product).astype(bf16)
    for low in range(0, size, width):
        columns = slice(low, low + width)
        update[:, columns] = jnp.dot(
            first[...], right[:, columns], preferred_element_type=f32
        ).astype(bf16)


def completed(part, left, rows, right):
    half, size = part.shape
    return pl.pallas_call(
        complete_kernel,
        out_shape=jax.ShapeDtypeStruct((half, size), bf16),
        in_specs=[whole_in(pltpu.VMEM)] * 4,
        out_specs=whole_in(pltpu.VMEM),
        scratch_shapes=[pltpu.VMEM((half, size), bf16)],
        compiler_params=pltpu.CompilerParams(vmem_limit_bytes=24 << 20),
        cost_estimate=pl.CostEstimate(flops=2 * size**3, bytes_accessed=7 * size**2, transcendentals=0),
        name="complete",
    )(part, left, rows, right)


def statistics_kernel(core, own, other, stat, out, gradient):
    size = gradient.shape[0]
    tile = stat.shape[0]
    step = pl.program_id(0)
    mine = core[0]

    @pl.when(step == 0)
    def _():
        interleaved(mine, own, other, gradient)

    rows = pl.ds(pl.multiple_of(step * tile, tile), tile)

    @pl.when(mine == 0)
    def _():
        outer = lax.dot_general(
            gradient[rows, :], gradient[...], (((1,), (1,)), ((), ())), preferred_element_type=f32
        )
        out[...] = keep_rate * stat[...] + (1.0 - keep_rate) / size * outer

    @pl.when(mine == 1)
    def _():
        outer = lax.dot_general(
            gradient[:, rows], gradient[...], (((0,), (0,)), ((), ())), preferred_element_type=f32
        )
        out[...] = keep_rate * stat[...] + (1.0 - keep_rate) / size * outer


def statistics(core, own, other, stat):
    size = stat.shape[0]
    tile = size // 4
    block = pl.BlockSpec((tile, size), lambda step: (step, 0))
    return pl.pallas_call(
        statistics_kernel,
        grid=(size // tile,),
        out_shape=jax.ShapeDtypeStruct(stat.shape, f32),
        in_specs=[whole_in(pltpu.SMEM)] + [whole_in(pltpu.VMEM)] * 2 + [block],
        out_specs=block,
        scratch_shapes=[pltpu.VMEM((size, size), bf16)],
        compiler_params=pltpu.CompilerParams(vmem_limit_bytes=16 << 20),
        cost_estimate=pl.CostEstimate(flops=2 * size**3, bytes_accessed=12 * size**2, transcendentals=0),
        name="statistics",
    )(core, own, other, stat)


def step_kernel(order, old, update, low, high):
    half = low.shape[0]

    def step(place, carry):
        block = order[place]
        fresh = old[block].astype(f32) - step_size * update[place].astype(f32)

        @pl.when(block < half)
        def _():
            low[block] = fresh.astype(bf16)

        @pl.when(block >= half)
        def _():
            high[block - half] = fresh.astype(bf16)

        return carry

    lax.fori_loop(0, old.shape[0], step, 0)


def stepped(order, old, update):
    shape = (old.shape[0] // 2,) + old.shape[1:]
    return pl.pallas_call(
        step_kernel,
        out_shape=[jax.ShapeDtypeStruct(shape, bf16)] * 2,
        in_specs=[whole_in(pltpu.SMEM)] + [whole_in(pltpu.VMEM)] * 2,
        out_specs=[whole_in(pltpu.VMEM)] * 2,
        compiler_params=pltpu.CompilerParams(vmem_limit_bytes=16 << 20),
        cost_estimate=pl.CostEstimate(flops=2 * old.size, bytes_accessed=6 * old.size, transcendentals=0),
        name="step",
    )(order, old, update)


def settle_kernel(replica, low_far, high_far, below, out, sems):
    half = low_far.shape[0]
    replicas = out.shape[0] // (2 * half)
    start = lax.rem(replica[0] + 2, replicas) * 2 * half
    copies = [
        pltpu.make_async_copy(piece, out.at[pl.ds(start + which * half, half)], sems.at[which])
        for which, piece in enumerate((low_far, high_far))
    ]
    for copy in copies:
        copy.start()
    for copy in copies:
        copy.wait()


def settled(replica, low_far, high_far, below):
    return pl.pallas_call(
        settle_kernel,
        out_shape=jax.ShapeDtypeStruct(below.shape, bf16),
        in_specs=[whole_in(pltpu.SMEM)] + [whole_in(pltpu.VMEM)] * 2 + [whole_in(pltpu.HBM)],
        out_specs=whole_in(pltpu.HBM),
        scratch_shapes=[pltpu.SemaphoreType.DMA((2,))],
        input_output_aliases={3: 0},
        compiler_params=pltpu.CompilerParams(vmem_limit_bytes=16 << 20),
        cost_estimate=pl.CostEstimate(flops=0, bytes_accessed=8 * low_far.size, transcendentals=0),
        name="settle",
    )(replica, low_far, high_far, below)


def on_device(grads, params, stats, roots, table):
    shards = lax.axis_size("shard")
    replicas = lax.axis_size("dp")
    blocks = grads.shape[1]
    group = blocks // replicas
    rows = grads.shape[2]
    size = grads.shape[3]
    half_rows = rows // 2
    half = group // 2
    replica = lax.axis_index("dp")
    core = (lax.axis_index("shard") % 2)[None]
    own_order = lax.dynamic_index_in_dim(table, replica, 0, keepdims=False)

    def piece(array, step, which):
        start = (replica + step) % replicas * group + which * half
        return lax.dynamic_slice_in_dim(array, start, half, 0)

    mine = grads[0]
    far = lax.optimization_barrier((piece(mine, 2, 0), piece(mine, 2, 1)))
    far_up = shifted(far[0], "dp", 1)
    far_down = shifted(far[1], "dp", -1)

    root = in_order((roots[0, 0],), far)[0].astype(bf16).reshape(shards, 2, half_rows, size)
    partner_root = other_core(root)
    mine = in_order((mine,), (partner_root,))[0]
    near = lax.optimization_barrier((piece(mine, 1, 1), piece(mine, 3, 0)))
    near_up = shifted(near[0], "dp", 1)
    near_down = shifted(near[1], "dp", -1)

    sums = lax.optimization_barrier(
        (added(piece(mine, 1, 0), far_up), added(piece(mine, 3, 1), far_down))
    )
    sum_up = shifted(sums[0], "dp", 1)
    sum_down = shifted(sums[1], "dp", -1)
    own, near_up, near_down = lax.optimization_barrier(
        (lax.dynamic_slice_in_dim(mine, replica * group, group, 0), near_up, near_down)
    )
    partial = lax.optimization_barrier((added(own[:half], near_down), added(own[half:], near_up)))
    whole = finish_sum(own_order, *partial, sum_up, sum_down)

    own_rows = exchanged(whole.reshape(shards, half_rows, size))
    root, partner_root = in_order((root, partner_root), (whole,))
    left, right = oriented(core, root, partner_root)
    own_rows, left, right = lax.optimization_barrier((own_rows, left, right))
    other_rows = other_core(own_rows)
    part = begun(left, own_rows)
    update = completed(part, left, other_rows, right)

    update = exchanged(update.reshape(shards, half_rows, size))
    new_stat = statistics(core, own_rows, other_rows, stats[0, 0])
    own_params = lax.dynamic_slice_in_dim(params, replica * group, group, 0)
    update, new_stat, own_params = lax.optimization_barrier((update, new_stat, own_params))
    low, high = stepped(own_order, own_params, update.reshape(group, rows, size))
    low_below = shifted(low, "dp", 1)
    high_above = shifted(high, "dp", -1)
    high_below = shifted(high, "dp", 1)
    low_above = shifted(low, "dp", -1)
    low_far = shifted(low_below, "dp", 1)
    high_far = shifted(high_above, "dp", -1)

    def placed(out, block, step, which):
        start = (replica + step) % replicas * group + which * half
        return lax.dynamic_update_slice_in_dim(out, block, start, 0)

    out = jnp.zeros(params.shape, bf16)
    out = placed(out, low_below, 3, 0)
    out = placed(out, high_above, 1, 1)
    out = placed(out, low, 0, 0)
    out = placed(out, high, 0, 1)
    out = placed(out, high_below, 3, 1)
    out = placed(out, low_above, 1, 0)
    out = settled(replica[None], low_far, high_far, out)
    return (out, new_stat[None, None])


def solution(mesh):
    placed = (
        P("dp", None, "shard", None),
        P(None, "shard", None),
        P("dp", "shard", None, None),
        P("dp", "shard", None, None),
        P(),
    )
    return jax.shard_map(
        on_device,
        mesh=mesh,
        in_specs=placed,
        out_specs=(P(None, "shard", None), P("dp", "shard", None, None)),
        check_vma=False,
    )
```

time: 161 us -> 138 us (0.86)
  blocking collectives: 29.7 us -> 0 us
  Pallas kernels: 0 us -> 14.3 us
  matrix products: 13.1 us -> 0 us
  other arithmetic: 16.1 us -> 4.85 us
  starting transfers between devices: 22.5 us -> 31 us
  waiting for transfers between devices: 65 us -> 71.7 us
  local copies, waits for them, and re-layouts: 12.7 us -> 14.8 us
    all_to_all x1 -> x0, blocking collectives: 29.7 us -> none  [exchanged(): lax.all_to_all(blocks, 'shard', split_axis=0, concat_axis=0, tiled=True)]
    pallas_call x0 -> x7, Pallas kernels: none -> 14.3 us  [the longest x1 4.51 us: statistics(): pl.pallas_call(statistics_kernel, grid=(size // tile,), out_shape=jax.Sha...]
    dot_general x2 -> x0, matrix products: 13.1 us -> none  [the longest x1 7.84 us: on_device(): outer_product = jnp.dot(oriented, oriented.T, preferred_element_type=f32)]
    all_to_all x1 -> x2, waiting for transfers between devices: 6.79 us -> 19.7 us  [exchanged(): lax.all_to_all(blocks, 'shard', split_axis=0, concat_axis=0, tiled=True)]
    all_to_all x1 -> x2, starting transfers between devices: 3.95 us -> 12.4 us  [exchanged(): lax.all_to_all(blocks, 'shard', split_axis=0, concat_axis=0, tiled=True)]
    unnamed x8 -> x22, local copies, waits for them, and re-layouts: 2.02 us -> 8.79 us
    select_n x4 -> x0, other arithmetic: 6.26 us -> none  [the longest x1 3.87 us: on_device(): right = jnp.where(core == 0, partner_root, root)]
    ppermute x12, waiting for transfers between devices: 56.3 us -> 50.6 us  [shifted(): lax.ppermute(block, axis, [(i, (i + offset) % count) for i in range(count)])]
  transfers between devices with their start and end apart: 15 -> 16, of which waited for: 13 -> 11; matrix products, arithmetic and copies ran while one was open for 13% -> 5% of each run, Pallas kernels for 0% -> 6%
where the time goes in v2:
time: 138 us
  waiting for transfers between devices  71.7 us (52%)
  starting transfers between devices  31 us (22%)
  local copies, waits for them, and re-layouts  14.8 us (11%)
  Pallas kernels  14.3 us (10%)
  other arithmetic  4.85 us (4%)
    ppermute x12, waiting for transfers between devices, shifted(): lax.ppermute(block, axis, [(i, (i + offset) % count) for i in range(count)])  50.6 us
    all_to_all x2, waiting for transfers between devices, exchanged(): lax.all_to_all(blocks, 'shard', split_axis=0, concat_axis=0, tiled=True)  19.7 us
    ppermute x12, starting transfers between devices, shifted(): lax.ppermute(block, axis, [(i, (i + offset) % count) for i in range(count)])  16.7 us
    all_to_all x2, starting transfers between devices, exchanged(): lax.all_to_all(blocks, 'shard', split_axis=0, concat_axis=0, tiled=True)  12.4 us
    unnamed x22, local copies, waits for them, and re-layouts  8.79 us
    pallas_call x1, Pallas kernels, statistics(): pl.pallas_call(statistics_kernel, grid=(size // tile,), out_shape=jax.Sha...  4.51 us
    pallas_call x1, Pallas kernels, oriented(): pl.pallas_call(orient_kernel, out_shape=[jax.ShapeDtypeStruct((2, half, h...  3.18 us
    pallas_call x1, Pallas kernels, completed(): pl.pallas_call(complete_kernel, out_shape=jax.ShapeDtypeStruct((half, siz...  2.77 us
  transfers between devices with their start and end apart: 16, of which 11 were waited for; matrix products, arithmetic and copies ran while one was open for 5% of the time, Pallas kernels for 6%

profile of v2, /device:TPU:1, one launch (start us, length us, event | category | flops | bytes accessed | tf_op | source)
XLA Modules:
  0.0 137.6 jit_solution(4123867166528225322)
XLA Ops:
  0.7 1.3 dynamic-slice_bitcast_fusion
  2.0 2.5 %convert_element_type.39 = bf16[1024,1024]{1,0:T(8,128)(2,1)S(1)} convert(f32[1024,1024]{1,0:T(8,128)} %bitcast.21) | non-fusion elementwise | flops 1048576 | bytes 6291456 | tf_op jit(solution)/shard_map/convert_element_type | solution.py:324
  4.5 1.5 %collective-permute-start = (bf16[32,2,16,1024]{3,2,1,0:T(8,128)(2,1)S(1)}, bf16[32,2,16,1024]{3,2,1,0:T(8,128)(2,1)}, u32[]{:S(2)}, u32[]{:S(2)}) collective-permute-start(bf16[32,2,16,1024]{3,2,1,0:T(8,128)(2,1)S(1)} %bitcast.16), channel_id=1, source_target_pairs={{0,1},{1,0},{2,3},{3,2},{4,5},{5,4},{6,7},{7,6},{8,9},{9,8},{10,11... | collective-permute-start | bytes 6291464 | tf_op jit(solution)/shard_map/ppermute | solution.py:23
  6.0 1.4 %collective-permute-start.3 = (bf16[8,32,1024]{2,1,0:T(8,128)(2,1)S(1)}, bf16[8,32,1024]{2,1,0:T(8,128)(2,1)}, u32[]{:S(2)}, u32[]{:S(2)}) collective-permute-start(bf16[8,32,1024]{2,1,0:T(8,128)(2,1)S(1)} %get-tuple-element.27), channel_id=1, source_target_pairs={{0,32},{32,64},{64,96},{96,0},{1,33},{33,65},{65,97},{97,1},{2,34}... | collective-permute-start | bytes 1572872 | tf_op jit(solution)/shard_map/ppermute | solution.py:18
  7.4 1.4 %collective-permute-start.4 = (bf16[8,32,1024]{2,1,0:T(8,128)(2,1)S(1)}, bf16[8,32,1024]{2,1,0:T(8,128)(2,1)}, u32[]{:S(2)}, u32[]{:S(2)}) collective-permute-start(bf16[8,32,1024]{2,1,0:T(8,128)(2,1)S(1)} %get-tuple-element.28), channel_id=1, source_target_pairs={{0,96},{32,0},{64,32},{96,64},{1,97},{33,1},{65,33},{97,65},{2,98}... | collective-permute-start | bytes 1572872 | tf_op jit(solution)/shard_map/ppermute | solution.py:18
  9.9 1.3 constant_dynamic-slice_fusion.1
  11.2 1.4 %collective-permute-start.1 = (bf16[8,32,1024]{2,1,0:T(8,128)(2,1)S(1)}, bf16[8,32,1024]{2,1,0:T(8,128)(2,1)S(1)}, u32[]{:S(2)}, u32[]{:S(2)}) collective-permute-start(bf16[8,32,1024]{2,1,0:T(8,128)(2,1)S(1)} %get-tuple-element.31), channel_id=1, source_target_pairs={{0,32},{32,64},{64,96},{96,0},{1,33},{33,65},{65,97},{97,1},{2,34}... | collective-permute-start | bytes 1572872 | tf_op jit(solution)/shard_map/ppermute | solution.py:18
  12.7 1.5 %collective-permute-start.2 = (bf16[8,32,1024]{2,1,0:T(8,128)(2,1)S(1)}, bf16[8,32,1024]{2,1,0:T(8,128)(2,1)S(1)}, u32[]{:S(2)}, u32[]{:S(2)}) collective-permute-start(bf16[8,32,1024]{2,1,0:T(8,128)(2,1)S(1)} %get-tuple-element.32), channel_id=1, source_target_pairs={{0,96},{32,0},{64,32},{96,64},{1,97},{33,1},{65,33},{97,65},{2,98}... | collective-permute-start | bytes 1572872 | tf_op jit(solution)/shard_map/ppermute | solution.py:18
  14.2 6.9 %collective-permute-done.3 = bf16[8,32,1024]{2,1,0:T(8,128)(2,1)} collective-permute-done((bf16[8,32,1024]{2,1,0:T(8,128)(2,1)S(1)}, bf16[8,32,1024]{2,1,0:T(8,128)(2,1)}, u32[]{:S(2)}, u32[]{:S(2)}) %collective-permute-start.3) | collective-permute-done | bytes 524320 | tf_op jit(solution)/shard_map/ppermute | solution.py:18
  21.1 1.9 %add_convert_fusion = (bf16[8,32,1024]{2,1,0:T(8,128)(2,1)S(1)}, bf16[8,32,1024]{2,1,0:T(8,128)(2,1)S(1)}) fusion(bf16[8,32,1024]{2,1,0:T(8,128)(2,1)} %collective-permute-done.4, bf16[64,32,1024]{2,1,0:T(8,128)(2,1)} %bitcast.24, s32[]{:T(128)S(6)} %select_n.85, bf16[8,32,1024]{2,1,0:T(8,128)(2,1)} %collective-permute-done.3, s32[]{:T(128)S(6)} %select_n.84), kind=kLoop, calls=%fused_computation | loop fusion | flops 2097152 | bytes 3145736 | tf_op jit(solution)/shard_map/convert_element_type | solution.py:34
  24.0 1.8 %collective-permute-start.6 = (bf16[8,32,1024]{2,1,0:T(8,128)(2,1)S(1)}, bf16[8,32,1024]{2,1,0:T(8,128)(2,1)S(1)}, u32[]{:S(2)}, u32[]{:S(2)}) collective-permute-start(bf16[8,32,1024]{2,1,0:T(8,128)(2,1)S(1)} %get-tuple-element.39), channel_id=1, source_target_pairs={{0,96},{32,0},{64,32},{96,64},{1,97},{33,1},{65,33},{97,65},{2,98}... | collective-permute-start | bytes 1572872 | tf_op jit(solution)/shard_map/ppermute | solution.py:18
  25.8 1.3 constant_dynamic-slice_fusion.3
  27.1 5.1 %collective-permute-done.1 = bf16[8,32,1024]{2,1,0:T(8,128)(2,1)S(1)} collective-permute-done((bf16[8,32,1024]{2,1,0:T(8,128)(2,1)S(1)}, bf16[8,32,1024]{2,1,0:T(8,128)(2,1)S(1)}, u32[]{:S(2)}, u32[]{:S(2)}) %collective-permute-start.1) | collective-permute-done | bytes 524320 | tf_op jit(solution)/shard_map/ppermute | solution.py:18
  32.6 10.8 %collective-permute-done.5.sum_low = bf16[8,32,1024]{2,1,0:T(8,128)(2,1)S(1)} collective-permute-done((bf16[8,32,1024]{2,1,0:T(8,128)(2,1)S(1)}, bf16[8,32,1024]{2,1,0:T(8,128)(2,1)S(1)}, u32[]{:S(2)}, u32[]{:S(2)}) %collective-permute-start.5) | collective-permute-done | bytes 524320 | tf_op jit(solution)/shard_map/ppermute | solution.py:18
  45.5 8.7 %all-to-all-start = ((bf16[32,16,1024]{2,1,0:T(8,128)(2,1)}), bf16[32,16,1024]{2,1,0:T(8,128)(2,1)S(1)}, u32[]{:S(2)}, u32[]{:S(2)}) async-start(bf16[32,16,1024]{2,1,0:T(8,128)(2,1)} %bitcast.20), calls=%async_computation | async-start | bytes 2097152 | tf_op jit(solution)/shard_map/all_to_all | solution.py:27
  54.2 3.2 %orient.1 = (bf16[2,512,512]{2,1,0:T(8,128)(2,1)S(1)}, bf16[1024,1024]{1,0:T(8,128)(2,1)S(1)}) custom-call(s32[1]{0:T(128)} %bitcast.8.core, bf16[32,2,16,1024]{3,2,1,0:T(8,128)(2,1)S(1)} %bitcast.17, bf16[32,2,16,1024]{3,2,1,0:T(8,128)(2,1)} %collective-permute-done.partner), custom_call_target="tpu_custom_call" | custom-call | flops 1073741824 | bytes 12582912 | tf_op jit(solution)/shard_map/orient/pallas_call | solution.py:129
  58.4 1.3 copy-done.8
  59.7 11.7 %all-to-all-done.rows.own = bf16[32,16,1024]{2,1,0:T(8,128)(2,1)S(1)} async-done(((bf16[32,16,1024]{2,1,0:T(8,128)(2,1)}), bf16[32,16,1024]{2,1,0:T(8,128)(2,1)S(1)}, u32[]{:S(2)}, u32[]{:S(2)}) %all-to-all-start) | async-done | bytes 1048608 | tf_op jit(solution)/shard_map/all_to_all | solution.py:27
  71.8 1.2 copy-done.4
  74.9 2.8 %complete.1 = bf16[512,1024]{1,0:T(8,128)(2,1)} custom-call(f32[512,1024]{1,0:T(8,128)S(1)} %begin.1.part, bf16[2,512,512]{2,1,0:T(8,128)(2,1)S(1)} %copy-done.5, bf16[32,16,1024]{2,1,0:T(8,128)(2,1)S(1)} %collective-permute-done.7.rows.other, bf16[1024,1024]{1,0:T(8,128)(2,1)S(1)} %copy-done.9), custom_call_target="tpu_custom_call" | custom-call | flops 2147483648 | bytes 7340032 | tf_op jit(solution)/shard_map/complete/pallas_call | solution.py:185
  77.7 3.7 %all-to-all-start.1 = ((bf16[32,16,1024]{2,1,0:T(8,128)(2,1)}), bf16[32,16,1024]{2,1,0:T(8,128)(2,1)S(1)}, u32[]{:S(2)}, u32[]{:S(2)}) async-start(bf16[32,16,1024]{2,1,0:T(8,128)(2,1)} %bitcast.9), calls=%async_computation.1 | async-start | bytes 2097152 | tf_op jit(solution)/shard_map/all_to_all | solution.py:27
  81.4 1.3 constant_dynamic-slice_fusion.old
  82.8 2.2 %copy-done.1 = f32[1,1,1024,1024]{3,2,1,0:T(8,128)S(1)} copy-done((f32[1,1,1024,1024]{3,2,1,0:T(8,128)S(1)}, f32[1,1,1024,1024]{3,2,1,0:T(8,128)}, u32[]{:S(2)}) %copy-start.1) | copy-done | bytes 4194328
  86.2 4.5 %statistics.1 = f32[1024,1024]{1,0:T(8,128)} custom-call(s32[1]{0:T(128)} %bitcast.8.core, bf16[32,16,1024]{2,1,0:T(8,128)(2,1)S(1)} %all-to-all-done.rows.own, bf16[32,16,1024]{2,1,0:T(8,128)(2,1)S(1)} %copy-done.7, f32[1024,1024]{1,0:T(8,128)S(1)} %bitcast.19), custom_call_target="tpu_custom_call" | custom-call | flops 2147483648 | bytes 12582912 | tf_op jit(solution)/shard_map/statistics/pallas_call | solution.py:228
  90.7 8.0 %all-to-all-done.1 = bf16[32,16,1024]{2,1,0:T(8,128)(2,1)S(1)} async-done(((bf16[32,16,1024]{2,1,0:T(8,128)(2,1)}), bf16[32,16,1024]{2,1,0:T(8,128)(2,1)S(1)}, u32[]{:S(2)}, u32[]{:S(2)}) %all-to-all-start.1) | async-done | bytes 1048608 | tf_op jit(solution)/shard_map/all_to_all | solution.py:27
  99.8 1.4 collective-permute-start.8
  101.1 1.4 %collective-permute-start.10 = (bf16[8,32,1024]{2,1,0:T(8,128)(2,1)S(1)}, bf16[8,32,1024]{2,1,0:T(8,128)(2,1)S(1)}, u32[]{:S(2)}, u32[]{:S(2)}) collective-permute-start(bf16[8,32,1024]{2,1,0:T(8,128)(2,1)S(1)} %get-tuple-element.50), channel_id=1, source_target_pairs={{0,96},{32,0},{64,32},{96,64},{1,97},{33,1},{65,33},{97,65},{2,98}... | collective-permute-start | bytes 1572872 | tf_op jit(solution)/shard_map/ppermute | solution.py:18
  102.6 2.6 %collective-permute-start.13 = (bf16[8,32,1024]{2,1,0:T(8,128)(2,1)S(1)}, bf16[8,32,1024]{2,1,0:T(8,128)(2,1)S(1)}, u32[]{:S(2)}, u32[]{:S(2)}) collective-permute-start(bf16[8,32,1024]{2,1,0:T(8,128)(2,1)S(1)} %get-tuple-element.49), channel_id=1, source_target_pairs={{0,96},{32,0},{64,32},{96,64},{1,97},{33,1},{65,33},{97,65},{2,98}... | collective-permute-start | bytes 1572872 | tf_op jit(solution)/shard_map/ppermute | solution.py:18
  105.2 8.9 %collective-permute-done.8 = bf16[8,32,1024]{2,1,0:T(8,128)(2,1)S(1)} collective-permute-done((bf16[8,32,1024]{2,1,0:T(8,128)(2,1)S(1)}, bf16[8,32,1024]{2,1,0:T(8,128)(2,1)S(1)}, u32[]{:S(2)}, u32[]{:S(2)}) %collective-permute-start.8) | collective-permute-done | bytes 524320 | tf_op jit(solution)/shard_map/ppermute | solution.py:18
  114.8 2.7 %collective-permute-start.11 = (bf16[8,32,1024]{2,1,0:T(8,128)(2,1)S(1)}, bf16[8,32,1024]{2,1,0:T(8,128)(2,1)S(1)}, u32[]{:S(2)}, u32[]{:S(2)}) collective-permute-start(bf16[8,32,1024]{2,1,0:T(8,128)(2,1)S(1)} %collective-permute-done.10), channel_id=1, source_target_pairs={{0,96},{32,0},{64,32},{96,64},{1,97},{33,1},{65,33},{97,65},{2,98}... | collective-permute-start | bytes 1572872 | tf_op jit(solution)/shard_map/ppermute | solution.py:18
  117.7 7.7 %collective-permute-done.12 = bf16[8,32,1024]{2,1,0:T(8,128)(2,1)S(1)} collective-permute-done((bf16[8,32,1024]{2,1,0:T(8,128)(2,1)S(1)}, bf16[8,32,1024]{2,1,0:T(8,128)(2,1)S(1)}, u32[]{:S(2)}, u32[]{:S(2)}) %collective-permute-start.12) | collective-permute-done | bytes 524320 | tf_op jit(solution)/shard_map/ppermute | solution.py:18
  125.5 10.9 %collective-permute-done.11.high_far = bf16[8,32,1024]{2,1,0:T(8,128)(2,1)S(1)} collective-permute-done((bf16[8,32,1024]{2,1,0:T(8,128)(2,1)S(1)}, bf16[8,32,1024]{2,1,0:T(8,128)(2,1)S(1)}, u32[]{:S(2)}, u32[]{:S(2)}) %collective-permute-start.11) | collective-permute-done | bytes 524320 | tf_op jit(solution)/shard_map/ppermute | solution.py:18
  (44 shorter events, 12.3 us)
Async XLA Ops:
  0.6 25.1 %copy-start = (s32[4,16]{1,0:T(4,128)S(1)}, s32[4,16]{1,0:T(4,128)}, u32[]{:S(2)}) copy-start(s32[4,16]{1,0:T(4,128)} %param.9) | copy-start | bytes 772
  4.5 5.4 %collective-permute-start = (bf16[32,2,16,1024]{3,2,1,0:T(8,128)(2,1)S(1)}, bf16[32,2,16,1024]{3,2,1,0:T(8,128)(2,1)}, u32[]{:S(2)}, u32[]{:S(2)}) collective-permute-start(bf16[32,2,16,1024]{3,2,1,0:T(8,128)(2,1)S(1)} %bitcast.16), channel_id=1, source_target_pairs={{0,1},{1,0},{2,3},{3,2},{4,5},{5,4},{6,7},{7,6},{8,9},{9,8},{10,11... | collective-permute-start | bytes 6291464 | tf_op jit(solution)/shard_map/ppermute | solution.py:23
  6.0 15.1 %collective-permute-start.3 = (bf16[8,32,1024]{2,1,0:T(8,128)(2,1)S(1)}, bf16[8,32,1024]{2,1,0:T(8,128)(2,1)}, u32[]{:S(2)}, u32[]{:S(2)}) collective-permute-start(bf16[8,32,1024]{2,1,0:T(8,128)(2,1)S(1)} %get-tuple-element.27), channel_id=1, source_target_pairs={{0,32},{32,64},{64,96},{96,0},{1,33},{33,65},{65,97},{97,1},{2,34}... | collective-permute-start | bytes 1572872 | tf_op jit(solution)/shard_map/ppermute | solution.py:18
  7.4 13.7 %collective-permute-start.4 = (bf16[8,32,1024]{2,1,0:T(8,128)(2,1)S(1)}, bf16[8,32,1024]{2,1,0:T(8,128)(2,1)}, u32[]{:S(2)}, u32[]{:S(2)}) collective-permute-start(bf16[8,32,1024]{2,1,0:T(8,128)(2,1)S(1)} %get-tuple-element.28), channel_id=1, source_target_pairs={{0,96},{32,0},{64,32},{96,64},{1,97},{33,1},{65,33},{97,65},{2,98}... | collective-permute-start | bytes 1572872 | tf_op jit(solution)/shard_map/ppermute | solution.py:18
  11.2 21.0 %collective-permute-start.1 = (bf16[8,32,1024]{2,1,0:T(8,128)(2,1)S(1)}, bf16[8,32,1024]{2,1,0:T(8,128)(2,1)S(1)}, u32[]{:S(2)}, u32[]{:S(2)}) collective-permute-start(bf16[8,32,1024]{2,1,0:T(8,128)(2,1)S(1)} %get-tuple-element.31), channel_id=1, source_target_pairs={{0,32},{32,64},{64,96},{96,0},{1,33},{33,65},{65,97},{97,1},{2,34}... | collective-permute-start | bytes 1572872 | tf_op jit(solution)/shard_map/ppermute | solution.py:18
  12.7 19.6 %collective-permute-start.2 = (bf16[8,32,1024]{2,1,0:T(8,128)(2,1)S(1)}, bf16[8,32,1024]{2,1,0:T(8,128)(2,1)S(1)}, u32[]{:S(2)}, u32[]{:S(2)}) collective-permute-start(bf16[8,32,1024]{2,1,0:T(8,128)(2,1)S(1)} %get-tuple-element.32), channel_id=1, source_target_pairs={{0,96},{32,0},{64,32},{96,64},{1,97},{33,1},{65,33},{97,65},{2,98}... | collective-permute-start | bytes 1572872 | tf_op jit(solution)/shard_map/ppermute | solution.py:18
  23.0 20.4 %collective-permute-start.5 = (bf16[8,32,1024]{2,1,0:T(8,128)(2,1)S(1)}, bf16[8,32,1024]{2,1,0:T(8,128)(2,1)S(1)}, u32[]{:S(2)}, u32[]{:S(2)}) collective-permute-start(bf16[8,32,1024]{2,1,0:T(8,128)(2,1)S(1)} %get-tuple-element.38), channel_id=1, source_target_pairs={{0,32},{32,64},{64,96},{96,0},{1,33},{33,65},{65,97},{97,1},{2,34}... | collective-permute-start | bytes 1572872 | tf_op jit(solution)/shard_map/ppermute | solution.py:18
  24.0 19.5 %collective-permute-start.6 = (bf16[8,32,1024]{2,1,0:T(8,128)(2,1)S(1)}, bf16[8,32,1024]{2,1,0:T(8,128)(2,1)S(1)}, u32[]{:S(2)}, u32[]{:S(2)}) collective-permute-start(bf16[8,32,1024]{2,1,0:T(8,128)(2,1)S(1)} %get-tuple-element.39), channel_id=1, source_target_pairs={{0,96},{32,0},{64,32},{96,64},{1,97},{33,1},{65,33},{97,65},{2,98}... | collective-permute-start | bytes 1572872 | tf_op jit(solution)/shard_map/ppermute | solution.py:18
  44.5 1.0 copy-start.2
  45.5 25.9 %all-to-all-start = ((bf16[32,16,1024]{2,1,0:T(8,128)(2,1)}), bf16[32,16,1024]{2,1,0:T(8,128)(2,1)S(1)}, u32[]{:S(2)}, u32[]{:S(2)}) async-start(bf16[32,16,1024]{2,1,0:T(8,128)(2,1)} %bitcast.20), calls=%async_computation | async-start | bytes 2097152 | tf_op jit(solution)/shard_map/all_to_all | solution.py:27
  57.4 1.0 copy-start.3
  58.4 1.3 copy-start.8
  71.4 2.7 %collective-permute-start.7 = (bf16[32,16,1024]{2,1,0:T(8,128)(2,1)S(1)}, bf16[32,16,1024]{2,1,0:T(8,128)(2,1)S(1)}, u32[]{:S(2)}, u32[]{:S(2)}) collective-permute-start(bf16[32,16,1024]{2,1,0:T(8,128)(2,1)S(1)} %all-to-all-done.rows.own), channel_id=1, source_target_pairs={{0,1},{1,0},{2,3},{3,2},{4,5},{5,4},{6,7},{7,6},{8,9},{9,8},{10,11... | collective-permute-start | bytes 3145736 | tf_op jit(solution)/shard_map/ppermute | solution.py:23
  71.8 1.2 copy-start.4
  73.0 1.2 copy-start.5
  73.0 1.9 %copy-start.9 = (bf16[1024,1024]{1,0:T(8,128)(2,1)S(1)}, bf16[1024,1024]{1,0:T(8,128)(2,1)}, u32[]{:S(2)}) copy-start(bf16[1024,1024]{1,0:T(8,128)(2,1)} %copy-done.8) | copy-start | bytes 6291460
  74.9 2.8 %copy-start.6 = (bf16[32,16,1024]{2,1,0:T(8,128)(2,1)}, bf16[32,16,1024]{2,1,0:T(8,128)(2,1)S(1)}, u32[]{:S(2)}) copy-start(bf16[32,16,1024]{2,1,0:T(8,128)(2,1)S(1)} %collective-permute-done.7.rows.other) | copy-start | bytes 3145732
  77.7 21.0 %all-to-all-start.1 = ((bf16[32,16,1024]{2,1,0:T(8,128)(2,1)}), bf16[32,16,1024]{2,1,0:T(8,128)(2,1)S(1)}, u32[]{:S(2)}, u32[]{:S(2)}) async-start(bf16[32,16,1024]{2,1,0:T(8,128)(2,1)} %bitcast.9), calls=%async_computation.1 | async-start | bytes 2097152 | tf_op jit(solution)/shard_map/all_to_all | solution.py:27
  82.8 2.2 %copy-start.1 = (f32[1,1,1024,1024]{3,2,1,0:T(8,128)S(1)}, f32[1,1,1024,1024]{3,2,1,0:T(8,128)}, u32[]{:S(2)}) copy-start(f32[1,1,1024,1024]{3,2,1,0:T(8,128)} %param.7) | copy-start | bytes 12582916
  85.0 1.2 copy-start.7
  99.8 14.4 %collective-permute-start.8 = (bf16[8,32,1024]{2,1,0:T(8,128)(2,1)S(1)}, bf16[8,32,1024]{2,1,0:T(8,128)(2,1)S(1)}, u32[]{:S(2)}, u32[]{:S(2)}) collective-permute-start(bf16[8,32,1024]{2,1,0:T(8,128)(2,1)S(1)} %get-tuple-element.49), channel_id=1, source_target_pairs={{0,32},{32,64},{64,96},{96,0},{1,33},{33,65},{65,97},{97,1},{2,34}... | collective-permute-start | bytes 1572872 | tf_op jit(solution)/shard_map/ppermute | solution.py:18
  101.1 13.7 %collective-permute-start.10 = (bf16[8,32,1024]{2,1,0:T(8,128)(2,1)S(1)}, bf16[8,32,1024]{2,1,0:T(8,128)(2,1)S(1)}, u32[]{:S(2)}, u32[]{:S(2)}) collective-permute-start(bf16[8,32,1024]{2,1,0:T(8,128)(2,1)S(1)} %get-tuple-element.50), channel_id=1, source_target_pairs={{0,96},{32,0},{64,32},{96,64},{1,97},{33,1},{65,33},{97,65},{2,98}... | collective-permute-start | bytes 1572872 | tf_op jit(solution)/shard_map/ppermute | solution.py:18
  102.6 22.8 %collective-permute-start.12 = (bf16[8,32,1024]{2,1,0:T(8,128)(2,1)S(1)}, bf16[8,32,1024]{2,1,0:T(8,128)(2,1)S(1)}, u32[]{:S(2)}, u32[]{:S(2)}) collective-permute-start(bf16[8,32,1024]{2,1,0:T(8,128)(2,1)S(1)} %get-tuple-element.50), channel_id=1, source_target_pairs={{0,32},{32,64},{64,96},{96,0},{1,33},{33,65},{65,97},{97,1},{2,34}... | collective-permute-start | bytes 1572872 | tf_op jit(solution)/shard_map/ppermute | solution.py:18
  102.6 22.8 %collective-permute-start.13 = (bf16[8,32,1024]{2,1,0:T(8,128)(2,1)S(1)}, bf16[8,32,1024]{2,1,0:T(8,128)(2,1)S(1)}, u32[]{:S(2)}, u32[]{:S(2)}) collective-permute-start(bf16[8,32,1024]{2,1,0:T(8,128)(2,1)S(1)} %get-tuple-element.49), channel_id=1, source_target_pairs={{0,96},{32,0},{64,32},{96,64},{1,97},{33,1},{65,33},{97,65},{2,98}... | collective-permute-start | bytes 1572872 | tf_op jit(solution)/shard_map/ppermute | solution.py:18
  114.2 22.5 %collective-permute-start.9 = (bf16[8,32,1024]{2,1,0:T(8,128)(2,1)S(1)}, bf16[8,32,1024]{2,1,0:T(8,128)(2,1)S(1)}, u32[]{:S(2)}, u32[]{:S(2)}) collective-permute-start(bf16[8,32,1024]{2,1,0:T(8,128)(2,1)S(1)} %collective-permute-done.8), channel_id=1, source_target_pairs={{0,32},{32,64},{64,96},{96,0},{1,33},{33,65},{65,97},{97,1},{2,34}... | collective-permute-start | bytes 1572872 | tf_op jit(solution)/shard_map/ppermute | solution.py:18
  114.8 21.6 %collective-permute-start.11 = (bf16[8,32,1024]{2,1,0:T(8,128)(2,1)S(1)}, bf16[8,32,1024]{2,1,0:T(8,128)(2,1)S(1)}, u32[]{:S(2)}, u32[]{:S(2)}) collective-permute-start(bf16[8,32,1024]{2,1,0:T(8,128)(2,1)S(1)} %collective-permute-done.10), channel_id=1, source_target_pairs={{0,96},{32,0},{64,32},{96,64},{1,97},{33,1},{65,33},{97,65},{2,98}... | collective-permute-start | bytes 1572872 | tf_op jit(solution)/shard_map/ppermute | solution.py:18
  125.5 11.1 %copy-start.10 = (bf16[64,32,1024]{2,1,0:T(8,128)(2,1)}, bf16[64,32,1024]{2,1,0:T(8,128)(2,1)S(1)}, u32[]{:S(2)}) copy-start(bf16[64,32,1024]{2,1,0:T(8,128)(2,1)S(1)} %constant_dynamic-update-slice_fusion.below) | copy-start | bytes 12582916

commit v3 on v2

--- a/solution.py
+++ b/solution.py
@@ -90,37 +90,37 @@
     lax.fori_loop(0, own.shape[0], place, 0, unroll=4)
 
 
-def orient_kernel(core, root, partner, left, right, rows, moved):
-    shards, _, half_rows, size = root.shape
+def orient_kernel(core, root, partner, left, right, left_in, right_in, moved, sems):
+    shards, half_rows, size = left_in.shape
     half = size // 2
 
-    def rows_of(shard):
-        return pl.ds(pl.multiple_of(shard * half_rows, half_rows), half_rows)
-
-    def place_from(source, which):
-        def place(shard, carry):
-            rows[rows_of(shard), :] = source[shard, which]
-            return carry
-
-        lax.fori_loop(0, shards, place, 0)
+    def left_copy(source, which):
+        return pltpu.make_async_copy(source.at[:, which], left_in, sems.at[0])
+
+    def right_copy(source):
+        return pltpu.make_async_copy(source, right_in, sems.at[1])
 
     @pl.when(core[0] == 0)
     def _():
-        right[...] = partner[...].reshape(size, size)
-        place_from(root, 0)
+        left_copy(root, 0).start()
+        right_copy(partner).start()
 
     @pl.when(core[0] == 1)
     def _():
-        right[...] = root[...].reshape(size, size)
-        place_from(partner, 1)
-
+        left_copy(partner, 1).start()
+        right_copy(root).start()
+
+    left_copy(root, 0).wait()
+    rows = left_in[...].reshape(half, size).astype(bf16)
     for side in range(2):
         place = lax.broadcasted_iota(jnp.int32, (size, half), 1)
         which = core[0] if side == 0 else 1 - core[0]
         source = 2 * half_rows * (place // half_rows) + which * half_rows + place % half_rows
         chosen = lax.broadcasted_iota(jnp.int32, (size, half), 0) == source
         moved[...] = jnp.where(chosen, 1.0, 0.0).astype(bf16)
-        left[side] = jnp.dot(rows[...], moved[...], preferred_element_type=f32).astype(bf16)
+        left[side] = jnp.dot(rows, moved[...], preferred_element_type=f32).astype(bf16)
+    right_copy(root).wait()
+    right[...] = right_in[...].reshape(size, size).astype(bf16)
 
 
 def oriented(core, root, partner):
@@ -132,9 +132,14 @@
             jax.ShapeDtypeStruct((2, half, half), bf16),
             jax.ShapeDtypeStruct((size, size), bf16),
         ],
-        in_specs=[whole_in(pltpu.SMEM)] + [whole_in(pltpu.VMEM)] * 2,
+        in_specs=[whole_in(pltpu.SMEM)] + [whole_in(pl.ANY)] * 2,
         out_specs=[whole_in(pltpu.VMEM)] * 2,
-        scratch_shapes=[pltpu.VMEM((half, size), bf16), pltpu.VMEM((size, half), bf16)],
+        scratch_shapes=[
+            pltpu.VMEM((shards, half_rows, size), f32),
+            pltpu.VMEM(root.shape, f32),
+            pltpu.VMEM((size, half), bf16),
+            pltpu.SemaphoreType.DMA((2,)),
+        ],
         compiler_params=pltpu.CompilerParams(vmem_limit_bytes=24 << 20),
         cost_estimate=pl.CostEstimate(flops=size**3, bytes_accessed=12 * size**2, transcendentals=0),
         name="orient",
@@ -164,15 +169,18 @@
     )(left, rows)
 
 
-def complete_kernel(part, left, rows, right, update, first):
+def complete_kernel(part, left, rows, right_in, update, first, right, arrived):
     half, size = part.shape
     width = size // 4
+    fetch = pltpu.make_async_copy(right_in, right, arrived)
+    fetch.start()
     for low in range(0, size, width):
         columns = slice(low, low + width)
         product = jnp.dot(
             left[1], rows[:, :, columns].reshape(half, width), preferred_element_type=f32
         )
         first[:, columns] = (part[:, columns] + product).astype(bf16)
+    fetch.wait()
     for low in range(0, size, width):
         columns = slice(low, low + width)
         update[:, columns] = jnp.dot(
@@ -185,9 +193,13 @@
     return pl.pallas_call(
         complete_kernel,
         out_shape=jax.ShapeDtypeStruct((half, size), bf16),
-        in_specs=[whole_in(pltpu.VMEM)] * 4,
+        in_specs=[whole_in(pltpu.VMEM)] * 3 + [whole_in(pl.ANY)],
         out_specs=whole_in(pltpu.VMEM),
-        scratch_shapes=[pltpu.VMEM((half, size), bf16)],
+        scratch_shapes=[
+            pltpu.VMEM((half, size), bf16),
+            pltpu.VMEM((size, size), bf16),
+            pltpu.SemaphoreType.DMA(()),
+        ],
         compiler_params=pltpu.CompilerParams(vmem_limit_bytes=24 << 20),
         cost_estimate=pl.CostEstimate(flops=2 * size**3, bytes_accessed=7 * size**2, transcendentals=0),
         name="complete",
@@ -321,7 +333,7 @@
     far_up = shifted(far[0], "dp", 1)
     far_down = shifted(far[1], "dp", -1)
 
-    root = in_order((roots[0, 0],), far)[0].astype(bf16).reshape(shards, 2, half_rows, size)
+    root = in_order((roots[0, 0],), far)[0].reshape(shards, 2, half_rows, size)
     partner_root = other_core(root)
     mine = in_order((mine,), (partner_root,))[0]
     near = lax.optimization_barrier((piece(mine, 1, 1), piece(mine, 3, 0)))

time: 138 us -> 135 us (0.978)
  other arithmetic: 4.85 us -> 2 us
  local copies, waits for them, and re-layouts: 14.8 us -> 12.9 us
    ppermute x2, waiting for transfers between devices: 1.44 us -> 5.88 us  [other_core(): return lax.ppermute(block, 'shard', [(i, i ^ 1) for i in range(count)])]
    ppermute x12, waiting for transfers between devices: 50.6 us -> 47.8 us  [shifted(): lax.ppermute(block, axis, [(i, (i + offset) % count) for i in range(count)])]
    convert_element_type x1 -> x0, other arithmetic: 2.51 us -> none  [on_device(): in_order((roots[0, 0],), far)[0].astype(bf16)]
    unnamed x22 -> x16, local copies, waits for them, and re-layouts: 8.79 us -> 6.93 us
where the time goes in v3:
time: 135 us
  waiting for transfers between devices  72.2 us (53%)
  starting transfers between devices  31.3 us (23%)
  Pallas kernels  15.5 us (11%)
  local copies, waits for them, and re-layouts  12.9 us (10%)
  other arithmetic  2 us (1%)
    ppermute x12, waiting for transfers between devices, shifted(): lax.ppermute(block, axis, [(i, (i + offset) % count) for i in range(count)])  47.8 us
    all_to_all x2, waiting for transfers between devices, exchanged(): lax.all_to_all(blocks, 'shard', split_axis=0, concat_axis=0, tiled=True)  18.6 us
    ppermute x12, starting transfers between devices, shifted(): lax.ppermute(block, axis, [(i, (i + offset) % count) for i in range(count)])  16.7 us
    all_to_all x2, starting transfers between devices, exchanged(): lax.all_to_all(blocks, 'shard', split_axis=0, concat_axis=0, tiled=True)  12.7 us
    unnamed x16, local copies, waits for them, and re-layouts  6.93 us
    ppermute x2, waiting for transfers between devices, other_core(): return lax.ppermute(block, 'shard', [(i, i ^ 1) for i in range(count)])  5.88 us
    pallas_call x1, Pallas kernels, statistics(): pl.pallas_call(statistics_kernel, grid=(size // tile,), out_shape=jax.Sha...  4.52 us
    pallas_call x1, Pallas kernels, completed(): pl.pallas_call(complete_kernel, out_shape=jax.ShapeDtypeStruct((half, siz...  3.1 us
  transfers between devices with their start and end apart: 16, of which 11 were waited for; matrix products, arithmetic and copies ran while one was open for 5% of the time, Pallas kernels for 6%

profile of v3, /device:TPU:1, one launch (start us, length us, event | category | flops | bytes accessed | tf_op | source)
XLA Modules:
  0.0 134.8 jit_solution(17188074539697431129)
XLA Ops:
  2.0 1.5 %collective-permute-start = (f32[32,2,16,1024]{3,2,1,0:T(8,128)}, f32[32,2,16,1024]{3,2,1,0:T(8,128)}, u32[]{:S(2)}, u32[]{:S(2)}) collective-permute-start(f32[32,2,16,1024]{3,2,1,0:T(8,128)} %bitcast.17), channel_id=1, source_target_pairs={{0,1},{1,0},{2,3},{3,2},{4,5},{5,4},{6,7},{7,6},{8,9},{9,8},{10,11... | collective-permute-start | bytes 12582920 | tf_op jit(solution)/shard_map/ppermute | solution.py:23
  3.5 1.4 %collective-permute-start.3 = (bf16[8,32,1024]{2,1,0:T(8,128)(2,1)S(1)}, bf16[8,32,1024]{2,1,0:T(8,128)(2,1)S(1)}, u32[]{:S(2)}, u32[]{:S(2)}) collective-permute-start(bf16[8,32,1024]{2,1,0:T(8,128)(2,1)S(1)} %get-tuple-element.27), channel_id=1, source_target_pairs={{0,32},{32,64},{64,96},{96,0},{1,33},{33,65},{65,97},{97,1},{2,34}... | collective-permute-start | bytes 1572872 | tf_op jit(solution)/shard_map/ppermute | solution.py:18
  4.9 1.4 %collective-permute-start.4 = (bf16[8,32,1024]{2,1,0:T(8,128)(2,1)S(1)}, bf16[8,32,1024]{2,1,0:T(8,128)(2,1)S(1)}, u32[]{:S(2)}, u32[]{:S(2)}) collective-permute-start(bf16[8,32,1024]{2,1,0:T(8,128)(2,1)S(1)} %get-tuple-element.28), channel_id=1, source_target_pairs={{0,96},{32,0},{64,32},{96,64},{1,97},{33,1},{65,33},{97,65},{2,98}... | collective-permute-start | bytes 1572872 | tf_op jit(solution)/shard_map/ppermute | solution.py:18
  6.3 4.3 %collective-permute-done.partner = f32[32,2,16,1024]{3,2,1,0:T(8,128)} collective-permute-done((f32[32,2,16,1024]{3,2,1,0:T(8,128)}, f32[32,2,16,1024]{3,2,1,0:T(8,128)}, u32[]{:S(2)}, u32[]{:S(2)}) %collective-permute-start) | collective-permute-done | bytes 4194336 | tf_op jit(solution)/shard_map/ppermute | solution.py:23
  11.9 1.4 %collective-permute-start.1 = (bf16[8,32,1024]{2,1,0:T(8,128)(2,1)S(1)}, bf16[8,32,1024]{2,1,0:T(8,128)(2,1)S(1)}, u32[]{:S(2)}, u32[]{:S(2)}) collective-permute-start(bf16[8,32,1024]{2,1,0:T(8,128)(2,1)S(1)} %get-tuple-element.31), channel_id=1, source_target_pairs={{0,32},{32,64},{64,96},{96,0},{1,33},{33,65},{65,97},{97,1},{2,34}... | collective-permute-start | bytes 1572872 | tf_op jit(solution)/shard_map/ppermute | solution.py:18
  13.3 1.5 %collective-permute-start.2 = (bf16[8,32,1024]{2,1,0:T(8,128)(2,1)S(1)}, bf16[8,32,1024]{2,1,0:T(8,128)(2,1)S(1)}, u32[]{:S(2)}, u32[]{:S(2)}) collective-permute-start(bf16[8,32,1024]{2,1,0:T(8,128)(2,1)S(1)} %get-tuple-element.32), channel_id=1, source_target_pairs={{0,96},{32,0},{64,32},{96,64},{1,97},{33,1},{65,33},{97,65},{2,98}... | collective-permute-start | bytes 1572872 | tf_op jit(solution)/shard_map/ppermute | solution.py:18
  14.9 3.6 %collective-permute-done.3 = bf16[8,32,1024]{2,1,0:T(8,128)(2,1)S(1)} collective-permute-done((bf16[8,32,1024]{2,1,0:T(8,128)(2,1)S(1)}, bf16[8,32,1024]{2,1,0:T(8,128)(2,1)S(1)}, u32[]{:S(2)}, u32[]{:S(2)}) %collective-permute-start.3) | collective-permute-done | bytes 524320 | tf_op jit(solution)/shard_map/ppermute | solution.py:18
  18.5 1.6 %add_convert_fusion = (bf16[8,32,1024]{2,1,0:T(8,128)(2,1)S(1)}, bf16[8,32,1024]{2,1,0:T(8,128)(2,1)S(1)}) fusion(bf16[8,32,1024]{2,1,0:T(8,128)(2,1)S(1)} %collective-permute-done.4, bf16[64,32,1024]{2,1,0:T(8,128)(2,1)} %bitcast.22, s32[]{:T(128)S(6)} %select_n.85, bf16[8,32,1024]{2,1,0:T(8,128)(2,1)S(1)} %collective-permute-done.3, s32[]{:T(128)S(6)} %select_n.84), kind=kLoop, calls=%fused_computation | loop fusion | flops 2097152 | bytes 3145736 | tf_op jit(solution)/shard_map/convert_element_type | solution.py:34
  21.0 1.8 %collective-permute-start.6 = (bf16[8,32,1024]{2,1,0:T(8,128)(2,1)S(1)}, bf16[8,32,1024]{2,1,0:T(8,128)(2,1)S(1)}, u32[]{:S(2)}, u32[]{:S(2)}) collective-permute-start(bf16[8,32,1024]{2,1,0:T(8,128)(2,1)S(1)} %get-tuple-element.39), channel_id=1, source_target_pairs={{0,96},{32,0},{64,32},{96,64},{1,97},{33,1},{65,33},{97,65},{2,98}... | collective-permute-start | bytes 1572872 | tf_op jit(solution)/shard_map/ppermute | solution.py:18
  22.8 1.3 constant_dynamic-slice_fusion.3
  24.1 5.6 %collective-permute-done.1 = bf16[8,32,1024]{2,1,0:T(8,128)(2,1)S(1)} collective-permute-done((bf16[8,32,1024]{2,1,0:T(8,128)(2,1)S(1)}, bf16[8,32,1024]{2,1,0:T(8,128)(2,1)S(1)}, u32[]{:S(2)}, u32[]{:S(2)}) %collective-permute-start.1) | collective-permute-done | bytes 524320 | tf_op jit(solution)/shard_map/ppermute | solution.py:18
  30.1 10.8 %collective-permute-done.5.sum_low = bf16[8,32,1024]{2,1,0:T(8,128)(2,1)S(1)} collective-permute-done((bf16[8,32,1024]{2,1,0:T(8,128)(2,1)S(1)}, bf16[8,32,1024]{2,1,0:T(8,128)(2,1)S(1)}, u32[]{:S(2)}, u32[]{:S(2)}) %collective-permute-start.5) | collective-permute-done | bytes 524320 | tf_op jit(solution)/shard_map/ppermute | solution.py:18
  40.9 2.0 %finish_sum.1 = bf16[16,32,1024]{2,1,0:T(8,128)(2,1)} custom-call(s32[16]{0:T(128)S(1)} %fusion.order, bf16[8,32,1024]{2,1,0:T(8,128)(2,1)S(1)} %get-tuple-element.36.low, bf16[8,32,1024]{2,1,0:T(8,128)(2,1)S(1)} %get-tuple-element.37.high, bf16[8,32,1024]{2,1,0:T(8,128)(2,1)S(1)} %collective-permute-done.5.sum_low, ...), custom_call_target="tpu_custom_call" | custom-call | flops 524288 | bytes 3145728 | tf_op jit(solution)/shard_map/finish_sum/pallas_call | solution.py:68
  43.0 8.7 %all-to-all-start = ((bf16[32,16,1024]{2,1,0:T(8,128)(2,1)}), bf16[32,16,1024]{2,1,0:T(8,128)(2,1)S(1)}, u32[]{:S(2)}, u32[]{:S(2)}) async-start(bf16[32,16,1024]{2,1,0:T(8,128)(2,1)} %bitcast.7), calls=%async_computation | async-start | bytes 2097152 | tf_op jit(solution)/shard_map/all_to_all | solution.py:27
  51.7 2.2 %copy-done.1 = f32[1,1,1024,1024]{3,2,1,0:T(8,128)S(1)} copy-done((f32[1,1,1024,1024]{3,2,1,0:T(8,128)S(1)}, f32[1,1,1024,1024]{3,2,1,0:T(8,128)}, u32[]{:S(2)}) %copy-start.1) | copy-done | bytes 4194328
  53.9 3.1 %orient.1 = (bf16[2,512,512]{2,1,0:T(8,128)(2,1)S(1)}, bf16[1024,1024]{1,0:T(8,128)(2,1)S(1)}) custom-call(s32[1]{0:T(128)} %bitcast.8.core, f32[32,2,16,1024]{3,2,1,0:T(8,128)S(1)} %bitcast.18, f32[32,2,16,1024]{3,2,1,0:T(8,128)} %collective-permute-done.partner), custom_call_target="tpu_custom_call" | custom-call | flops 1073741824 | bytes 12582912 | tf_op jit(solution)/shard_map/orient/pallas_call | solution.py:129
  57.0 1.3 copy-done.5
  58.3 10.6 %all-to-all-done.rows.own = bf16[32,16,1024]{2,1,0:T(8,128)(2,1)S(1)} async-done(((bf16[32,16,1024]{2,1,0:T(8,128)(2,1)}), bf16[32,16,1024]{2,1,0:T(8,128)(2,1)S(1)}, u32[]{:S(2)}, u32[]{:S(2)}) %all-to-all-start) | async-done | bytes 1048608 | tf_op jit(solution)/shard_map/all_to_all | solution.py:27
  69.9 1.6 %collective-permute-done.7.rows.other = bf16[32,16,1024]{2,1,0:T(8,128)(2,1)S(1)} collective-permute-done((bf16[32,16,1024]{2,1,0:T(8,128)(2,1)S(1)}, bf16[32,16,1024]{2,1,0:T(8,128)(2,1)S(1)}, u32[]{:S(2)}, u32[]{:S(2)}) %collective-permute-start.7) | collective-permute-done | bytes 1048608 | tf_op jit(solution)/shard_map/ppermute | solution.py:23
  71.5 3.1 %complete.1 = bf16[512,1024]{1,0:T(8,128)(2,1)} custom-call(f32[512,1024]{1,0:T(8,128)S(1)} %begin.1.part, bf16[2,512,512]{2,1,0:T(8,128)(2,1)S(1)} %get-tuple-element.44.left, bf16[32,16,1024]{2,1,0:T(8,128)(2,1)S(1)} %collective-permute-done.7.rows.other, bf16[1024,1024]{1,0:T(8,128)(2,1)S(1)} %copy-done.6), custom_call_target="tpu_custom_call" | custom-call | flops 2147483648 | bytes 7340032 | tf_op jit(solution)/shard_map/complete/pallas_call | solution.py:193
  74.6 4.0 %all-to-all-start.1 = ((bf16[32,16,1024]{2,1,0:T(8,128)(2,1)}), bf16[32,16,1024]{2,1,0:T(8,128)(2,1)S(1)}, u32[]{:S(2)}, u32[]{:S(2)}) async-start(bf16[32,16,1024]{2,1,0:T(8,128)(2,1)} %bitcast.9), calls=%async_computation.1 | async-start | bytes 2097152 | tf_op jit(solution)/shard_map/all_to_all | solution.py:27
  78.6 1.3 constant_dynamic-slice_fusion.old
  80.0 2.2 %copy-done.2 = f32[1,1,1024,1024]{3,2,1,0:T(8,128)S(1)} copy-done((f32[1,1,1024,1024]{3,2,1,0:T(8,128)S(1)}, f32[1,1,1024,1024]{3,2,1,0:T(8,128)}, u32[]{:S(2)}) %copy-start.2) | copy-done | bytes 4194328
  83.4 4.5 %statistics.1 = f32[1024,1024]{1,0:T(8,128)} custom-call(s32[1]{0:T(128)} %bitcast.8.core, bf16[32,16,1024]{2,1,0:T(8,128)(2,1)S(1)} %all-to-all-done.rows.own, bf16[32,16,1024]{2,1,0:T(8,128)(2,1)S(1)} %copy-done.4, f32[1024,1024]{1,0:T(8,128)S(1)} %bitcast.19), custom_call_target="tpu_custom_call" | custom-call | flops 2147483648 | bytes 12582912 | tf_op jit(solution)/shard_map/statistics/pallas_call | solution.py:240
  87.9 8.0 %all-to-all-done.1 = bf16[32,16,1024]{2,1,0:T(8,128)(2,1)S(1)} async-done(((bf16[32,16,1024]{2,1,0:T(8,128)(2,1)}), bf16[32,16,1024]{2,1,0:T(8,128)(2,1)S(1)}, u32[]{:S(2)}, u32[]{:S(2)}) %all-to-all-start.1) | async-done | bytes 1048608 | tf_op jit(solution)/shard_map/all_to_all | solution.py:27
  97.0 1.4 %collective-permute-start.8 = (bf16[8,32,1024]{2,1,0:T(8,128)(2,1)S(1)}, bf16[8,32,1024]{2,1,0:T(8,128)(2,1)S(1)}, u32[]{:S(2)}, u32[]{:S(2)}) collective-permute-start(bf16[8,32,1024]{2,1,0:T(8,128)(2,1)S(1)} %get-tuple-element.49), channel_id=1, source_target_pairs={{0,32},{32,64},{64,96},{96,0},{1,33},{33,65},{65,97},{97,1},{2,34}... | collective-permute-start | bytes 1572872 | tf_op jit(solution)/shard_map/ppermute | solution.py:18
  98.4 1.4 %collective-permute-start.10 = (bf16[8,32,1024]{2,1,0:T(8,128)(2,1)S(1)}, bf16[8,32,1024]{2,1,0:T(8,128)(2,1)S(1)}, u32[]{:S(2)}, u32[]{:S(2)}) collective-permute-start(bf16[8,32,1024]{2,1,0:T(8,128)(2,1)S(1)} %get-tuple-element.50), channel_id=1, source_target_pairs={{0,96},{32,0},{64,32},{96,64},{1,97},{33,1},{65,33},{97,65},{2,98}... | collective-permute-start | bytes 1572872 | tf_op jit(solution)/shard_map/ppermute | solution.py:18
  99.8 2.6 %collective-permute-start.13 = (bf16[8,32,1024]{2,1,0:T(8,128)(2,1)S(1)}, bf16[8,32,1024]{2,1,0:T(8,128)(2,1)S(1)}, u32[]{:S(2)}, u32[]{:S(2)}) collective-permute-start(bf16[8,32,1024]{2,1,0:T(8,128)(2,1)S(1)} %get-tuple-element.49), channel_id=1, source_target_pairs={{0,96},{32,0},{64,32},{96,64},{1,97},{33,1},{65,33},{97,65},{2,98}... | collective-permute-start | bytes 1572872 | tf_op jit(solution)/shard_map/ppermute | solution.py:18
  102.5 8.9 %collective-permute-done.8 = bf16[8,32,1024]{2,1,0:T(8,128)(2,1)S(1)} collective-permute-done((bf16[8,32,1024]{2,1,0:T(8,128)(2,1)S(1)}, bf16[8,32,1024]{2,1,0:T(8,128)(2,1)S(1)}, u32[]{:S(2)}, u32[]{:S(2)}) %collective-permute-start.8) | collective-permute-done | bytes 524320 | tf_op jit(solution)/shard_map/ppermute | solution.py:18
  112.1 2.7 %collective-permute-start.11 = (bf16[8,32,1024]{2,1,0:T(8,128)(2,1)S(1)}, bf16[8,32,1024]{2,1,0:T(8,128)(2,1)S(1)}, u32[]{:S(2)}, u32[]{:S(2)}) collective-permute-start(bf16[8,32,1024]{2,1,0:T(8,128)(2,1)S(1)} %collective-permute-done.10), channel_id=1, source_target_pairs={{0,96},{32,0},{64,32},{96,64},{1,97},{33,1},{65,33},{97,65},{2,98}... | collective-permute-start | bytes 1572872 | tf_op jit(solution)/shard_map/ppermute | solution.py:18
  114.9 7.7 %collective-permute-done.12 = bf16[8,32,1024]{2,1,0:T(8,128)(2,1)S(1)} collective-permute-done((bf16[8,32,1024]{2,1,0:T(8,128)(2,1)S(1)}, bf16[8,32,1024]{2,1,0:T(8,128)(2,1)S(1)}, u32[]{:S(2)}, u32[]{:S(2)}) %collective-permute-start.12) | collective-permute-done | bytes 524320 | tf_op jit(solution)/shard_map/ppermute | solution.py:18
  122.7 10.9 %collective-permute-done.11.high_far = bf16[8,32,1024]{2,1,0:T(8,128)(2,1)S(1)} collective-permute-done((bf16[8,32,1024]{2,1,0:T(8,128)(2,1)S(1)}, bf16[8,32,1024]{2,1,0:T(8,128)(2,1)S(1)}, u32[]{:S(2)}, u32[]{:S(2)}) %collective-permute-start.11) | collective-permute-done | bytes 524320 | tf_op jit(solution)/shard_map/ppermute | solution.py:18
  (37 shorter events, 9.5 us)
Async XLA Ops:
  0.6 22.2 %copy-start = (s32[4,16]{1,0:T(4,128)S(1)}, s32[4,16]{1,0:T(4,128)}, u32[]{:S(2)}) copy-start(s32[4,16]{1,0:T(4,128)} %param.9) | copy-start | bytes 772
  2.0 8.6 %collective-permute-start = (f32[32,2,16,1024]{3,2,1,0:T(8,128)}, f32[32,2,16,1024]{3,2,1,0:T(8,128)}, u32[]{:S(2)}, u32[]{:S(2)}) collective-permute-start(f32[32,2,16,1024]{3,2,1,0:T(8,128)} %bitcast.17), channel_id=1, source_target_pairs={{0,1},{1,0},{2,3},{3,2},{4,5},{5,4},{6,7},{7,6},{8,9},{9,8},{10,11... | collective-permute-start | bytes 12582920 | tf_op jit(solution)/shard_map/ppermute | solution.py:23
  3.5 15.0 %collective-permute-start.3 = (bf16[8,32,1024]{2,1,0:T(8,128)(2,1)S(1)}, bf16[8,32,1024]{2,1,0:T(8,128)(2,1)S(1)}, u32[]{:S(2)}, u32[]{:S(2)}) collective-permute-start(bf16[8,32,1024]{2,1,0:T(8,128)(2,1)S(1)} %get-tuple-element.27), channel_id=1, source_target_pairs={{0,32},{32,64},{64,96},{96,0},{1,33},{33,65},{65,97},{97,1},{2,34}... | collective-permute-start | bytes 1572872 | tf_op jit(solution)/shard_map/ppermute | solution.py:18
  4.9 13.6 %collective-permute-start.4 = (bf16[8,32,1024]{2,1,0:T(8,128)(2,1)S(1)}, bf16[8,32,1024]{2,1,0:T(8,128)(2,1)S(1)}, u32[]{:S(2)}, u32[]{:S(2)}) collective-permute-start(bf16[8,32,1024]{2,1,0:T(8,128)(2,1)S(1)} %get-tuple-element.28), channel_id=1, source_target_pairs={{0,96},{32,0},{64,32},{96,64},{1,97},{33,1},{65,33},{97,65},{2,98}... | collective-permute-start | bytes 1572872 | tf_op jit(solution)/shard_map/ppermute | solution.py:18
  11.9 17.8 %collective-permute-start.1 = (bf16[8,32,1024]{2,1,0:T(8,128)(2,1)S(1)}, bf16[8,32,1024]{2,1,0:T(8,128)(2,1)S(1)}, u32[]{:S(2)}, u32[]{:S(2)}) collective-permute-start(bf16[8,32,1024]{2,1,0:T(8,128)(2,1)S(1)} %get-tuple-element.31), channel_id=1, source_target_pairs={{0,32},{32,64},{64,96},{96,0},{1,33},{33,65},{65,97},{97,1},{2,34}... | collective-permute-start | bytes 1572872 | tf_op jit(solution)/shard_map/ppermute | solution.py:18
  13.3 16.3 %collective-permute-start.2 = (bf16[8,32,1024]{2,1,0:T(8,128)(2,1)S(1)}, bf16[8,32,1024]{2,1,0:T(8,128)(2,1)S(1)}, u32[]{:S(2)}, u32[]{:S(2)}) collective-permute-start(bf16[8,32,1024]{2,1,0:T(8,128)(2,1)S(1)} %get-tuple-element.32), channel_id=1, source_target_pairs={{0,96},{32,0},{64,32},{96,64},{1,97},{33,1},{65,33},{97,65},{2,98}... | collective-permute-start | bytes 1572872 | tf_op jit(solution)/shard_map/ppermute | solution.py:18
  20.0 20.9 %collective-permute-start.5 = (bf16[8,32,1024]{2,1,0:T(8,128)(2,1)S(1)}, bf16[8,32,1024]{2,1,0:T(8,128)(2,1)S(1)}, u32[]{:S(2)}, u32[]{:S(2)}) collective-permute-start(bf16[8,32,1024]{2,1,0:T(8,128)(2,1)S(1)} %get-tuple-element.38), channel_id=1, source_target_pairs={{0,32},{32,64},{64,96},{96,0},{1,33},{33,65},{65,97},{97,1},{2,34}... | collective-permute-start | bytes 1572872 | tf_op jit(solution)/shard_map/ppermute | solution.py:18
  21.0 19.9 %collective-permute-start.6 = (bf16[8,32,1024]{2,1,0:T(8,128)(2,1)S(1)}, bf16[8,32,1024]{2,1,0:T(8,128)(2,1)S(1)}, u32[]{:S(2)}, u32[]{:S(2)}) collective-permute-start(bf16[8,32,1024]{2,1,0:T(8,128)(2,1)S(1)} %get-tuple-element.39), channel_id=1, source_target_pairs={{0,96},{32,0},{64,32},{96,64},{1,97},{33,1},{65,33},{97,65},{2,98}... | collective-permute-start | bytes 1572872 | tf_op jit(solution)/shard_map/ppermute | solution.py:18
  43.0 25.9 %all-to-all-start = ((bf16[32,16,1024]{2,1,0:T(8,128)(2,1)}), bf16[32,16,1024]{2,1,0:T(8,128)(2,1)S(1)}, u32[]{:S(2)}, u32[]{:S(2)}) async-start(bf16[32,16,1024]{2,1,0:T(8,128)(2,1)} %bitcast.7), calls=%async_computation | async-start | bytes 2097152 | tf_op jit(solution)/shard_map/all_to_all | solution.py:27
  51.7 2.2 %copy-start.1 = (f32[1,1,1024,1024]{3,2,1,0:T(8,128)S(1)}, f32[1,1,1024,1024]{3,2,1,0:T(8,128)}, u32[]{:S(2)}) copy-start(f32[1,1,1024,1024]{3,2,1,0:T(8,128)} %param.8) | copy-start | bytes 12582916
  56.9 1.3 copy-start.5
  68.8 2.7 %copy-start.6 = (bf16[1024,1024]{1,0:T(8,128)(2,1)S(1)}, bf16[1024,1024]{1,0:T(8,128)(2,1)}, u32[]{:S(2)}) copy-start(bf16[1024,1024]{1,0:T(8,128)(2,1)} %copy-done.5) | copy-start | bytes 6291460
  68.8 2.7 %collective-permute-start.7 = (bf16[32,16,1024]{2,1,0:T(8,128)(2,1)S(1)}, bf16[32,16,1024]{2,1,0:T(8,128)(2,1)S(1)}, u32[]{:S(2)}, u32[]{:S(2)}) collective-permute-start(bf16[32,16,1024]{2,1,0:T(8,128)(2,1)S(1)} %all-to-all-done.rows.own), channel_id=1, source_target_pairs={{0,1},{1,0},{2,3},{3,2},{4,5},{5,4},{6,7},{7,6},{8,9},{9,8},{10,11... | collective-permute-start | bytes 3145736 | tf_op jit(solution)/shard_map/ppermute | solution.py:23
  71.5 3.1 %copy-start.3 = (bf16[32,16,1024]{2,1,0:T(8,128)(2,1)}, bf16[32,16,1024]{2,1,0:T(8,128)(2,1)S(1)}, u32[]{:S(2)}) copy-start(bf16[32,16,1024]{2,1,0:T(8,128)(2,1)S(1)} %collective-permute-done.7.rows.other) | copy-start | bytes 3145732
  74.6 21.3 %all-to-all-start.1 = ((bf16[32,16,1024]{2,1,0:T(8,128)(2,1)}), bf16[32,16,1024]{2,1,0:T(8,128)(2,1)S(1)}, u32[]{:S(2)}, u32[]{:S(2)}) async-start(bf16[32,16,1024]{2,1,0:T(8,128)(2,1)} %bitcast.9), calls=%async_computation.1 | async-start | bytes 2097152 | tf_op jit(solution)/shard_map/all_to_all | solution.py:27
  80.0 2.2 %copy-start.2 = (f32[1,1,1024,1024]{3,2,1,0:T(8,128)S(1)}, f32[1,1,1024,1024]{3,2,1,0:T(8,128)}, u32[]{:S(2)}) copy-start(f32[1,1,1024,1024]{3,2,1,0:T(8,128)} %param.7) | copy-start | bytes 12582916
  82.1 1.2 copy-start.4
  97.0 14.4 %collective-permute-start.8 = (bf16[8,32,1024]{2,1,0:T(8,128)(2,1)S(1)}, bf16[8,32,1024]{2,1,0:T(8,128)(2,1)S(1)}, u32[]{:S(2)}, u32[]{:S(2)}) collective-permute-start(bf16[8,32,1024]{2,1,0:T(8,128)(2,1)S(1)} %get-tuple-element.49), channel_id=1, source_target_pairs={{0,32},{32,64},{64,96},{96,0},{1,33},{33,65},{65,97},{97,1},{2,34}... | collective-permute-start | bytes 1572872 | tf_op jit(solution)/shard_map/ppermute | solution.py:18
  98.4 13.7 %collective-permute-start.10 = (bf16[8,32,1024]{2,1,0:T(8,128)(2,1)S(1)}, bf16[8,32,1024]{2,1,0:T(8,128)(2,1)S(1)}, u32[]{:S(2)}, u32[]{:S(2)}) collective-permute-start(bf16[8,32,1024]{2,1,0:T(8,128)(2,1)S(1)} %get-tuple-element.50), channel_id=1, source_target_pairs={{0,96},{32,0},{64,32},{96,64},{1,97},{33,1},{65,33},{97,65},{2,98}... | collective-permute-start | bytes 1572872 | tf_op jit(solution)/shard_map/ppermute | solution.py:18
  99.8 22.8 %collective-permute-start.12 = (bf16[8,32,1024]{2,1,0:T(8,128)(2,1)S(1)}, bf16[8,32,1024]{2,1,0:T(8,128)(2,1)S(1)}, u32[]{:S(2)}, u32[]{:S(2)}) collective-permute-start(bf16[8,32,1024]{2,1,0:T(8,128)(2,1)S(1)} %get-tuple-element.50), channel_id=1, source_target_pairs={{0,32},{32,64},{64,96},{96,0},{1,33},{33,65},{65,97},{97,1},{2,34}... | collective-permute-start | bytes 1572872 | tf_op jit(solution)/shard_map/ppermute | solution.py:18
  99.8 22.8 %collective-permute-start.13 = (bf16[8,32,1024]{2,1,0:T(8,128)(2,1)S(1)}, bf16[8,32,1024]{2,1,0:T(8,128)(2,1)S(1)}, u32[]{:S(2)}, u32[]{:S(2)}) collective-permute-start(bf16[8,32,1024]{2,1,0:T(8,128)(2,1)S(1)} %get-tuple-element.49), channel_id=1, source_target_pairs={{0,96},{32,0},{64,32},{96,64},{1,97},{33,1},{65,33},{97,65},{2,98}... | collective-permute-start | bytes 1572872 | tf_op jit(solution)/shard_map/ppermute | solution.py:18
  111.4 22.5 %collective-permute-start.9 = (bf16[8,32,1024]{2,1,0:T(8,128)(2,1)S(1)}, bf16[8,32,1024]{2,1,0:T(8,128)(2,1)S(1)}, u32[]{:S(2)}, u32[]{:S(2)}) collective-permute-start(bf16[8,32,1024]{2,1,0:T(8,128)(2,1)S(1)} %collective-permute-done.8), channel_id=1, source_target_pairs={{0,32},{32,64},{64,96},{96,0},{1,33},{33,65},{65,97},{97,1},{2,34}... | collective-permute-start | bytes 1572872 | tf_op jit(solution)/shard_map/ppermute | solution.py:18
  112.1 21.6 %collective-permute-start.11 = (bf16[8,32,1024]{2,1,0:T(8,128)(2,1)S(1)}, bf16[8,32,1024]{2,1,0:T(8,128)(2,1)S(1)}, u32[]{:S(2)}, u32[]{:S(2)}) collective-permute-start(bf16[8,32,1024]{2,1,0:T(8,128)(2,1)S(1)} %collective-permute-done.10), channel_id=1, source_target_pairs={{0,96},{32,0},{64,32},{96,64},{1,97},{33,1},{65,33},{97,65},{2,98}... | collective-permute-start | bytes 1572872 | tf_op jit(solution)/shard_map/ppermute | solution.py:18
  122.7 11.1 %copy-start.7 = (bf16[64,32,1024]{2,1,0:T(8,128)(2,1)}, bf16[64,32,1024]{2,1,0:T(8,128)(2,1)S(1)}, u32[]{:S(2)}) copy-start(bf16[64,32,1024]{2,1,0:T(8,128)(2,1)S(1)} %constant_dynamic-update-slice_fusion.below) | copy-start | bytes 12582916

commit v4 on v3

--- a/solution.py
+++ b/solution.py
@@ -43,167 +43,185 @@
     return pl.BlockSpec(memory_space=space)
 
 
-def finish_sum_kernel(order, low, high, sum_low, sum_high, out):
+def finish_sum_kernel(order, low, high, sum_low, sum_high, out, made, sems):
     half = low.shape[0]
+    columns = out.shape[3]
+
+    def sent(place, side):
+        source = made.at[place, :, pl.ds(side * columns, columns)]
+        return pltpu.make_async_copy(source, out.at[place, side], sems.at[side])
 
     def step(place, carry):
         block = order[place]
 
         @pl.when(block < half)
         def _():
-            out[place] = added(low[block], sum_low[block])
+            made[place] = added(low[block], sum_low[block])
 
         @pl.when(block >= half)
         def _():
-            out[place] = added(high[block - half], sum_high[block - half])
-
+            made[place] = added(high[block - half], sum_high[block - half])
+
+        for side in range(2):
+            sent(place, side).start()
         return carry
 
-    lax.fori_loop(0, out.shape[0], step, 0)
+    def finish(place, carry):
+        for side in range(2):
+            sent(place, side).wait()
+        return carry
+
+    lax.fori_loop(0, made.shape[0], step, 0)
+    lax.fori_loop(0, made.shape[0], finish, 0)
 
 
 def finish_sum(order, *terms):
-    shape = (order.shape[0],) + terms[0].shape[1:]
+    group, (rows, columns) = order.shape[0], terms[0].shape[1:]
     size = terms[0].size * 2
     return pl.pallas_call(
         finish_sum_kernel,
-        out_shape=jax.ShapeDtypeStruct(shape, bf16),
+        out_shape=jax.ShapeDtypeStruct((group, 2, rows, columns // 2), bf16),
         in_specs=[whole_in(pltpu.SMEM)] + [whole_in(pltpu.VMEM)] * 4,
-        out_specs=whole_in(pltpu.VMEM),
+        out_specs=whole_in(pl.ANY),
+        scratch_shapes=[pltpu.VMEM((group, rows, columns), bf16), pltpu.SemaphoreType.DMA((2,))],
         compiler_params=pltpu.CompilerParams(vmem_limit_bytes=16 << 20),
         cost_estimate=pl.CostEstimate(flops=size, bytes_accessed=6 * size, transcendentals=0),
         name="finish_sum",
     )(order, *terms)
 
 
-def interleaved(core, own, other, gradient):
-    half_rows = own.shape[1]
-
-    def place(shard, carry):
-        start = shard * 2 * half_rows
-        here = pl.multiple_of(start + core * half_rows, half_rows)
-        there = pl.multiple_of(start + (1 - core) * half_rows, half_rows)
-        gradient[pl.ds(here, half_rows), :] = own[shard]
-        gradient[pl.ds(there, half_rows), :] = other[shard]
-        return carry
-
-    lax.fori_loop(0, own.shape[0], place, 0, unroll=4)
-
-
-def orient_kernel(core, root, partner, left, right, left_in, right_in, moved, sems):
-    shards, half_rows, size = left_in.shape
-    half = size // 2
-
-    def left_copy(source, which):
-        return pltpu.make_async_copy(source.at[:, which], left_in, sems.at[0])
+def orient_kernel(
+    core, root, root_halves, partner, partner_halves, left, right, left_in, right_in, sems
+):
+    shards, _, half_rows, size = left_in.shape
+    mine = core[0]
+
+    def left_copy(source):
+        return pltpu.make_async_copy(source, left_in, sems.at[0])
 
     def right_copy(source):
         return pltpu.make_async_copy(source, right_in, sems.at[1])
 
-    @pl.when(core[0] == 0)
-    def _():
-        left_copy(root, 0).start()
-        right_copy(partner).start()
-
-    @pl.when(core[0] == 1)
-    def _():
-        left_copy(partner, 1).start()
-        right_copy(root).start()
-
-    left_copy(root, 0).wait()
-    rows = left_in[...].reshape(half, size).astype(bf16)
-    for side in range(2):
-        place = lax.broadcasted_iota(jnp.int32, (size, half), 1)
-        which = core[0] if side == 0 else 1 - core[0]
-        source = 2 * half_rows * (place // half_rows) + which * half_rows + place % half_rows
-        chosen = lax.broadcasted_iota(jnp.int32, (size, half), 0) == source
-        moved[...] = jnp.where(chosen, 1.0, 0.0).astype(bf16)
-        left[side] = jnp.dot(rows, moved[...], preferred_element_type=f32).astype(bf16)
-    right_copy(root).wait()
-    right[...] = right_in[...].reshape(size, size).astype(bf16)
-
-
-def oriented(core, root, partner):
-    shards, _, half_rows, size = root.shape
+    @pl.when(mine == 0)
+    def _():
+        left_copy(root).start()
+        right_copy(partner_halves).start()
+
+    @pl.when(mine == 1)
+    def _():
+        left_copy(partner).start()
+        right_copy(root_halves).start()
+
+    left_copy(root).wait()
+
+    def place(shard, carry):
+        rows = pl.ds(pl.multiple_of(shard * half_rows, half_rows), half_rows)
+        left[0, rows, :] = left_in[shard, mine].astype(bf16)
+        left[1, rows, :] = left_in[shard, 1 - mine].astype(bf16)
+        return carry
+
+    lax.fori_loop(0, shards, place, 0, unroll=4)
+    right_copy(root_halves).wait()
+    right[0] = right_in[mine].astype(bf16)
+    right[1] = right_in[1 - mine].astype(bf16)
+
+
+def oriented(core, root, partner, half_rows):
+    size = root.shape[0]
     half = size // 2
+    tall = (size // (2 * half_rows), 2, half_rows, size)
+    root, partner = (
+        (array.reshape(tall), array.reshape(2, half, size)) for array in (root, partner)
+    )
     return pl.pallas_call(
         orient_kernel,
-        out_shape=[
-            jax.ShapeDtypeStruct((2, half, half), bf16),
-            jax.ShapeDtypeStruct((size, size), bf16),
-        ],
-        in_specs=[whole_in(pltpu.SMEM)] + [whole_in(pl.ANY)] * 2,
+        out_shape=[jax.ShapeDtypeStruct((2, half, size), bf16)] * 2,
+        in_specs=[whole_in(pltpu.SMEM)] + [whole_in(pl.ANY)] * 4,
         out_specs=[whole_in(pltpu.VMEM)] * 2,
         scratch_shapes=[
-            pltpu.VMEM((shards, half_rows, size), f32),
-            pltpu.VMEM(root.shape, f32),
-            pltpu.VMEM((size, half), bf16),
+            pltpu.VMEM(tall, f32),
+            pltpu.VMEM((2, half, size), f32),
             pltpu.SemaphoreType.DMA((2,)),
         ],
-        compiler_params=pltpu.CompilerParams(vmem_limit_bytes=24 << 20),
-        cost_estimate=pl.CostEstimate(flops=size**3, bytes_accessed=12 * size**2, transcendentals=0),
+        compiler_params=pltpu.CompilerParams(vmem_limit_bytes=32 << 20),
+        cost_estimate=pl.CostEstimate(flops=size**2, bytes_accessed=12 * size**2, transcendentals=0),
         name="orient",
-    )(core, root, partner)
-
-
-def begin_kernel(left, rows, part):
-    half, size = part.shape
+    )(core, *root, *partner)
+
+
+def begin_kernel(left, columns, kept, swapped):
+    size, half = left.shape[2], left.shape[1]
+    rows = columns[...].reshape(size, half)
+    tile = half // 2
+    for side, out in ((1, swapped), (0, kept)):
+        for low in range(0, half, tile):
+            out[low : low + tile, :] = jnp.dot(
+                left[side, low : low + tile, :], rows, preferred_element_type=f32
+            ).astype(bf16)
+
+
+def begun(left, columns):
+    half = left.shape[1]
+    return pl.pallas_call(
+        begin_kernel,
+        out_shape=[jax.ShapeDtypeStruct((half, half), bf16)] * 2,
+        in_specs=[whole_in(pltpu.VMEM)] * 2,
+        out_specs=[whole_in(pltpu.VMEM)] * 2,
+        compiler_params=pltpu.CompilerParams(vmem_limit_bytes=16 << 20),
+        cost_estimate=pl.CostEstimate(flops=8 * half**3, bytes_accessed=16 * half**2, transcendentals=0),
+        name="begin",
+    )(left, columns)
+
+
+def share_kernel(kept, right, part):
+    size = part.shape[1]
     width = size // 4
     for low in range(0, size, width):
         columns = slice(low, low + width)
-        part[:, columns] = jnp.dot(
-            left[0], rows[:, :, columns].reshape(half, width), preferred_element_type=f32
-        )
-
-
-def begun(left, rows):
-    half, size = left.shape[1], rows.shape[2]
-    return pl.pallas_call(
-        begin_kernel,
+        part[:, columns] = jnp.dot(kept[...], right[0, :, columns], preferred_element_type=f32)
+
+
+def shared(kept, right):
+    half, size = right.shape[1:]
+    return pl.pallas_call(
+        share_kernel,
         out_shape=jax.ShapeDtypeStruct((half, size), f32),
         in_specs=[whole_in(pltpu.VMEM)] * 2,
         out_specs=whole_in(pltpu.VMEM),
         compiler_params=pltpu.CompilerParams(vmem_limit_bytes=16 << 20),
-        cost_estimate=pl.CostEstimate(flops=size**3 // 2, bytes_accessed=4 * size**2, transcendentals=0),
-        name="begin",
-    )(left, rows)
-
-
-def complete_kernel(part, left, rows, right_in, update, first, right, arrived):
-    half, size = part.shape
+        cost_estimate=pl.CostEstimate(flops=4 * half**3, bytes_accessed=16 * half**2, transcendentals=0),
+        name="share",
+    )(kept, right)
+
+
+def complete_kernel(part, other, right, update, made, sems):
+    size = part.shape[1]
     width = size // 4
-    fetch = pltpu.make_async_copy(right_in, right, arrived)
-    fetch.start()
-    for low in range(0, size, width):
+    copies = []
+    for index, low in enumerate(range(0, size, width)):
         columns = slice(low, low + width)
-        product = jnp.dot(
-            left[1], rows[:, :, columns].reshape(half, width), preferred_element_type=f32
+        product = jnp.dot(other[...], right[1, :, columns], preferred_element_type=f32)
+        made[:, columns] = (part[:, columns] + product).astype(bf16)
+        copies.append(
+            pltpu.make_async_copy(made.at[:, columns], update.at[:, columns], sems.at[index])
         )
-        first[:, columns] = (part[:, columns] + product).astype(bf16)
-    fetch.wait()
-    for low in range(0, size, width):
-        columns = slice(low, low + width)
-        update[:, columns] = jnp.dot(
-            first[...], right[:, columns], preferred_element_type=f32
-        ).astype(bf16)
-
-
-def completed(part, left, rows, right):
+        copies[-1].start()
+    for copy in copies:
+        copy.wait()
+
+
+def completed(part, other, right):
     half, size = part.shape
     return pl.pallas_call(
         complete_kernel,
         out_shape=jax.ShapeDtypeStruct((half, size), bf16),
-        in_specs=[whole_in(pltpu.VMEM)] * 3 + [whole_in(pl.ANY)],
-        out_specs=whole_in(pltpu.VMEM),
-        scratch_shapes=[
-            pltpu.VMEM((half, size), bf16),
-            pltpu.VMEM((size, size), bf16),
-            pltpu.SemaphoreType.DMA(()),
-        ],
-        compiler_params=pltpu.CompilerParams(vmem_limit_bytes=24 << 20),
-        cost_estimate=pl.CostEstimate(flops=2 * size**3, bytes_accessed=7 * size**2, transcendentals=0),
+        in_specs=[whole_in(pltpu.VMEM)] * 3,
+        out_specs=whole_in(pl.ANY),
+        scratch_shapes=[pltpu.VMEM((half, size), bf16), pltpu.SemaphoreType.DMA((4,))],
+        compiler_params=pltpu.CompilerParams(vmem_limit_bytes=16 << 20),
+        cost_estimate=pl.CostEstimate(flops=4 * half**3, bytes_accessed=16 * half**2, transcendentals=0),
         name="complete",
-    )(part, left, rows, right)
+    )(part, other, right)
 
 
 def statistics_kernel(core, own, other, stat, out, gradient):
@@ -212,9 +230,15 @@
     step = pl.program_id(0)
     mine = core[0]
 
-    @pl.when(step == 0)
-    def _():
-        interleaved(mine, own, other, gradient)
+    @pl.when((step == 0) & (mine == 0))
+    def _():
+        gradient[:, : size // 2] = own[...].reshape(size, size // 2)
+        gradient[:, size // 2 :] = other[...].reshape(size, size // 2)
+
+    @pl.when((step == 0) & (mine == 1))
+    def _():
+        gradient[:, size // 2 :] = own[...].reshape(size, size // 2)
+        gradient[:, : size // 2] = other[...].reshape(size, size // 2)
 
     rows = pl.ds(pl.multiple_of(step * tile, tile), tile)
 
@@ -333,7 +357,7 @@
     far_up = shifted(far[0], "dp", 1)
     far_down = shifted(far[1], "dp", -1)
 
-    root = in_order((roots[0, 0],), far)[0].reshape(shards, 2, half_rows, size)
+    root = in_order((roots[0, 0],), far)[0]
     partner_root = other_core(root)
     mine = in_order((mine,), (partner_root,))[0]
     near = lax.optimization_barrier((piece(mine, 1, 1), piece(mine, 3, 0)))
@@ -349,18 +373,21 @@
         (lax.dynamic_slice_in_dim(mine, replica * group, group, 0), near_up, near_down)
     )
     partial = lax.optimization_barrier((added(own[:half], near_down), added(own[half:], near_up)))
+    root, partner_root = in_order((root, partner_root), partial)
+    left, right = oriented(core, root, partner_root, half_rows)
+    sum_up, sum_down, left, right = lax.optimization_barrier((sum_up, sum_down, left, right))
     whole = finish_sum(own_order, *partial, sum_up, sum_down)
 
-    own_rows = exchanged(whole.reshape(shards, half_rows, size))
-    root, partner_root = in_order((root, partner_root), (whole,))
-    left, right = oriented(core, root, partner_root)
-    own_rows, left, right = lax.optimization_barrier((own_rows, left, right))
-    other_rows = other_core(own_rows)
-    part = begun(left, own_rows)
-    update = completed(part, left, other_rows, right)
-
+    own_columns = exchanged(whole.reshape(shards, rows, size // 2))
+    kept, swapped = begun(left, own_columns)
+    swapped = other_core(swapped)
+    part = shared(kept, right)
+    update = completed(part, swapped, right)
+
+    own_columns = in_order((own_columns,), (update,))[0]
     update = exchanged(update.reshape(shards, half_rows, size))
-    new_stat = statistics(core, own_rows, other_rows, stats[0, 0])
+    other_columns = other_core(own_columns)
+    new_stat = statistics(core, own_columns, other_columns, stats[0, 0])
     own_params = lax.dynamic_slice_in_dim(params, replica * group, group, 0)
     update, new_stat, own_params = lax.optimization_barrier((update, new_stat, own_params))
     low, high = stepped(own_order, own_params, update.reshape(group, rows, size))

time: 135 us -> 134 us (level)
  blocking collectives: 0 us -> 25.7 us
  waiting for transfers between devices: 72.2 us -> 58.2 us
  starting transfers between devices: 31.3 us -> 22.9 us
  local copies, waits for them, and re-layouts: 12.9 us -> 8.2 us
    all_to_all x0 -> x1, blocking collectives: none -> 25.7 us  [exchanged(): lax.all_to_all(blocks, 'shard', split_axis=0, concat_axis=0, tiled=True)]
    all_to_all x2 -> x1, waiting for transfers between devices: 18.6 us -> 8.04 us  [exchanged(): lax.all_to_all(blocks, 'shard', split_axis=0, concat_axis=0, tiled=True)]
    all_to_all x2 -> x1, starting transfers between devices: 12.7 us -> 3.73 us  [exchanged(): lax.all_to_all(blocks, 'shard', split_axis=0, concat_axis=0, tiled=True)]
    unnamed x16 -> x8, local copies, waits for them, and re-layouts: 6.93 us -> 2.21 us
    ppermute x12, waiting for transfers between devices: 47.8 us -> 45.1 us  [shifted(): lax.ppermute(block, axis, [(i, (i + offset) % count) for i in range(count)])]
    pallas_call x1, Pallas kernels: 3.1 us -> 1.59 us  [completed(): pl.pallas_call(complete_kernel, out_shape=jax.ShapeDtypeStruct((half, siz...]
    ppermute x2 -> x3, waiting for transfers between devices: 5.88 us -> 5.14 us  [other_core(): return lax.ppermute(block, 'shard', [(i, i ^ 1) for i in range(count)])]
    pallas_call x3 -> x4, Pallas kernels: 5.83 us -> 6.19 us  [the longest x1 2.65 us: oriented(): pl.pallas_call(orient_kernel, out_shape=[jax.ShapeDtypeStruct((2, half, s...]
  transfers between devices with their start and end apart: 16 -> 16, of which waited for: 11 -> 9; matrix products, arithmetic and copies ran while one was open for 5% -> 5% of each run, Pallas kernels for 6% -> 7%
where the time goes in v4:
time: 134 us; the launch traced here: 133 us
  waiting for transfers between devices  58.2 us (43%)
  blocking collectives  25.7 us (19%)
  starting transfers between devices  22.9 us (17%)
  Pallas kernels  15.5 us (12%)
  local copies, waits for them, and re-layouts  8.2 us (6%)
  other arithmetic  2.02 us (2%)
    ppermute x12, waiting for transfers between devices, shifted(): lax.ppermute(block, axis, [(i, (i + offset) % count) for i in range(count)])  45.1 us
    all_to_all x1, blocking collectives, exchanged(): lax.all_to_all(blocks, 'shard', split_axis=0, concat_axis=0, tiled=True)  25.7 us
    ppermute x12, starting transfers between devices, shifted(): lax.ppermute(block, axis, [(i, (i + offset) % count) for i in range(count)])  16.7 us
    all_to_all x1, waiting for transfers between devices, exchanged(): lax.all_to_all(blocks, 'shard', split_axis=0, concat_axis=0, tiled=True)  8.04 us
    pallas_call x1, Pallas kernels, statistics(): pl.pallas_call(statistics_kernel, grid=(size // tile,), out_shape=jax.Sha...  5.71 us
    ppermute x3, waiting for transfers between devices, other_core(): return lax.ppermute(block, 'shard', [(i, i ^ 1) for i in range(count)])  5.14 us
    all_to_all x1, starting transfers between devices, exchanged(): lax.all_to_all(blocks, 'shard', split_axis=0, concat_axis=0, tiled=True)  3.73 us
  transfers between devices with their start and end apart: 16, of which 9 were waited for; matrix products, arithmetic and copies ran while one was open for 5% of the time, Pallas kernels for 7%

profile of v4, /device:TPU:1, one launch (start us, length us, event | category | flops | bytes accessed | tf_op | source)
XLA Modules:
  0.0 133.4 jit_solution(3182262107096053928)
XLA Ops:
  0.7 1.3 dynamic-slice_bitcast_fusion
  2.0 1.5 %collective-permute-start = (f32[1024,1024]{1,0:T(8,128)}, f32[1024,1024]{1,0:T(8,128)}, u32[]{:S(2)}, u32[]{:S(2)}) collective-permute-start(f32[1024,1024]{1,0:T(8,128)} %bitcast.19), channel_id=1, source_target_pairs={{0,1},{1,0},{2,3},{3,2},{4,5},{5,4},{6,7},{7,6},{8,9},{9,8},{10,11... | collective-permute-start | bytes 12582920 | tf_op jit(solution)/shard_map/ppermute | solution.py:23
  3.5 1.4 %collective-permute-start.1 = (bf16[8,32,1024]{2,1,0:T(8,128)(2,1)S(1)}, bf16[8,32,1024]{2,1,0:T(8,128)(2,1)S(1)}, u32[]{:S(2)}, u32[]{:S(2)}) collective-permute-start(bf16[8,32,1024]{2,1,0:T(8,128)(2,1)S(1)} %get-tuple-element.31), channel_id=1, source_target_pairs={{0,32},{32,64},{64,96},{96,0},{1,33},{33,65},{65,97},{97,1},{2,34}... | collective-permute-start | bytes 1572872 | tf_op jit(solution)/shard_map/ppermute | solution.py:18
  4.9 1.4 %collective-permute-start.2 = (bf16[8,32,1024]{2,1,0:T(8,128)(2,1)S(1)}, bf16[8,32,1024]{2,1,0:T(8,128)(2,1)S(1)}, u32[]{:S(2)}, u32[]{:S(2)}) collective-permute-start(bf16[8,32,1024]{2,1,0:T(8,128)(2,1)S(1)} %get-tuple-element.32), channel_id=1, source_target_pairs={{0,96},{32,0},{64,32},{96,64},{1,97},{33,1},{65,33},{97,65},{2,98}... | collective-permute-start | bytes 1572872 | tf_op jit(solution)/shard_map/ppermute | solution.py:18
  6.3 4.3 %collective-permute-done = f32[1024,1024]{1,0:T(8,128)} collective-permute-done((f32[1024,1024]{1,0:T(8,128)}, f32[1024,1024]{1,0:T(8,128)}, u32[]{:S(2)}, u32[]{:S(2)}) %collective-permute-start) | collective-permute-done | bytes 4194336 | tf_op jit(solution)/shard_map/ppermute | solution.py:23
  10.6 1.3 constant_dynamic-slice_fusion.1
  11.9 1.4 %collective-permute-start.5 = (bf16[8,32,1024]{2,1,0:T(8,128)(2,1)S(1)}, bf16[8,32,1024]{2,1,0:T(8,128)(2,1)S(1)}, u32[]{:S(2)}, u32[]{:S(2)}) collective-permute-start(bf16[8,32,1024]{2,1,0:T(8,128)(2,1)S(1)} %get-tuple-element.37), channel_id=1, source_target_pairs={{0,32},{32,64},{64,96},{96,0},{1,33},{33,65},{65,97},{97,1},{2,34}... | collective-permute-start | bytes 1572872 | tf_op jit(solution)/shard_map/ppermute | solution.py:18
  13.4 1.5 %collective-permute-start.6 = (bf16[8,32,1024]{2,1,0:T(8,128)(2,1)S(1)}, bf16[8,32,1024]{2,1,0:T(8,128)(2,1)S(1)}, u32[]{:S(2)}, u32[]{:S(2)}) collective-permute-start(bf16[8,32,1024]{2,1,0:T(8,128)(2,1)S(1)} %get-tuple-element.38), channel_id=1, source_target_pairs={{0,96},{32,0},{64,32},{96,64},{1,97},{33,1},{65,33},{97,65},{2,98}... | collective-permute-start | bytes 1572872 | tf_op jit(solution)/shard_map/ppermute | solution.py:18
  14.9 3.6 %collective-permute-done.1 = bf16[8,32,1024]{2,1,0:T(8,128)(2,1)S(1)} collective-permute-done((bf16[8,32,1024]{2,1,0:T(8,128)(2,1)S(1)}, bf16[8,32,1024]{2,1,0:T(8,128)(2,1)S(1)}, u32[]{:S(2)}, u32[]{:S(2)}) %collective-permute-start.1) | collective-permute-done | bytes 524320 | tf_op jit(solution)/shard_map/ppermute | solution.py:18
  18.5 1.6 %add_convert_fusion.2 = (bf16[8,32,1024]{2,1,0:T(8,128)(2,1)S(1)}, bf16[8,32,1024]{2,1,0:T(8,128)(2,1)S(1)}) fusion(bf16[8,32,1024]{2,1,0:T(8,128)(2,1)S(1)} %collective-permute-done.2, bf16[64,32,1024]{2,1,0:T(8,128)(2,1)} %bitcast.27, s32[]{:T(128)S(6)} %select_n.82, bf16[8,32,1024]{2,1,0:T(8,128)(2,1)S(1)} %collective-permute-done.1, s32[]{:T(128)S(6)} %select_n.80), kind=kLoop, calls=%fused_computation.2 | loop fusion | flops 2097152 | bytes 3145736 | tf_op jit(solution)/shard_map/convert_element_type | solution.py:34
  21.0 1.8 %collective-permute-start.4 = (bf16[8,32,1024]{2,1,0:T(8,128)(2,1)S(1)}, bf16[8,32,1024]{2,1,0:T(8,128)(2,1)S(1)}, u32[]{:S(2)}, u32[]{:S(2)}) collective-permute-start(bf16[8,32,1024]{2,1,0:T(8,128)(2,1)S(1)} %get-tuple-element.36), channel_id=1, source_target_pairs={{0,96},{32,0},{64,32},{96,64},{1,97},{33,1},{65,33},{97,65},{2,98}... | collective-permute-start | bytes 1572872 | tf_op jit(solution)/shard_map/ppermute | solution.py:18
  22.8 1.3 constant_dynamic-slice_fusion.3
  24.1 5.5 %collective-permute-done.5 = bf16[8,32,1024]{2,1,0:T(8,128)(2,1)S(1)} collective-permute-done((bf16[8,32,1024]{2,1,0:T(8,128)(2,1)S(1)}, bf16[8,32,1024]{2,1,0:T(8,128)(2,1)S(1)}, u32[]{:S(2)}, u32[]{:S(2)}) %collective-permute-start.5) | collective-permute-done | bytes 524320 | tf_op jit(solution)/shard_map/ppermute | solution.py:18
  30.1 2.7 %orient.1 = (bf16[2,512,1024]{2,1,0:T(8,128)(2,1)S(1)}, bf16[2,512,1024]{2,1,0:T(8,128)(2,1)S(1)}) custom-call(s32[1]{0:T(128)} %bitcast.6.core, f32[32,2,16,1024]{3,2,1,0:T(8,128)S(1)} %bitcast.20, f32[2,512,1024]{2,1,0:T(8,128)S(1)} %bitcast.21, f32[32,2,16,1024]{3,2,1,0:T(8,128)} %bitcast.9.partner, f32[2,512,1024]{2,1,0:T(8,128)} %bitcast.10.partner_halves), custom_call_target="tpu_custom_call" | custom-call | flops 1048576 | bytes 12582912 | tf_op jit(solution)/shard_map/orient/pallas_call | solution.py:136
  32.8 8.1 %collective-permute-done.3.sum_low = bf16[8,32,1024]{2,1,0:T(8,128)(2,1)S(1)} collective-permute-done((bf16[8,32,1024]{2,1,0:T(8,128)(2,1)S(1)}, bf16[8,32,1024]{2,1,0:T(8,128)(2,1)S(1)}, u32[]{:S(2)}, u32[]{:S(2)}) %collective-permute-start.3) | collective-permute-done | bytes 524320 | tf_op jit(solution)/shard_map/ppermute | solution.py:18
  40.9 1.6 %finish_sum.1 = bf16[16,2,32,512]{3,2,1,0:T(8,128)(2,1)S(1)} custom-call(s32[16]{0:T(128)S(1)} %fusion.order, bf16[8,32,1024]{2,1,0:T(8,128)(2,1)S(1)} %get-tuple-element.42.low, bf16[8,32,1024]{2,1,0:T(8,128)(2,1)S(1)} %get-tuple-element.43.high, bf16[8,32,1024]{2,1,0:T(8,128)(2,1)S(1)} %collective-permute-done.3.sum_low, ...), custom_call_target="tpu_custom_call" | custom-call | flops 524288 | bytes 3145728 | tf_op jit(solution)/shard_map/finish_sum/pallas_call | solution.py:81
  42.5 25.7 %all_to_all.10.columns.own = bf16[32,32,512]{2,1,0:T(8,128)(2,1)S(1)} all-to-all(bf16[32,32,512]{2,1,0:T(8,128)(2,1)S(1)} %bitcast.24), channel_id=1, replica_groups=mesh['dp'=4,'shard'=32] {'shard'}, dimensions={0} | all-to-all | bytes 2097152 | tf_op jit(solution)/shard_map/all_to_all | solution.py:27
  68.1 1.3 begin.1
  71.4 1.6 %complete.1 = bf16[512,1024]{1,0:T(8,128)(2,1)} custom-call(f32[512,1024]{1,0:T(8,128)S(1)} %share.1.part, bf16[512,512]{1,0:T(8,128)(2,1)S(1)} %collective-permute-done.7.other, bf16[2,512,1024]{2,1,0:T(8,128)(2,1)S(1)} %get-tuple-element.52.right), custom_call_target="tpu_custom_call" | custom-call | flops 536870912 | bytes 4194304 | tf_op jit(solution)/shard_map/complete/pallas_call | solution.py:215
  73.5 3.7 %all-to-all-start.1 = ((bf16[32,16,1024]{2,1,0:T(8,128)(2,1)}), bf16[32,16,1024]{2,1,0:T(8,128)(2,1)S(1)}, u32[]{:S(2)}, u32[]{:S(2)}) async-start(bf16[32,16,1024]{2,1,0:T(8,128)(2,1)} %bitcast.12), calls=%async_computation.1 | async-start | bytes 2097152 | tf_op jit(solution)/shard_map/all_to_all | solution.py:27
  77.2 1.3 constant_dynamic-slice_fusion.old
  78.6 2.2 %copy-done.2 = f32[1,1,1024,1024]{3,2,1,0:T(8,128)S(1)} copy-done((f32[1,1,1024,1024]{3,2,1,0:T(8,128)S(1)}, f32[1,1,1024,1024]{3,2,1,0:T(8,128)}, u32[]{:S(2)}) %copy-start.2) | copy-done | bytes 4194328
  80.8 5.7 %statistics.1 = f32[1024,1024]{1,0:T(8,128)} custom-call(s32[1]{0:T(128)} %bitcast.6.core, bf16[32,32,512]{2,1,0:T(8,128)(2,1)S(1)} %all_to_all.10.columns.own, bf16[32,32,512]{2,1,0:T(8,128)(2,1)} %collective-permute-done.8.other, f32[1024,1024]{1,0:T(8,128)S(1)} %bitcast.23), custom_call_target="tpu_custom_call" | custom-call | flops 2147483648 | bytes 12582912 | tf_op jit(solution)/shard_map/statistics/pallas_call | solution.py:264
  86.5 8.0 %all-to-all-done.1 = bf16[32,16,1024]{2,1,0:T(8,128)(2,1)S(1)} async-done(((bf16[32,16,1024]{2,1,0:T(8,128)(2,1)}), bf16[32,16,1024]{2,1,0:T(8,128)(2,1)S(1)}, u32[]{:S(2)}, u32[]{:S(2)}) %all-to-all-start.1) | async-done | bytes 1048608 | tf_op jit(solution)/shard_map/all_to_all | solution.py:27
  94.5 1.1 step.1
  95.6 1.4 %collective-permute-start.9 = (bf16[8,32,1024]{2,1,0:T(8,128)(2,1)S(1)}, bf16[8,32,1024]{2,1,0:T(8,128)(2,1)S(1)}, u32[]{:S(2)}, u32[]{:S(2)}) collective-permute-start(bf16[8,32,1024]{2,1,0:T(8,128)(2,1)S(1)} %get-tuple-element.57), channel_id=1, source_target_pairs={{0,32},{32,64},{64,96},{96,0},{1,33},{33,65},{65,97},{97,1},{2,34}... | collective-permute-start | bytes 1572872 | tf_op jit(solution)/shard_map/ppermute | solution.py:18
  97.0 1.4 %collective-permute-start.11 = (bf16[8,32,1024]{2,1,0:T(8,128)(2,1)S(1)}, bf16[8,32,1024]{2,1,0:T(8,128)(2,1)S(1)}, u32[]{:S(2)}, u32[]{:S(2)}) collective-permute-start(bf16[8,32,1024]{2,1,0:T(8,128)(2,1)S(1)} %get-tuple-element.58), channel_id=1, source_target_pairs={{0,96},{32,0},{64,32},{96,64},{1,97},{33,1},{65,33},{97,65},{2,98}... | collective-permute-start | bytes 1572872 | tf_op jit(solution)/shard_map/ppermute | solution.py:18
  98.4 2.6 %collective-permute-start.14 = (bf16[8,32,1024]{2,1,0:T(8,128)(2,1)S(1)}, bf16[8,32,1024]{2,1,0:T(8,128)(2,1)S(1)}, u32[]{:S(2)}, u32[]{:S(2)}) collective-permute-start(bf16[8,32,1024]{2,1,0:T(8,128)(2,1)S(1)} %get-tuple-element.57), channel_id=1, source_target_pairs={{0,96},{32,0},{64,32},{96,64},{1,97},{33,1},{65,33},{97,65},{2,98}... | collective-permute-start | bytes 1572872 | tf_op jit(solution)/shard_map/ppermute | solution.py:18
  101.0 8.9 %collective-permute-done.9 = bf16[8,32,1024]{2,1,0:T(8,128)(2,1)S(1)} collective-permute-done((bf16[8,32,1024]{2,1,0:T(8,128)(2,1)S(1)}, bf16[8,32,1024]{2,1,0:T(8,128)(2,1)S(1)}, u32[]{:S(2)}, u32[]{:S(2)}) %collective-permute-start.9) | collective-permute-done | bytes 524320 | tf_op jit(solution)/shard_map/ppermute | solution.py:18
  110.7 2.7 %collective-permute-start.12 = (bf16[8,32,1024]{2,1,0:T(8,128)(2,1)S(1)}, bf16[8,32,1024]{2,1,0:T(8,128)(2,1)S(1)}, u32[]{:S(2)}, u32[]{:S(2)}) collective-permute-start(bf16[8,32,1024]{2,1,0:T(8,128)(2,1)S(1)} %collective-permute-done.11), channel_id=1, source_target_pairs={{0,96},{32,0},{64,32},{96,64},{1,97},{33,1},{65,33},{97,65},{2,98}... | collective-permute-start | bytes 1572872 | tf_op jit(solution)/shard_map/ppermute | solution.py:18
  113.5 7.7 %collective-permute-done.13 = bf16[8,32,1024]{2,1,0:T(8,128)(2,1)S(1)} collective-permute-done((bf16[8,32,1024]{2,1,0:T(8,128)(2,1)S(1)}, bf16[8,32,1024]{2,1,0:T(8,128)(2,1)S(1)}, u32[]{:S(2)}, u32[]{:S(2)}) %collective-permute-start.13) | collective-permute-done | bytes 524320 | tf_op jit(solution)/shard_map/ppermute | solution.py:18
  121.3 11.1 %collective-permute-done.10.low_far = bf16[8,32,1024]{2,1,0:T(8,128)(2,1)S(1)} collective-permute-done((bf16[8,32,1024]{2,1,0:T(8,128)(2,1)S(1)}, bf16[8,32,1024]{2,1,0:T(8,128)(2,1)S(1)}, u32[]{:S(2)}, u32[]{:S(2)}) %collective-permute-start.10) | collective-permute-done | bytes 524320 | tf_op jit(solution)/shard_map/ppermute | solution.py:18
  (31 shorter events, 5.8 us)
Async XLA Ops:
  0.6 22.2 %copy-start = (s32[4,16]{1,0:T(4,128)S(1)}, s32[4,16]{1,0:T(4,128)}, u32[]{:S(2)}) copy-start(s32[4,16]{1,0:T(4,128)} %param.9) | copy-start | bytes 772
  2.0 8.6 %collective-permute-start = (f32[1024,1024]{1,0:T(8,128)}, f32[1024,1024]{1,0:T(8,128)}, u32[]{:S(2)}, u32[]{:S(2)}) collective-permute-start(f32[1024,1024]{1,0:T(8,128)} %bitcast.19), channel_id=1, source_target_pairs={{0,1},{1,0},{2,3},{3,2},{4,5},{5,4},{6,7},{7,6},{8,9},{9,8},{10,11... | collective-permute-start | bytes 12582920 | tf_op jit(solution)/shard_map/ppermute | solution.py:23
  3.5 15.0 %collective-permute-start.1 = (bf16[8,32,1024]{2,1,0:T(8,128)(2,1)S(1)}, bf16[8,32,1024]{2,1,0:T(8,128)(2,1)S(1)}, u32[]{:S(2)}, u32[]{:S(2)}) collective-permute-start(bf16[8,32,1024]{2,1,0:T(8,128)(2,1)S(1)} %get-tuple-element.31), channel_id=1, source_target_pairs={{0,32},{32,64},{64,96},{96,0},{1,33},{33,65},{65,97},{97,1},{2,34}... | collective-permute-start | bytes 1572872 | tf_op jit(solution)/shard_map/ppermute | solution.py:18
  4.9 13.6 %collective-permute-start.2 = (bf16[8,32,1024]{2,1,0:T(8,128)(2,1)S(1)}, bf16[8,32,1024]{2,1,0:T(8,128)(2,1)S(1)}, u32[]{:S(2)}, u32[]{:S(2)}) collective-permute-start(bf16[8,32,1024]{2,1,0:T(8,128)(2,1)S(1)} %get-tuple-element.32), channel_id=1, source_target_pairs={{0,96},{32,0},{64,32},{96,64},{1,97},{33,1},{65,33},{97,65},{2,98}... | collective-permute-start | bytes 1572872 | tf_op jit(solution)/shard_map/ppermute | solution.py:18
  11.9 18.2 %copy-start.1 = (f32[1,1,1024,1024]{3,2,1,0:T(8,128)S(1)}, f32[1,1,1024,1024]{3,2,1,0:T(8,128)}, u32[]{:S(2)}) copy-start(f32[1,1,1024,1024]{3,2,1,0:T(8,128)} %param.8) | copy-start | bytes 12582916
  11.9 17.8 %collective-permute-start.5 = (bf16[8,32,1024]{2,1,0:T(8,128)(2,1)S(1)}, bf16[8,32,1024]{2,1,0:T(8,128)(2,1)S(1)}, u32[]{:S(2)}, u32[]{:S(2)}) collective-permute-start(bf16[8,32,1024]{2,1,0:T(8,128)(2,1)S(1)} %get-tuple-element.37), channel_id=1, source_target_pairs={{0,32},{32,64},{64,96},{96,0},{1,33},{33,65},{65,97},{97,1},{2,34}... | collective-permute-start | bytes 1572872 | tf_op jit(solution)/shard_map/ppermute | solution.py:18
  13.4 16.3 %collective-permute-start.6 = (bf16[8,32,1024]{2,1,0:T(8,128)(2,1)S(1)}, bf16[8,32,1024]{2,1,0:T(8,128)(2,1)S(1)}, u32[]{:S(2)}, u32[]{:S(2)}) collective-permute-start(bf16[8,32,1024]{2,1,0:T(8,128)(2,1)S(1)} %get-tuple-element.38), channel_id=1, source_target_pairs={{0,96},{32,0},{64,32},{96,64},{1,97},{33,1},{65,33},{97,65},{2,98}... | collective-permute-start | bytes 1572872 | tf_op jit(solution)/shard_map/ppermute | solution.py:18
  20.1 20.9 %collective-permute-start.3 = (bf16[8,32,1024]{2,1,0:T(8,128)(2,1)S(1)}, bf16[8,32,1024]{2,1,0:T(8,128)(2,1)S(1)}, u32[]{:S(2)}, u32[]{:S(2)}) collective-permute-start(bf16[8,32,1024]{2,1,0:T(8,128)(2,1)S(1)} %get-tuple-element.35), channel_id=1, source_target_pairs={{0,32},{32,64},{64,96},{96,0},{1,33},{33,65},{65,97},{97,1},{2,34}... | collective-permute-start | bytes 1572872 | tf_op jit(solution)/shard_map/ppermute | solution.py:18
  21.0 19.9 %collective-permute-start.4 = (bf16[8,32,1024]{2,1,0:T(8,128)(2,1)S(1)}, bf16[8,32,1024]{2,1,0:T(8,128)(2,1)S(1)}, u32[]{:S(2)}, u32[]{:S(2)}) collective-permute-start(bf16[8,32,1024]{2,1,0:T(8,128)(2,1)S(1)} %get-tuple-element.36), channel_id=1, source_target_pairs={{0,96},{32,0},{64,32},{96,64},{1,97},{33,1},{65,33},{97,65},{2,98}... | collective-permute-start | bytes 1572872 | tf_op jit(solution)/shard_map/ppermute | solution.py:18
  69.4 2.0 %collective-permute-start.7 = (bf16[512,512]{1,0:T(8,128)(2,1)S(1)}, bf16[512,512]{1,0:T(8,128)(2,1)S(1)}, u32[]{:S(2)}, u32[]{:S(2)}) collective-permute-start(bf16[512,512]{1,0:T(8,128)(2,1)S(1)} %get-tuple-element.53), channel_id=1, source_target_pairs={{0,1},{1,0},{2,3},{3,2},{4,5},{5,4},{6,7},{7,6},{8,9},{9,8},{10,11... | collective-permute-start | bytes 1572872 | tf_op jit(solution)/shard_map/ppermute | solution.py:23
  73.0 5.5 %collective-permute-start.8 = (bf16[32,32,512]{2,1,0:T(8,128)(2,1)S(1)}, bf16[32,32,512]{2,1,0:T(8,128)(2,1)}, u32[]{:S(2)}, u32[]{:S(2)}) collective-permute-start(bf16[32,32,512]{2,1,0:T(8,128)(2,1)S(1)} %all_to_all.10.columns.own), channel_id=1, source_target_pairs={{0,1},{1,0},{2,3},{3,2},{4,5},{5,4},{6,7},{7,6},{8,9},{9,8},{10,11... | collective-permute-start | bytes 3145736 | tf_op jit(solution)/shard_map/ppermute | solution.py:23
  73.5 21.0 %all-to-all-start.1 = ((bf16[32,16,1024]{2,1,0:T(8,128)(2,1)}), bf16[32,16,1024]{2,1,0:T(8,128)(2,1)S(1)}, u32[]{:S(2)}, u32[]{:S(2)}) async-start(bf16[32,16,1024]{2,1,0:T(8,128)(2,1)} %bitcast.12), calls=%async_computation.1 | async-start | bytes 2097152 | tf_op jit(solution)/shard_map/all_to_all | solution.py:27
  78.6 2.2 %copy-start.2 = (f32[1,1,1024,1024]{3,2,1,0:T(8,128)S(1)}, f32[1,1,1024,1024]{3,2,1,0:T(8,128)}, u32[]{:S(2)}) copy-start(f32[1,1,1024,1024]{3,2,1,0:T(8,128)} %param.7) | copy-start | bytes 12582916
  95.6 14.4 %collective-permute-start.9 = (bf16[8,32,1024]{2,1,0:T(8,128)(2,1)S(1)}, bf16[8,32,1024]{2,1,0:T(8,128)(2,1)S(1)}, u32[]{:S(2)}, u32[]{:S(2)}) collective-permute-start(bf16[8,32,1024]{2,1,0:T(8,128)(2,1)S(1)} %get-tuple-element.57), channel_id=1, source_target_pairs={{0,32},{32,64},{64,96},{96,0},{1,33},{33,65},{65,97},{97,1},{2,34}... | collective-permute-start | bytes 1572872 | tf_op jit(solution)/shard_map/ppermute | solution.py:18
  97.0 13.7 %collective-permute-start.11 = (bf16[8,32,1024]{2,1,0:T(8,128)(2,1)S(1)}, bf16[8,32,1024]{2,1,0:T(8,128)(2,1)S(1)}, u32[]{:S(2)}, u32[]{:S(2)}) collective-permute-start(bf16[8,32,1024]{2,1,0:T(8,128)(2,1)S(1)} %get-tuple-element.58), channel_id=1, source_target_pairs={{0,96},{32,0},{64,32},{96,64},{1,97},{33,1},{65,33},{97,65},{2,98}... | collective-permute-start | bytes 1572872 | tf_op jit(solution)/shard_map/ppermute | solution.py:18
  98.4 22.8 %collective-permute-start.13 = (bf16[8,32,1024]{2,1,0:T(8,128)(2,1)S(1)}, bf16[8,32,1024]{2,1,0:T(8,128)(2,1)S(1)}, u32[]{:S(2)}, u32[]{:S(2)}) collective-permute-start(bf16[8,32,1024]{2,1,0:T(8,128)(2,1)S(1)} %get-tuple-element.58), channel_id=1, source_target_pairs={{0,32},{32,64},{64,96},{96,0},{1,33},{33,65},{65,97},{97,1},{2,34}... | collective-permute-start | bytes 1572872 | tf_op jit(solution)/shard_map/ppermute | solution.py:18
  98.4 22.8 %collective-permute-start.14 = (bf16[8,32,1024]{2,1,0:T(8,128)(2,1)S(1)}, bf16[8,32,1024]{2,1,0:T(8,128)(2,1)S(1)}, u32[]{:S(2)}, u32[]{:S(2)}) collective-permute-start(bf16[8,32,1024]{2,1,0:T(8,128)(2,1)S(1)} %get-tuple-element.57), channel_id=1, source_target_pairs={{0,96},{32,0},{64,32},{96,64},{1,97},{33,1},{65,33},{97,65},{2,98}... | collective-permute-start | bytes 1572872 | tf_op jit(solution)/shard_map/ppermute | solution.py:18
  110.0 22.5 %collective-permute-start.10 = (bf16[8,32,1024]{2,1,0:T(8,128)(2,1)S(1)}, bf16[8,32,1024]{2,1,0:T(8,128)(2,1)S(1)}, u32[]{:S(2)}, u32[]{:S(2)}) collective-permute-start(bf16[8,32,1024]{2,1,0:T(8,128)(2,1)S(1)} %collective-permute-done.9), channel_id=1, source_target_pairs={{0,32},{32,64},{64,96},{96,0},{1,33},{33,65},{65,97},{97,1},{2,34}... | collective-permute-start | bytes 1572872 | tf_op jit(solution)/shard_map/ppermute | solution.py:18
  110.7 21.8 %collective-permute-start.12 = (bf16[8,32,1024]{2,1,0:T(8,128)(2,1)S(1)}, bf16[8,32,1024]{2,1,0:T(8,128)(2,1)S(1)}, u32[]{:S(2)}, u32[]{:S(2)}) collective-permute-start(bf16[8,32,1024]{2,1,0:T(8,128)(2,1)S(1)} %collective-permute-done.11), channel_id=1, source_target_pairs={{0,96},{32,0},{64,32},{96,64},{1,97},{33,1},{65,33},{97,65},{2,98}... | collective-permute-start | bytes 1572872 | tf_op jit(solution)/shard_map/ppermute | solution.py:18
  121.3 11.1 %copy-start.3 = (bf16[64,32,1024]{2,1,0:T(8,128)(2,1)}, bf16[64,32,1024]{2,1,0:T(8,128)(2,1)S(1)}, u32[]{:S(2)}) copy-start(bf16[64,32,1024]{2,1,0:T(8,128)(2,1)S(1)} %constant_dynamic-update-slice_fusion.below) | copy-start | bytes 12582916

commit v5 on v4

--- a/solution.py
+++ b/solution.py
@@ -71,8 +71,8 @@
             sent(place, side).wait()
         return carry
 
-    lax.fori_loop(0, made.shape[0], step, 0)
-    lax.fori_loop(0, made.shape[0], finish, 0)
+    lax.fori_loop(0, made.shape[0], step, 0, unroll=4)
+    lax.fori_loop(0, made.shape[0], finish, 0, unroll=4)
 
 
 def finish_sum(order, *terms):
@@ -149,49 +149,55 @@
     )(core, *root, *partner)
 
 
-def begin_kernel(left, columns, kept, swapped):
-    size, half = left.shape[2], left.shape[1]
+def begin_kernel(left, columns, swapped):
+    half, size = left.shape[1:]
     rows = columns[...].reshape(size, half)
     tile = half // 2
-    for side, out in ((1, swapped), (0, kept)):
-        for low in range(0, half, tile):
-            out[low : low + tile, :] = jnp.dot(
-                left[side, low : low + tile, :], rows, preferred_element_type=f32
-            ).astype(bf16)
+    for low in range(0, half, tile):
+        swapped[low : low + tile, :] = jnp.dot(
+            left[1, low : low + tile, :], rows, preferred_element_type=f32
+        ).astype(bf16)
 
 
 def begun(left, columns):
     half = left.shape[1]
     return pl.pallas_call(
         begin_kernel,
-        out_shape=[jax.ShapeDtypeStruct((half, half), bf16)] * 2,
+        out_shape=jax.ShapeDtypeStruct((half, half), bf16),
         in_specs=[whole_in(pltpu.VMEM)] * 2,
-        out_specs=[whole_in(pltpu.VMEM)] * 2,
-        compiler_params=pltpu.CompilerParams(vmem_limit_bytes=16 << 20),
-        cost_estimate=pl.CostEstimate(flops=8 * half**3, bytes_accessed=16 * half**2, transcendentals=0),
+        out_specs=whole_in(pltpu.VMEM),
+        compiler_params=pltpu.CompilerParams(vmem_limit_bytes=16 << 20),
+        cost_estimate=pl.CostEstimate(flops=4 * half**3, bytes_accessed=8 * half**2, transcendentals=0),
         name="begin",
     )(left, columns)
 
 
-def share_kernel(kept, right, part):
-    size = part.shape[1]
-    width = size // 4
-    for low in range(0, size, width):
-        columns = slice(low, low + width)
-        part[:, columns] = jnp.dot(kept[...], right[0, :, columns], preferred_element_type=f32)
-
-
-def shared(kept, right):
+def share_kernel(left, columns, right, part, kept):
+    half, size = left.shape[1:]
+    rows = columns[...].reshape(size, half)
+    tile = half // 2
+    for low in range(0, half, tile):
+        kept[low : low + tile, :] = jnp.dot(
+            left[0, low : low + tile, :], rows, preferred_element_type=f32
+        ).astype(bf16)
+    for low in range(0, size, tile):
+        part[:, low : low + tile] = jnp.dot(
+            kept[...], right[0, :, low : low + tile], preferred_element_type=f32
+        )
+
+
+def shared(left, columns, right):
     half, size = right.shape[1:]
     return pl.pallas_call(
         share_kernel,
         out_shape=jax.ShapeDtypeStruct((half, size), f32),
-        in_specs=[whole_in(pltpu.VMEM)] * 2,
+        in_specs=[whole_in(pltpu.VMEM)] * 3,
         out_specs=whole_in(pltpu.VMEM),
-        compiler_params=pltpu.CompilerParams(vmem_limit_bytes=16 << 20),
-        cost_estimate=pl.CostEstimate(flops=4 * half**3, bytes_accessed=16 * half**2, transcendentals=0),
+        scratch_shapes=[pltpu.VMEM((half, half), bf16)],
+        compiler_params=pltpu.CompilerParams(vmem_limit_bytes=16 << 20),
+        cost_estimate=pl.CostEstimate(flops=8 * half**3, bytes_accessed=20 * half**2, transcendentals=0),
         name="share",
-    )(kept, right)
+    )(left, columns, right)
 
 
 def complete_kernel(part, other, right, update, made, sems):
@@ -291,7 +297,7 @@
 
         return carry
 
-    lax.fori_loop(0, old.shape[0], step, 0)
+    lax.fori_loop(0, old.shape[0], step, 0, unroll=4)
 
 
 def stepped(order, old, update):
@@ -379,9 +385,8 @@
     whole = finish_sum(own_order, *partial, sum_up, sum_down)
 
     own_columns = exchanged(whole.reshape(shards, rows, size // 2))
-    kept, swapped = begun(left, own_columns)
-    swapped = other_core(swapped)
-    part = shared(kept, right)
+    swapped = other_core(begun(left, own_columns))
+    part = shared(left, own_columns, right)
     update = completed(part, swapped, right)
 
     own_columns = in_order((own_columns,), (update,))[0]

time: 134 us -> 133 us (level)
  no operation moved by 1% of the time
where the time goes in v5:
time: 133 us
  waiting for transfers between devices  57.7 us (43%)
  blocking collectives  25.7 us (19%)
  starting transfers between devices  22.9 us (17%)
  Pallas kernels  15.3 us (12%)
  local copies, waits for them, and re-layouts  8.22 us (6%)
  other arithmetic  2 us (2%)
    ppermute x12, waiting for transfers between devices, shifted(): lax.ppermute(block, axis, [(i, (i + offset) % count) for i in range(count)])  45.1 us
    all_to_all x1, blocking collectives, exchanged(): lax.all_to_all(blocks, 'shard', split_axis=0, concat_axis=0, tiled=True)  25.7 us
    ppermute x12, starting transfers between devices, shifted(): lax.ppermute(block, axis, [(i, (i + offset) % count) for i in range(count)])  16.7 us
    all_to_all x1, waiting for transfers between devices, exchanged(): lax.all_to_all(blocks, 'shard', split_axis=0, concat_axis=0, tiled=True)  8.04 us
    pallas_call x1, Pallas kernels, statistics(): pl.pallas_call(statistics_kernel, grid=(size // tile,), out_shape=jax.Sha...  5.71 us
    ppermute x3, waiting for transfers between devices, other_core(): return lax.ppermute(block, 'shard', [(i, i ^ 1) for i in range(count)])  4.59 us
    all_to_all x1, starting transfers between devices, exchanged(): lax.all_to_all(blocks, 'shard', split_axis=0, concat_axis=0, tiled=True)  3.73 us
  transfers between devices with their start and end apart: 16, of which 9 were waited for; matrix products, arithmetic and copies ran while one was open for 5% of the time, Pallas kernels for 7%

profile of v5, /device:TPU:1, one launch (start us, length us, event | category | flops | bytes accessed | tf_op | source)
XLA Modules:
  0.0 132.7 jit_solution(1998095612628022657)
XLA Ops:
  0.7 1.3 dynamic-slice_bitcast_fusion
  2.0 1.5 %collective-permute-start = (f32[1024,1024]{1,0:T(8,128)}, f32[1024,1024]{1,0:T(8,128)}, u32[]{:S(2)}, u32[]{:S(2)}) collective-permute-start(f32[1024,1024]{1,0:T(8,128)} %bitcast.19), channel_id=1, source_target_pairs={{0,1},{1,0},{2,3},{3,2},{4,5},{5,4},{6,7},{7,6},{8,9},{9,8},{10,11... | collective-permute-start | bytes 12582920 | tf_op jit(solution)/shard_map/ppermute | solution.py:23
  3.5 1.4 %collective-permute-start.1 = (bf16[8,32,1024]{2,1,0:T(8,128)(2,1)S(1)}, bf16[8,32,1024]{2,1,0:T(8,128)(2,1)S(1)}, u32[]{:S(2)}, u32[]{:S(2)}) collective-permute-start(bf16[8,32,1024]{2,1,0:T(8,128)(2,1)S(1)} %get-tuple-element.29), channel_id=1, source_target_pairs={{0,32},{32,64},{64,96},{96,0},{1,33},{33,65},{65,97},{97,1},{2,34}... | collective-permute-start | bytes 1572872 | tf_op jit(solution)/shard_map/ppermute | solution.py:18
  4.9 1.4 %collective-permute-start.2 = (bf16[8,32,1024]{2,1,0:T(8,128)(2,1)S(1)}, bf16[8,32,1024]{2,1,0:T(8,128)(2,1)S(1)}, u32[]{:S(2)}, u32[]{:S(2)}) collective-permute-start(bf16[8,32,1024]{2,1,0:T(8,128)(2,1)S(1)} %get-tuple-element.30), channel_id=1, source_target_pairs={{0,96},{32,0},{64,32},{96,64},{1,97},{33,1},{65,33},{97,65},{2,98}... | collective-permute-start | bytes 1572872 | tf_op jit(solution)/shard_map/ppermute | solution.py:18
  6.3 4.3 %collective-permute-done = f32[1024,1024]{1,0:T(8,128)} collective-permute-done((f32[1024,1024]{1,0:T(8,128)}, f32[1024,1024]{1,0:T(8,128)}, u32[]{:S(2)}, u32[]{:S(2)}) %collective-permute-start) | collective-permute-done | bytes 4194336 | tf_op jit(solution)/shard_map/ppermute | solution.py:23
  10.6 1.3 constant_dynamic-slice_fusion.1
  11.9 1.4 %collective-permute-start.5 = (bf16[8,32,1024]{2,1,0:T(8,128)(2,1)S(1)}, bf16[8,32,1024]{2,1,0:T(8,128)(2,1)S(1)}, u32[]{:S(2)}, u32[]{:S(2)}) collective-permute-start(bf16[8,32,1024]{2,1,0:T(8,128)(2,1)S(1)} %get-tuple-element.35), channel_id=1, source_target_pairs={{0,32},{32,64},{64,96},{96,0},{1,33},{33,65},{65,97},{97,1},{2,34}... | collective-permute-start | bytes 1572872 | tf_op jit(solution)/shard_map/ppermute | solution.py:18
  13.4 1.5 %collective-permute-start.6 = (bf16[8,32,1024]{2,1,0:T(8,128)(2,1)S(1)}, bf16[8,32,1024]{2,1,0:T(8,128)(2,1)S(1)}, u32[]{:S(2)}, u32[]{:S(2)}) collective-permute-start(bf16[8,32,1024]{2,1,0:T(8,128)(2,1)S(1)} %get-tuple-element.36), channel_id=1, source_target_pairs={{0,96},{32,0},{64,32},{96,64},{1,97},{33,1},{65,33},{97,65},{2,98}... | collective-permute-start | bytes 1572872 | tf_op jit(solution)/shard_map/ppermute | solution.py:18
  14.9 3.6 %collective-permute-done.1 = bf16[8,32,1024]{2,1,0:T(8,128)(2,1)S(1)} collective-permute-done((bf16[8,32,1024]{2,1,0:T(8,128)(2,1)S(1)}, bf16[8,32,1024]{2,1,0:T(8,128)(2,1)S(1)}, u32[]{:S(2)}, u32[]{:S(2)}) %collective-permute-start.1) | collective-permute-done | bytes 524320 | tf_op jit(solution)/shard_map/ppermute | solution.py:18
  18.5 1.6 %add_convert_fusion.2 = (bf16[8,32,1024]{2,1,0:T(8,128)(2,1)S(1)}, bf16[8,32,1024]{2,1,0:T(8,128)(2,1)S(1)}) fusion(bf16[8,32,1024]{2,1,0:T(8,128)(2,1)S(1)} %collective-permute-done.2, bf16[64,32,1024]{2,1,0:T(8,128)(2,1)} %bitcast.27, s32[]{:T(128)S(6)} %select_n.82, bf16[8,32,1024]{2,1,0:T(8,128)(2,1)S(1)} %collective-permute-done.1, s32[]{:T(128)S(6)} %select_n.80), kind=kLoop, calls=%fused_computation.2 | loop fusion | flops 2097152 | bytes 3145736 | tf_op jit(solution)/shard_map/convert_element_type | solution.py:34
  21.0 1.8 %collective-permute-start.4 = (bf16[8,32,1024]{2,1,0:T(8,128)(2,1)S(1)}, bf16[8,32,1024]{2,1,0:T(8,128)(2,1)S(1)}, u32[]{:S(2)}, u32[]{:S(2)}) collective-permute-start(bf16[8,32,1024]{2,1,0:T(8,128)(2,1)S(1)} %get-tuple-element.34), channel_id=1, source_target_pairs={{0,96},{32,0},{64,32},{96,64},{1,97},{33,1},{65,33},{97,65},{2,98}... | collective-permute-start | bytes 1572872 | tf_op jit(solution)/shard_map/ppermute | solution.py:18
  22.8 1.3 constant_dynamic-slice_fusion.3
  24.1 5.5 %collective-permute-done.5 = bf16[8,32,1024]{2,1,0:T(8,128)(2,1)S(1)} collective-permute-done((bf16[8,32,1024]{2,1,0:T(8,128)(2,1)S(1)}, bf16[8,32,1024]{2,1,0:T(8,128)(2,1)S(1)}, u32[]{:S(2)}, u32[]{:S(2)}) %collective-permute-start.5) | collective-permute-done | bytes 524320 | tf_op jit(solution)/shard_map/ppermute | solution.py:18
  30.1 2.7 %orient.1 = (bf16[2,512,1024]{2,1,0:T(8,128)(2,1)S(1)}, bf16[2,512,1024]{2,1,0:T(8,128)(2,1)S(1)}) custom-call(s32[1]{0:T(128)} %bitcast.6.core, f32[32,2,16,1024]{3,2,1,0:T(8,128)S(1)} %bitcast.20, f32[2,512,1024]{2,1,0:T(8,128)S(1)} %bitcast.21, f32[32,2,16,1024]{3,2,1,0:T(8,128)} %bitcast.9.partner, f32[2,512,1024]{2,1,0:T(8,128)} %bitcast.10.partner_halves), custom_call_target="tpu_custom_call" | custom-call | flops 1048576 | bytes 12582912 | tf_op jit(solution)/shard_map/orient/pallas_call | solution.py:136
  32.8 8.2 %collective-permute-done.3.sum_low = bf16[8,32,1024]{2,1,0:T(8,128)(2,1)S(1)} collective-permute-done((bf16[8,32,1024]{2,1,0:T(8,128)(2,1)S(1)}, bf16[8,32,1024]{2,1,0:T(8,128)(2,1)S(1)}, u32[]{:S(2)}, u32[]{:S(2)}) %collective-permute-start.3) | collective-permute-done | bytes 524320 | tf_op jit(solution)/shard_map/ppermute | solution.py:18
  40.9 1.4 %finish_sum.1 = bf16[16,2,32,512]{3,2,1,0:T(8,128)(2,1)S(1)} custom-call(s32[16]{0:T(128)S(1)} %fusion.order, bf16[8,32,1024]{2,1,0:T(8,128)(2,1)S(1)} %get-tuple-element.40.low, bf16[8,32,1024]{2,1,0:T(8,128)(2,1)S(1)} %get-tuple-element.41.high, bf16[8,32,1024]{2,1,0:T(8,128)(2,1)S(1)} %collective-permute-done.3.sum_low, ...), custom_call_target="tpu_custom_call" | custom-call | flops 524288 | bytes 3145728 | tf_op jit(solution)/shard_map/finish_sum/pallas_call | solution.py:81
  42.4 25.7 %all_to_all.10.columns.own = bf16[32,32,512]{2,1,0:T(8,128)(2,1)S(1)} all-to-all(bf16[32,32,512]{2,1,0:T(8,128)(2,1)S(1)} %bitcast.24), channel_id=1, replica_groups=mesh['dp'=4,'shard'=32] {'shard'}, dimensions={0} | all-to-all | bytes 2097152 | tf_op jit(solution)/shard_map/all_to_all | solution.py:27
  69.2 1.3 share.1.part
  70.7 1.6 %complete.1 = bf16[512,1024]{1,0:T(8,128)(2,1)} custom-call(f32[512,1024]{1,0:T(8,128)S(1)} %share.1.part, bf16[512,512]{1,0:T(8,128)(2,1)S(1)} %collective-permute-done.7.other, bf16[2,512,1024]{2,1,0:T(8,128)(2,1)S(1)} %get-tuple-element.49.right), custom_call_target="tpu_custom_call" | custom-call | flops 536870912 | bytes 4194304 | tf_op jit(solution)/shard_map/complete/pallas_call | solution.py:221
  72.8 3.7 %all-to-all-start.1 = ((bf16[32,16,1024]{2,1,0:T(8,128)(2,1)}), bf16[32,16,1024]{2,1,0:T(8,128)(2,1)S(1)}, u32[]{:S(2)}, u32[]{:S(2)}) async-start(bf16[32,16,1024]{2,1,0:T(8,128)(2,1)} %bitcast.12), calls=%async_computation.1 | async-start | bytes 2097152 | tf_op jit(solution)/shard_map/all_to_all | solution.py:27
  76.5 1.3 constant_dynamic-slice_fusion.old
  77.9 2.2 %copy-done.2 = f32[1,1,1024,1024]{3,2,1,0:T(8,128)S(1)} copy-done((f32[1,1,1024,1024]{3,2,1,0:T(8,128)S(1)}, f32[1,1,1024,1024]{3,2,1,0:T(8,128)}, u32[]{:S(2)}) %copy-start.2) | copy-done | bytes 4194328
  80.1 5.7 %statistics.1 = f32[1024,1024]{1,0:T(8,128)} custom-call(s32[1]{0:T(128)} %bitcast.6.core, bf16[32,32,512]{2,1,0:T(8,128)(2,1)S(1)} %all_to_all.10.columns.own, bf16[32,32,512]{2,1,0:T(8,128)(2,1)} %collective-permute-done.8.other, f32[1024,1024]{1,0:T(8,128)S(1)} %bitcast.23), custom_call_target="tpu_custom_call" | custom-call | flops 2147483648 | bytes 12582912 | tf_op jit(solution)/shard_map/statistics/pallas_call | solution.py:270
  85.8 8.0 %all-to-all-done.1 = bf16[32,16,1024]{2,1,0:T(8,128)(2,1)S(1)} async-done(((bf16[32,16,1024]{2,1,0:T(8,128)(2,1)}), bf16[32,16,1024]{2,1,0:T(8,128)(2,1)S(1)}, u32[]{:S(2)}, u32[]{:S(2)}) %all-to-all-start.1) | async-done | bytes 1048608 | tf_op jit(solution)/shard_map/all_to_all | solution.py:27
  93.8 1.0 step.1
  94.8 1.4 %collective-permute-start.9 = (bf16[8,32,1024]{2,1,0:T(8,128)(2,1)S(1)}, bf16[8,32,1024]{2,1,0:T(8,128)(2,1)S(1)}, u32[]{:S(2)}, u32[]{:S(2)}) collective-permute-start(bf16[8,32,1024]{2,1,0:T(8,128)(2,1)S(1)} %get-tuple-element.53), channel_id=1, source_target_pairs={{0,32},{32,64},{64,96},{96,0},{1,33},{33,65},{65,97},{97,1},{2,34}... | collective-permute-start | bytes 1572872 | tf_op jit(solution)/shard_map/ppermute | solution.py:18
  96.2 1.4 %collective-permute-start.11 = (bf16[8,32,1024]{2,1,0:T(8,128)(2,1)S(1)}, bf16[8,32,1024]{2,1,0:T(8,128)(2,1)S(1)}, u32[]{:S(2)}, u32[]{:S(2)}) collective-permute-start(bf16[8,32,1024]{2,1,0:T(8,128)(2,1)S(1)} %get-tuple-element.54), channel_id=1, source_target_pairs={{0,96},{32,0},{64,32},{96,64},{1,97},{33,1},{65,33},{97,65},{2,98}... | collective-permute-start | bytes 1572872 | tf_op jit(solution)/shard_map/ppermute | solution.py:18
  97.6 2.6 %collective-permute-start.14 = (bf16[8,32,1024]{2,1,0:T(8,128)(2,1)S(1)}, bf16[8,32,1024]{2,1,0:T(8,128)(2,1)S(1)}, u32[]{:S(2)}, u32[]{:S(2)}) collective-permute-start(bf16[8,32,1024]{2,1,0:T(8,128)(2,1)S(1)} %get-tuple-element.53), channel_id=1, source_target_pairs={{0,96},{32,0},{64,32},{96,64},{1,97},{33,1},{65,33},{97,65},{2,98}... | collective-permute-start | bytes 1572872 | tf_op jit(solution)/shard_map/ppermute | solution.py:18
  100.3 8.9 %collective-permute-done.9 = bf16[8,32,1024]{2,1,0:T(8,128)(2,1)S(1)} collective-permute-done((bf16[8,32,1024]{2,1,0:T(8,128)(2,1)S(1)}, bf16[8,32,1024]{2,1,0:T(8,128)(2,1)S(1)}, u32[]{:S(2)}, u32[]{:S(2)}) %collective-permute-start.9) | collective-permute-done | bytes 524320 | tf_op jit(solution)/shard_map/ppermute | solution.py:18
  109.9 2.7 %collective-permute-start.12 = (bf16[8,32,1024]{2,1,0:T(8,128)(2,1)S(1)}, bf16[8,32,1024]{2,1,0:T(8,128)(2,1)S(1)}, u32[]{:S(2)}, u32[]{:S(2)}) collective-permute-start(bf16[8,32,1024]{2,1,0:T(8,128)(2,1)S(1)} %collective-permute-done.11), channel_id=1, source_target_pairs={{0,96},{32,0},{64,32},{96,64},{1,97},{33,1},{65,33},{97,65},{2,98}... | collective-permute-start | bytes 1572872 | tf_op jit(solution)/shard_map/ppermute | solution.py:18
  112.7 7.7 %collective-permute-done.13 = bf16[8,32,1024]{2,1,0:T(8,128)(2,1)S(1)} collective-permute-done((bf16[8,32,1024]{2,1,0:T(8,128)(2,1)S(1)}, bf16[8,32,1024]{2,1,0:T(8,128)(2,1)S(1)}, u32[]{:S(2)}, u32[]{:S(2)}) %collective-permute-start.13) | collective-permute-done | bytes 524320 | tf_op jit(solution)/shard_map/ppermute | solution.py:18
  120.6 11.1 %collective-permute-done.10.low_far = bf16[8,32,1024]{2,1,0:T(8,128)(2,1)S(1)} collective-permute-done((bf16[8,32,1024]{2,1,0:T(8,128)(2,1)S(1)}, bf16[8,32,1024]{2,1,0:T(8,128)(2,1)S(1)}, u32[]{:S(2)}, u32[]{:S(2)}) %collective-permute-start.10) | collective-permute-done | bytes 524320 | tf_op jit(solution)/shard_map/ppermute | solution.py:18
  (31 shorter events, 5.2 us)
Async XLA Ops:
  0.6 22.2 %copy-start = (s32[4,16]{1,0:T(4,128)S(1)}, s32[4,16]{1,0:T(4,128)}, u32[]{:S(2)}) copy-start(s32[4,16]{1,0:T(4,128)} %param.9) | copy-start | bytes 772
  2.0 8.6 %collective-permute-start = (f32[1024,1024]{1,0:T(8,128)}, f32[1024,1024]{1,0:T(8,128)}, u32[]{:S(2)}, u32[]{:S(2)}) collective-permute-start(f32[1024,1024]{1,0:T(8,128)} %bitcast.19), channel_id=1, source_target_pairs={{0,1},{1,0},{2,3},{3,2},{4,5},{5,4},{6,7},{7,6},{8,9},{9,8},{10,11... | collective-permute-start | bytes 12582920 | tf_op jit(solution)/shard_map/ppermute | solution.py:23
  3.5 15.0 %collective-permute-start.1 = (bf16[8,32,1024]{2,1,0:T(8,128)(2,1)S(1)}, bf16[8,32,1024]{2,1,0:T(8,128)(2,1)S(1)}, u32[]{:S(2)}, u32[]{:S(2)}) collective-permute-start(bf16[8,32,1024]{2,1,0:T(8,128)(2,1)S(1)} %get-tuple-element.29), channel_id=1, source_target_pairs={{0,32},{32,64},{64,96},{96,0},{1,33},{33,65},{65,97},{97,1},{2,34}... | collective-permute-start | bytes 1572872 | tf_op jit(solution)/shard_map/ppermute | solution.py:18
  4.9 13.6 %collective-permute-start.2 = (bf16[8,32,1024]{2,1,0:T(8,128)(2,1)S(1)}, bf16[8,32,1024]{2,1,0:T(8,128)(2,1)S(1)}, u32[]{:S(2)}, u32[]{:S(2)}) collective-permute-start(bf16[8,32,1024]{2,1,0:T(8,128)(2,1)S(1)} %get-tuple-element.30), channel_id=1, source_target_pairs={{0,96},{32,0},{64,32},{96,64},{1,97},{33,1},{65,33},{97,65},{2,98}... | collective-permute-start | bytes 1572872 | tf_op jit(solution)/shard_map/ppermute | solution.py:18
  11.9 18.2 %copy-start.1 = (f32[1,1,1024,1024]{3,2,1,0:T(8,128)S(1)}, f32[1,1,1024,1024]{3,2,1,0:T(8,128)}, u32[]{:S(2)}) copy-start(f32[1,1,1024,1024]{3,2,1,0:T(8,128)} %param.8) | copy-start | bytes 12582916
  11.9 17.8 %collective-permute-start.5 = (bf16[8,32,1024]{2,1,0:T(8,128)(2,1)S(1)}, bf16[8,32,1024]{2,1,0:T(8,128)(2,1)S(1)}, u32[]{:S(2)}, u32[]{:S(2)}) collective-permute-start(bf16[8,32,1024]{2,1,0:T(8,128)(2,1)S(1)} %get-tuple-element.35), channel_id=1, source_target_pairs={{0,32},{32,64},{64,96},{96,0},{1,33},{33,65},{65,97},{97,1},{2,34}... | collective-permute-start | bytes 1572872 | tf_op jit(solution)/shard_map/ppermute | solution.py:18
  13.4 16.3 %collective-permute-start.6 = (bf16[8,32,1024]{2,1,0:T(8,128)(2,1)S(1)}, bf16[8,32,1024]{2,1,0:T(8,128)(2,1)S(1)}, u32[]{:S(2)}, u32[]{:S(2)}) collective-permute-start(bf16[8,32,1024]{2,1,0:T(8,128)(2,1)S(1)} %get-tuple-element.36), channel_id=1, source_target_pairs={{0,96},{32,0},{64,32},{96,64},{1,97},{33,1},{65,33},{97,65},{2,98}... | collective-permute-start | bytes 1572872 | tf_op jit(solution)/shard_map/ppermute | solution.py:18
  20.1 20.9 %collective-permute-start.3 = (bf16[8,32,1024]{2,1,0:T(8,128)(2,1)S(1)}, bf16[8,32,1024]{2,1,0:T(8,128)(2,1)S(1)}, u32[]{:S(2)}, u32[]{:S(2)}) collective-permute-start(bf16[8,32,1024]{2,1,0:T(8,128)(2,1)S(1)} %get-tuple-element.33), channel_id=1, source_target_pairs={{0,32},{32,64},{64,96},{96,0},{1,33},{33,65},{65,97},{97,1},{2,34}... | collective-permute-start | bytes 1572872 | tf_op jit(solution)/shard_map/ppermute | solution.py:18
  21.0 19.9 %collective-permute-start.4 = (bf16[8,32,1024]{2,1,0:T(8,128)(2,1)S(1)}, bf16[8,32,1024]{2,1,0:T(8,128)(2,1)S(1)}, u32[]{:S(2)}, u32[]{:S(2)}) collective-permute-start(bf16[8,32,1024]{2,1,0:T(8,128)(2,1)S(1)} %get-tuple-element.34), channel_id=1, source_target_pairs={{0,96},{32,0},{64,32},{96,64},{1,97},{33,1},{65,33},{97,65},{2,98}... | collective-permute-start | bytes 1572872 | tf_op jit(solution)/shard_map/ppermute | solution.py:18
  68.7 2.0 %collective-permute-start.7 = (bf16[512,512]{1,0:T(8,128)(2,1)S(1)}, bf16[512,512]{1,0:T(8,128)(2,1)S(1)}, u32[]{:S(2)}, u32[]{:S(2)}) collective-permute-start(bf16[512,512]{1,0:T(8,128)(2,1)S(1)} %begin.1), channel_id=1, source_target_pairs={{0,1},{1,0},{2,3},{3,2},{4,5},{5,4},{6,7},{7,6},{8,9},{9,8},{10,11... | collective-permute-start | bytes 1572872 | tf_op jit(solution)/shard_map/ppermute | solution.py:23
  72.3 5.5 %collective-permute-start.8 = (bf16[32,32,512]{2,1,0:T(8,128)(2,1)S(1)}, bf16[32,32,512]{2,1,0:T(8,128)(2,1)}, u32[]{:S(2)}, u32[]{:S(2)}) collective-permute-start(bf16[32,32,512]{2,1,0:T(8,128)(2,1)S(1)} %all_to_all.10.columns.own), channel_id=1, source_target_pairs={{0,1},{1,0},{2,3},{3,2},{4,5},{5,4},{6,7},{7,6},{8,9},{9,8},{10,11... | collective-permute-start | bytes 3145736 | tf_op jit(solution)/shard_map/ppermute | solution.py:23
  72.8 21.0 %all-to-all-start.1 = ((bf16[32,16,1024]{2,1,0:T(8,128)(2,1)}), bf16[32,16,1024]{2,1,0:T(8,128)(2,1)S(1)}, u32[]{:S(2)}, u32[]{:S(2)}) async-start(bf16[32,16,1024]{2,1,0:T(8,128)(2,1)} %bitcast.12), calls=%async_computation.1 | async-start | bytes 2097152 | tf_op jit(solution)/shard_map/all_to_all | solution.py:27
  77.9 2.2 %copy-start.2 = (f32[1,1,1024,1024]{3,2,1,0:T(8,128)S(1)}, f32[1,1,1024,1024]{3,2,1,0:T(8,128)}, u32[]{:S(2)}) copy-start(f32[1,1,1024,1024]{3,2,1,0:T(8,128)} %param.7) | copy-start | bytes 12582916
  94.8 14.4 %collective-permute-start.9 = (bf16[8,32,1024]{2,1,0:T(8,128)(2,1)S(1)}, bf16[8,32,1024]{2,1,0:T(8,128)(2,1)S(1)}, u32[]{:S(2)}, u32[]{:S(2)}) collective-permute-start(bf16[8,32,1024]{2,1,0:T(8,128)(2,1)S(1)} %get-tuple-element.53), channel_id=1, source_target_pairs={{0,32},{32,64},{64,96},{96,0},{1,33},{33,65},{65,97},{97,1},{2,34}... | collective-permute-start | bytes 1572872 | tf_op jit(solution)/shard_map/ppermute | solution.py:18
  96.2 13.7 %collective-permute-start.11 = (bf16[8,32,1024]{2,1,0:T(8,128)(2,1)S(1)}, bf16[8,32,1024]{2,1,0:T(8,128)(2,1)S(1)}, u32[]{:S(2)}, u32[]{:S(2)}) collective-permute-start(bf16[8,32,1024]{2,1,0:T(8,128)(2,1)S(1)} %get-tuple-element.54), channel_id=1, source_target_pairs={{0,96},{32,0},{64,32},{96,64},{1,97},{33,1},{65,33},{97,65},{2,98}... | collective-permute-start | bytes 1572872 | tf_op jit(solution)/shard_map/ppermute | solution.py:18
  97.6 22.8 %collective-permute-start.13 = (bf16[8,32,1024]{2,1,0:T(8,128)(2,1)S(1)}, bf16[8,32,1024]{2,1,0:T(8,128)(2,1)S(1)}, u32[]{:S(2)}, u32[]{:S(2)}) collective-permute-start(bf16[8,32,1024]{2,1,0:T(8,128)(2,1)S(1)} %get-tuple-element.54), channel_id=1, source_target_pairs={{0,32},{32,64},{64,96},{96,0},{1,33},{33,65},{65,97},{97,1},{2,34}... | collective-permute-start | bytes 1572872 | tf_op jit(solution)/shard_map/ppermute | solution.py:18
  97.6 22.8 %collective-permute-start.14 = (bf16[8,32,1024]{2,1,0:T(8,128)(2,1)S(1)}, bf16[8,32,1024]{2,1,0:T(8,128)(2,1)S(1)}, u32[]{:S(2)}, u32[]{:S(2)}) collective-permute-start(bf16[8,32,1024]{2,1,0:T(8,128)(2,1)S(1)} %get-tuple-element.53), channel_id=1, source_target_pairs={{0,96},{32,0},{64,32},{96,64},{1,97},{33,1},{65,33},{97,65},{2,98}... | collective-permute-start | bytes 1572872 | tf_op jit(solution)/shard_map/ppermute | solution.py:18
  109.2 22.5 %collective-permute-start.10 = (bf16[8,32,1024]{2,1,0:T(8,128)(2,1)S(1)}, bf16[8,32,1024]{2,1,0:T(8,128)(2,1)S(1)}, u32[]{:S(2)}, u32[]{:S(2)}) collective-permute-start(bf16[8,32,1024]{2,1,0:T(8,128)(2,1)S(1)} %collective-permute-done.9), channel_id=1, source_target_pairs={{0,32},{32,64},{64,96},{96,0},{1,33},{33,65},{65,97},{97,1},{2,34}... | collective-permute-start | bytes 1572872 | tf_op jit(solution)/shard_map/ppermute | solution.py:18
  109.9 21.8 %collective-permute-start.12 = (bf16[8,32,1024]{2,1,0:T(8,128)(2,1)S(1)}, bf16[8,32,1024]{2,1,0:T(8,128)(2,1)S(1)}, u32[]{:S(2)}, u32[]{:S(2)}) collective-permute-start(bf16[8,32,1024]{2,1,0:T(8,128)(2,1)S(1)} %collective-permute-done.11), channel_id=1, source_target_pairs={{0,96},{32,0},{64,32},{96,64},{1,97},{33,1},{65,33},{97,65},{2,98}... | collective-permute-start | bytes 1572872 | tf_op jit(solution)/shard_map/ppermute | solution.py:18
  120.5 11.1 %copy-start.3 = (bf16[64,32,1024]{2,1,0:T(8,128)(2,1)}, bf16[64,32,1024]{2,1,0:T(8,128)(2,1)S(1)}, u32[]{:S(2)}) copy-start(bf16[64,32,1024]{2,1,0:T(8,128)(2,1)S(1)} %constant_dynamic-update-slice_fusion.below) | copy-start | bytes 12582916

commit v6 on v5

--- a/solution.py
+++ b/solution.py
@@ -43,40 +43,26 @@
     return pl.BlockSpec(memory_space=space)
 
 
-def finish_sum_kernel(order, low, high, sum_low, sum_high, out, made, sems):
+def finish_sum_kernel(places, low, high, sum_low, sum_high, out, made, sems):
     half = low.shape[0]
     columns = out.shape[3]
 
-    def sent(place, side):
-        source = made.at[place, :, pl.ds(side * columns, columns)]
-        return pltpu.make_async_copy(source, out.at[place, side], sems.at[side])
-
-    def step(place, carry):
-        block = order[place]
-
-        @pl.when(block < half)
-        def _():
-            made[place] = added(low[block], sum_low[block])
-
-        @pl.when(block >= half)
-        def _():
-            made[place] = added(high[block - half], sum_high[block - half])
-
+    def sent(block, side):
+        source = made.at[block, :, pl.ds(side * columns, columns)]
+        return pltpu.make_async_copy(source, out.at[places[block], side], sems.at[side])
+
+    for block in range(2 * half):
+        partial, total = (low, sum_low) if block < half else (high, sum_high)
+        made[block] = added(partial[block % half], total[block % half])
         for side in range(2):
-            sent(place, side).start()
-        return carry
-
-    def finish(place, carry):
+            sent(block, side).start()
+    for block in range(2 * half):
         for side in range(2):
-            sent(place, side).wait()
-        return carry
-
-    lax.fori_loop(0, made.shape[0], step, 0, unroll=4)
-    lax.fori_loop(0, made.shape[0], finish, 0, unroll=4)
-
-
-def finish_sum(order, *terms):
-    group, (rows, columns) = order.shape[0], terms[0].shape[1:]
+            sent(block, side).wait()
+
+
+def finish_sum(places, *terms):
+    group, (rows, columns) = places.shape[0], terms[0].shape[1:]
     size = terms[0].size * 2
     return pl.pallas_call(
         finish_sum_kernel,
@@ -87,7 +73,7 @@
         compiler_params=pltpu.CompilerParams(vmem_limit_bytes=16 << 20),
         cost_estimate=pl.CostEstimate(flops=size, bytes_accessed=6 * size, transcendentals=0),
         name="finish_sum",
-    )(order, *terms)
+    )(places, *terms)
 
 
 def orient_kernel(
@@ -280,27 +266,15 @@
     )(core, own, other, stat)
 
 
-def step_kernel(order, old, update, low, high):
+def step_kernel(places, old, update, low, high):
     half = low.shape[0]
-
-    def step(place, carry):
-        block = order[place]
-        fresh = old[block].astype(f32) - step_size * update[place].astype(f32)
-
-        @pl.when(block < half)
-        def _():
-            low[block] = fresh.astype(bf16)
-
-        @pl.when(block >= half)
-        def _():
-            high[block - half] = fresh.astype(bf16)
-
-        return carry
-
-    lax.fori_loop(0, old.shape[0], step, 0, unroll=4)
-
-
-def stepped(order, old, update):
+    for block in range(2 * half):
+        fresh = old[block].astype(f32) - step_size * update[places[block]].astype(f32)
+        out = low if block < half else high
+        out[block % half] = fresh.astype(bf16)
+
+
+def stepped(places, old, update):
     shape = (old.shape[0] // 2,) + old.shape[1:]
     return pl.pallas_call(
         step_kernel,
@@ -310,7 +284,7 @@
         compiler_params=pltpu.CompilerParams(vmem_limit_bytes=16 << 20),
         cost_estimate=pl.CostEstimate(flops=2 * old.size, bytes_accessed=6 * old.size, transcendentals=0),
         name="step",
-    )(order, old, update)
+    )(places, old, update)
 
 
 def settle_kernel(replica, low_far, high_far, below, out, sems):
@@ -353,6 +327,10 @@
     replica = lax.axis_index("dp")
     core = (lax.axis_index("shard") % 2)[None]
     own_order = lax.dynamic_index_in_dim(table, replica, 0, keepdims=False)
+    numbers = jnp.arange(group, dtype=table.dtype)
+    own_places = jnp.max(
+        jnp.where(own_order[None, :] == numbers[:, None], numbers[None, :], 0), axis=1
+    )
 
     def piece(array, step, which):
         start = (replica + step) % replicas * group + which * half
@@ -382,7 +360,7 @@
     root, partner_root = in_order((root, partner_root), partial)
     left, right = oriented(core, root, partner_root, half_rows)
     sum_up, sum_down, left, right = lax.optimization_barrier((sum_up, sum_down, left, right))
-    whole = finish_sum(own_order, *partial, sum_up, sum_down)
+    whole = finish_sum(own_places, *partial, sum_up, sum_down)
 
     own_columns = exchanged(whole.reshape(shards, rows, size // 2))
     swapped = other_core(begun(left, own_columns))
@@ -395,7 +373,7 @@
     new_stat = statistics(core, own_columns, other_columns, stats[0, 0])
     own_params = lax.dynamic_slice_in_dim(params, replica * group, group, 0)
     update, new_stat, own_params = lax.optimization_barrier((update, new_stat, own_params))
-    low, high = stepped(own_order, own_params, update.reshape(group, rows, size))
+    low, high = stepped(own_places, own_params, update.reshape(group, rows, size))
     low_below = shifted(low, "dp", 1)
     high_above = shifted(high, "dp", -1)
     high_below = shifted(high, "dp", 1)

time: 133 us -> 133 us (level)
  no operation moved by 1% of the time
where the time goes in v6:
time: 133 us; the launch traced here: 132 us
  waiting for transfers between devices  57.6 us (43%)
  blocking collectives  25.7 us (19%)
  starting transfers between devices  22.9 us (17%)
  Pallas kernels  15 us (11%)
  local copies, waits for them, and re-layouts  8.22 us (6%)
  other arithmetic  2.12 us (2%)
    ppermute x12, waiting for transfers between devices, shifted(): lax.ppermute(block, axis, [(i, (i + offset) % count) for i in range(count)])  44.9 us
    all_to_all x1, blocking collectives, exchanged(): lax.all_to_all(blocks, 'shard', split_axis=0, concat_axis=0, tiled=True)  25.7 us
    ppermute x12, starting transfers between devices, shifted(): lax.ppermute(block, axis, [(i, (i + offset) % count) for i in range(count)])  16.7 us
    all_to_all x1, waiting for transfers between devices, exchanged(): lax.all_to_all(blocks, 'shard', split_axis=0, concat_axis=0, tiled=True)  8.08 us
    pallas_call x1, Pallas kernels, statistics(): pl.pallas_call(statistics_kernel, grid=(size // tile,), out_shape=jax.Sha...  5.67 us
    ppermute x3, waiting for transfers between devices, other_core(): return lax.ppermute(block, 'shard', [(i, i ^ 1) for i in range(count)])  4.58 us
    all_to_all x1, starting transfers between devices, exchanged(): lax.all_to_all(blocks, 'shard', split_axis=0, concat_axis=0, tiled=True)  3.73 us
  transfers between devices with their start and end apart: 16, of which 9 were waited for; matrix products, arithmetic and copies ran while one was open for 5% of the time, Pallas kernels for 7%

profile of v6, /device:TPU:1, one launch (start us, length us, event | category | flops | bytes accessed | tf_op | source)
XLA Modules:
  0.0 132.4 jit_solution(10250616593801704402)
XLA Ops:
  0.7 1.3 dynamic-slice_bitcast_fusion
  2.0 1.5 %collective-permute-start = (f32[1024,1024]{1,0:T(8,128)}, f32[1024,1024]{1,0:T(8,128)}, u32[]{:S(2)}, u32[]{:S(2)}) collective-permute-start(f32[1024,1024]{1,0:T(8,128)} %bitcast.19), channel_id=1, source_target_pairs={{0,1},{1,0},{2,3},{3,2},{4,5},{5,4},{6,7},{7,6},{8,9},{9,8},{10,11... | collective-permute-start | bytes 12582920 | tf_op jit(solution)/shard_map/ppermute | solution.py:23
  3.5 1.4 %collective-permute-start.1 = (bf16[8,32,1024]{2,1,0:T(8,128)(2,1)S(1)}, bf16[8,32,1024]{2,1,0:T(8,128)(2,1)S(1)}, u32[]{:S(2)}, u32[]{:S(2)}) collective-permute-start(bf16[8,32,1024]{2,1,0:T(8,128)(2,1)S(1)} %get-tuple-element.29), channel_id=1, source_target_pairs={{0,32},{32,64},{64,96},{96,0},{1,33},{33,65},{65,97},{97,1},{2,34}... | collective-permute-start | bytes 1572872 | tf_op jit(solution)/shard_map/ppermute | solution.py:18
  4.9 1.4 %collective-permute-start.2 = (bf16[8,32,1024]{2,1,0:T(8,128)(2,1)S(1)}, bf16[8,32,1024]{2,1,0:T(8,128)(2,1)S(1)}, u32[]{:S(2)}, u32[]{:S(2)}) collective-permute-start(bf16[8,32,1024]{2,1,0:T(8,128)(2,1)S(1)} %get-tuple-element.30), channel_id=1, source_target_pairs={{0,96},{32,0},{64,32},{96,64},{1,97},{33,1},{65,33},{97,65},{2,98}... | collective-permute-start | bytes 1572872 | tf_op jit(solution)/shard_map/ppermute | solution.py:18
  6.3 4.3 %collective-permute-done = f32[1024,1024]{1,0:T(8,128)} collective-permute-done((f32[1024,1024]{1,0:T(8,128)}, f32[1024,1024]{1,0:T(8,128)}, u32[]{:S(2)}, u32[]{:S(2)}) %collective-permute-start) | collective-permute-done | bytes 4194336 | tf_op jit(solution)/shard_map/ppermute | solution.py:23
  10.6 1.3 constant_dynamic-slice_fusion.1
  11.9 1.4 %collective-permute-start.5 = (bf16[8,32,1024]{2,1,0:T(8,128)(2,1)S(1)}, bf16[8,32,1024]{2,1,0:T(8,128)(2,1)S(1)}, u32[]{:S(2)}, u32[]{:S(2)}) collective-permute-start(bf16[8,32,1024]{2,1,0:T(8,128)(2,1)S(1)} %get-tuple-element.35), channel_id=1, source_target_pairs={{0,32},{32,64},{64,96},{96,0},{1,33},{33,65},{65,97},{97,1},{2,34}... | collective-permute-start | bytes 1572872 | tf_op jit(solution)/shard_map/ppermute | solution.py:18
  13.4 1.5 %collective-permute-start.6 = (bf16[8,32,1024]{2,1,0:T(8,128)(2,1)S(1)}, bf16[8,32,1024]{2,1,0:T(8,128)(2,1)S(1)}, u32[]{:S(2)}, u32[]{:S(2)}) collective-permute-start(bf16[8,32,1024]{2,1,0:T(8,128)(2,1)S(1)} %get-tuple-element.36), channel_id=1, source_target_pairs={{0,96},{32,0},{64,32},{96,64},{1,97},{33,1},{65,33},{97,65},{2,98}... | collective-permute-start | bytes 1572872 | tf_op jit(solution)/shard_map/ppermute | solution.py:18
  14.9 3.6 %collective-permute-done.1 = bf16[8,32,1024]{2,1,0:T(8,128)(2,1)S(1)} collective-permute-done((bf16[8,32,1024]{2,1,0:T(8,128)(2,1)S(1)}, bf16[8,32,1024]{2,1,0:T(8,128)(2,1)S(1)}, u32[]{:S(2)}, u32[]{:S(2)}) %collective-permute-start.1) | collective-permute-done | bytes 524320 | tf_op jit(solution)/shard_map/ppermute | solution.py:18
  18.5 1.6 %add_convert_fusion.2 = (bf16[8,32,1024]{2,1,0:T(8,128)(2,1)S(1)}, bf16[8,32,1024]{2,1,0:T(8,128)(2,1)S(1)}) fusion(bf16[8,32,1024]{2,1,0:T(8,128)(2,1)S(1)} %collective-permute-done.2, bf16[64,32,1024]{2,1,0:T(8,128)(2,1)} %bitcast.27, s32[]{:T(128)S(6)} %select_n.87, bf16[8,32,1024]{2,1,0:T(8,128)(2,1)S(1)} %collective-permute-done.1, s32[]{:T(128)S(6)} %select_n.85), kind=kLoop, calls=%fused_computation.2 | loop fusion | flops 2097152 | bytes 3145736 | tf_op jit(solution)/shard_map/convert_element_type | solution.py:34
  21.0 1.8 %collective-permute-start.4 = (bf16[8,32,1024]{2,1,0:T(8,128)(2,1)S(1)}, bf16[8,32,1024]{2,1,0:T(8,128)(2,1)S(1)}, u32[]{:S(2)}, u32[]{:S(2)}) collective-permute-start(bf16[8,32,1024]{2,1,0:T(8,128)(2,1)S(1)} %get-tuple-element.34), channel_id=1, source_target_pairs={{0,96},{32,0},{64,32},{96,64},{1,97},{33,1},{65,33},{97,65},{2,98}... | collective-permute-start | bytes 1572872 | tf_op jit(solution)/shard_map/ppermute | solution.py:18
  22.9 1.3 constant_dynamic-slice_fusion.3
  24.3 5.4 %collective-permute-done.5 = bf16[8,32,1024]{2,1,0:T(8,128)(2,1)S(1)} collective-permute-done((bf16[8,32,1024]{2,1,0:T(8,128)(2,1)S(1)}, bf16[8,32,1024]{2,1,0:T(8,128)(2,1)S(1)}, u32[]{:S(2)}, u32[]{:S(2)}) %collective-permute-start.5) | collective-permute-done | bytes 524320 | tf_op jit(solution)/shard_map/ppermute | solution.py:18
  30.1 2.7 %orient.1 = (bf16[2,512,1024]{2,1,0:T(8,128)(2,1)S(1)}, bf16[2,512,1024]{2,1,0:T(8,128)(2,1)S(1)}) custom-call(s32[1]{0:T(128)} %bitcast.6.core, f32[32,2,16,1024]{3,2,1,0:T(8,128)S(1)} %bitcast.20, f32[2,512,1024]{2,1,0:T(8,128)S(1)} %bitcast.21, f32[32,2,16,1024]{3,2,1,0:T(8,128)} %bitcast.9.partner, f32[2,512,1024]{2,1,0:T(8,128)} %bitcast.10.partner_halves), custom_call_target="tpu_custom_call" | custom-call | flops 1048576 | bytes 12582912 | tf_op jit(solution)/shard_map/orient/pallas_call | solution.py:122
  32.8 8.2 %collective-permute-done.3.sum_low = bf16[8,32,1024]{2,1,0:T(8,128)(2,1)S(1)} collective-permute-done((bf16[8,32,1024]{2,1,0:T(8,128)(2,1)S(1)}, bf16[8,32,1024]{2,1,0:T(8,128)(2,1)S(1)}, u32[]{:S(2)}, u32[]{:S(2)}) %collective-permute-start.3) | collective-permute-done | bytes 524320 | tf_op jit(solution)/shard_map/ppermute | solution.py:18
  40.9 1.3 finish_sum.1
  42.2 25.7 %all_to_all.10.columns.own = bf16[32,32,512]{2,1,0:T(8,128)(2,1)S(1)} all-to-all(bf16[32,32,512]{2,1,0:T(8,128)(2,1)S(1)} %bitcast.24), channel_id=1, replica_groups=mesh['dp'=4,'shard'=32] {'shard'}, dimensions={0} | all-to-all | bytes 2097152 | tf_op jit(solution)/shard_map/all_to_all | solution.py:27
  69.1 1.3 share.1.part
  70.6 1.6 %complete.1 = bf16[512,1024]{1,0:T(8,128)(2,1)} custom-call(f32[512,1024]{1,0:T(8,128)S(1)} %share.1.part, bf16[512,512]{1,0:T(8,128)(2,1)S(1)} %collective-permute-done.7.other, bf16[2,512,1024]{2,1,0:T(8,128)(2,1)S(1)} %get-tuple-element.49.right), custom_call_target="tpu_custom_call" | custom-call | flops 536870912 | bytes 4194304 | tf_op jit(solution)/shard_map/complete/pallas_call | solution.py:207
  72.7 3.7 %all-to-all-start.1 = ((bf16[32,16,1024]{2,1,0:T(8,128)(2,1)}), bf16[32,16,1024]{2,1,0:T(8,128)(2,1)S(1)}, u32[]{:S(2)}, u32[]{:S(2)}) async-start(bf16[32,16,1024]{2,1,0:T(8,128)(2,1)} %bitcast.12), calls=%async_computation.1 | async-start | bytes 2097152 | tf_op jit(solution)/shard_map/all_to_all | solution.py:27
  76.4 1.3 constant_dynamic-slice_fusion.old
  77.8 2.2 %copy-done.2 = f32[1,1,1024,1024]{3,2,1,0:T(8,128)S(1)} copy-done((f32[1,1,1024,1024]{3,2,1,0:T(8,128)S(1)}, f32[1,1,1024,1024]{3,2,1,0:T(8,128)}, u32[]{:S(2)}) %copy-start.2) | copy-done | bytes 4194328
  79.9 5.7 %statistics.1 = f32[1024,1024]{1,0:T(8,128)} custom-call(s32[1]{0:T(128)} %bitcast.6.core, bf16[32,32,512]{2,1,0:T(8,128)(2,1)S(1)} %all_to_all.10.columns.own, bf16[32,32,512]{2,1,0:T(8,128)(2,1)} %collective-permute-done.8.other, f32[1024,1024]{1,0:T(8,128)S(1)} %bitcast.23), custom_call_target="tpu_custom_call" | custom-call | flops 2147483648 | bytes 12582912 | tf_op jit(solution)/shard_map/statistics/pallas_call | solution.py:256
  85.6 8.1 %all-to-all-done.1 = bf16[32,16,1024]{2,1,0:T(8,128)(2,1)S(1)} async-done(((bf16[32,16,1024]{2,1,0:T(8,128)(2,1)}), bf16[32,16,1024]{2,1,0:T(8,128)(2,1)S(1)}, u32[]{:S(2)}, u32[]{:S(2)}) %all-to-all-start.1) | async-done | bytes 1048608 | tf_op jit(solution)/shard_map/all_to_all | solution.py:27
  94.5 1.4 %collective-permute-start.9 = (bf16[8,32,1024]{2,1,0:T(8,128)(2,1)S(1)}, bf16[8,32,1024]{2,1,0:T(8,128)(2,1)S(1)}, u32[]{:S(2)}, u32[]{:S(2)}) collective-permute-start(bf16[8,32,1024]{2,1,0:T(8,128)(2,1)S(1)} %get-tuple-element.53), channel_id=1, source_target_pairs={{0,32},{32,64},{64,96},{96,0},{1,33},{33,65},{65,97},{97,1},{2,34}... | collective-permute-start | bytes 1572872 | tf_op jit(solution)/shard_map/ppermute | solution.py:18
  95.9 1.4 %collective-permute-start.11 = (bf16[8,32,1024]{2,1,0:T(8,128)(2,1)S(1)}, bf16[8,32,1024]{2,1,0:T(8,128)(2,1)S(1)}, u32[]{:S(2)}, u32[]{:S(2)}) collective-permute-start(bf16[8,32,1024]{2,1,0:T(8,128)(2,1)S(1)} %get-tuple-element.54), channel_id=1, source_target_pairs={{0,96},{32,0},{64,32},{96,64},{1,97},{33,1},{65,33},{97,65},{2,98}... | collective-permute-start | bytes 1572872 | tf_op jit(solution)/shard_map/ppermute | solution.py:18
  97.4 2.6 %collective-permute-start.14 = (bf16[8,32,1024]{2,1,0:T(8,128)(2,1)S(1)}, bf16[8,32,1024]{2,1,0:T(8,128)(2,1)S(1)}, u32[]{:S(2)}, u32[]{:S(2)}) collective-permute-start(bf16[8,32,1024]{2,1,0:T(8,128)(2,1)S(1)} %get-tuple-element.53), channel_id=1, source_target_pairs={{0,96},{32,0},{64,32},{96,64},{1,97},{33,1},{65,33},{97,65},{2,98}... | collective-permute-start | bytes 1572872 | tf_op jit(solution)/shard_map/ppermute | solution.py:18
  100.0 8.9 %collective-permute-done.9 = bf16[8,32,1024]{2,1,0:T(8,128)(2,1)S(1)} collective-permute-done((bf16[8,32,1024]{2,1,0:T(8,128)(2,1)S(1)}, bf16[8,32,1024]{2,1,0:T(8,128)(2,1)S(1)}, u32[]{:S(2)}, u32[]{:S(2)}) %collective-permute-start.9) | collective-permute-done | bytes 524320 | tf_op jit(solution)/shard_map/ppermute | solution.py:18
  109.6 2.7 %collective-permute-start.12 = (bf16[8,32,1024]{2,1,0:T(8,128)(2,1)S(1)}, bf16[8,32,1024]{2,1,0:T(8,128)(2,1)S(1)}, u32[]{:S(2)}, u32[]{:S(2)}) collective-permute-start(bf16[8,32,1024]{2,1,0:T(8,128)(2,1)S(1)} %collective-permute-done.11), channel_id=1, source_target_pairs={{0,96},{32,0},{64,32},{96,64},{1,97},{33,1},{65,33},{97,65},{2,98}... | collective-permute-start | bytes 1572872 | tf_op jit(solution)/shard_map/ppermute | solution.py:18
  112.4 7.7 %collective-permute-done.13 = bf16[8,32,1024]{2,1,0:T(8,128)(2,1)S(1)} collective-permute-done((bf16[8,32,1024]{2,1,0:T(8,128)(2,1)S(1)}, bf16[8,32,1024]{2,1,0:T(8,128)(2,1)S(1)}, u32[]{:S(2)}, u32[]{:S(2)}) %collective-permute-start.13) | collective-permute-done | bytes 524320 | tf_op jit(solution)/shard_map/ppermute | solution.py:18
  120.3 11.1 %collective-permute-done.10.low_far = bf16[8,32,1024]{2,1,0:T(8,128)(2,1)S(1)} collective-permute-done((bf16[8,32,1024]{2,1,0:T(8,128)(2,1)S(1)}, bf16[8,32,1024]{2,1,0:T(8,128)(2,1)S(1)}, u32[]{:S(2)}, u32[]{:S(2)}) %collective-permute-start.10) | collective-permute-done | bytes 524320 | tf_op jit(solution)/shard_map/ppermute | solution.py:18
  131.4 1.0 settle.1
  (32 shorter events, 5.2 us)
Async XLA Ops:
  0.6 5.7 %copy-start = (s32[4,16]{1,0:T(4,128)S(1)}, s32[4,16]{1,0:T(4,128)}, u32[]{:S(2)}) copy-start(s32[4,16]{1,0:T(4,128)} %param.9) | copy-start | bytes 772
  2.0 8.6 %collective-permute-start = (f32[1024,1024]{1,0:T(8,128)}, f32[1024,1024]{1,0:T(8,128)}, u32[]{:S(2)}, u32[]{:S(2)}) collective-permute-start(f32[1024,1024]{1,0:T(8,128)} %bitcast.19), channel_id=1, source_target_pairs={{0,1},{1,0},{2,3},{3,2},{4,5},{5,4},{6,7},{7,6},{8,9},{9,8},{10,11... | collective-permute-start | bytes 12582920 | tf_op jit(solution)/shard_map/ppermute | solution.py:23
  3.5 15.0 %collective-permute-start.1 = (bf16[8,32,1024]{2,1,0:T(8,128)(2,1)S(1)}, bf16[8,32,1024]{2,1,0:T(8,128)(2,1)S(1)}, u32[]{:S(2)}, u32[]{:S(2)}) collective-permute-start(bf16[8,32,1024]{2,1,0:T(8,128)(2,1)S(1)} %get-tuple-element.29), channel_id=1, source_target_pairs={{0,32},{32,64},{64,96},{96,0},{1,33},{33,65},{65,97},{97,1},{2,34}... | collective-permute-start | bytes 1572872 | tf_op jit(solution)/shard_map/ppermute | solution.py:18
  4.9 13.6 %collective-permute-start.2 = (bf16[8,32,1024]{2,1,0:T(8,128)(2,1)S(1)}, bf16[8,32,1024]{2,1,0:T(8,128)(2,1)S(1)}, u32[]{:S(2)}, u32[]{:S(2)}) collective-permute-start(bf16[8,32,1024]{2,1,0:T(8,128)(2,1)S(1)} %get-tuple-element.30), channel_id=1, source_target_pairs={{0,96},{32,0},{64,32},{96,64},{1,97},{33,1},{65,33},{97,65},{2,98}... | collective-permute-start | bytes 1572872 | tf_op jit(solution)/shard_map/ppermute | solution.py:18
  11.9 18.2 %copy-start.1 = (f32[1,1,1024,1024]{3,2,1,0:T(8,128)S(1)}, f32[1,1,1024,1024]{3,2,1,0:T(8,128)}, u32[]{:S(2)}) copy-start(f32[1,1,1024,1024]{3,2,1,0:T(8,128)} %param.8) | copy-start | bytes 12582916
  11.9 17.8 %collective-permute-start.5 = (bf16[8,32,1024]{2,1,0:T(8,128)(2,1)S(1)}, bf16[8,32,1024]{2,1,0:T(8,128)(2,1)S(1)}, u32[]{:S(2)}, u32[]{:S(2)}) collective-permute-start(bf16[8,32,1024]{2,1,0:T(8,128)(2,1)S(1)} %get-tuple-element.35), channel_id=1, source_target_pairs={{0,32},{32,64},{64,96},{96,0},{1,33},{33,65},{65,97},{97,1},{2,34}... | collective-permute-start | bytes 1572872 | tf_op jit(solution)/shard_map/ppermute | solution.py:18
  13.4 16.3 %collective-permute-start.6 = (bf16[8,32,1024]{2,1,0:T(8,128)(2,1)S(1)}, bf16[8,32,1024]{2,1,0:T(8,128)(2,1)S(1)}, u32[]{:S(2)}, u32[]{:S(2)}) collective-permute-start(bf16[8,32,1024]{2,1,0:T(8,128)(2,1)S(1)} %get-tuple-element.36), channel_id=1, source_target_pairs={{0,96},{32,0},{64,32},{96,64},{1,97},{33,1},{65,33},{97,65},{2,98}... | collective-permute-start | bytes 1572872 | tf_op jit(solution)/shard_map/ppermute | solution.py:18
  20.1 20.9 %collective-permute-start.3 = (bf16[8,32,1024]{2,1,0:T(8,128)(2,1)S(1)}, bf16[8,32,1024]{2,1,0:T(8,128)(2,1)S(1)}, u32[]{:S(2)}, u32[]{:S(2)}) collective-permute-start(bf16[8,32,1024]{2,1,0:T(8,128)(2,1)S(1)} %get-tuple-element.33), channel_id=1, source_target_pairs={{0,32},{32,64},{64,96},{96,0},{1,33},{33,65},{65,97},{97,1},{2,34}... | collective-permute-start | bytes 1572872 | tf_op jit(solution)/shard_map/ppermute | solution.py:18
  21.0 19.9 %collective-permute-start.4 = (bf16[8,32,1024]{2,1,0:T(8,128)(2,1)S(1)}, bf16[8,32,1024]{2,1,0:T(8,128)(2,1)S(1)}, u32[]{:S(2)}, u32[]{:S(2)}) collective-permute-start(bf16[8,32,1024]{2,1,0:T(8,128)(2,1)S(1)} %get-tuple-element.34), channel_id=1, source_target_pairs={{0,96},{32,0},{64,32},{96,64},{1,97},{33,1},{65,33},{97,65},{2,98}... | collective-permute-start | bytes 1572872 | tf_op jit(solution)/shard_map/ppermute | solution.py:18
  68.6 2.0 %collective-permute-start.7 = (bf16[512,512]{1,0:T(8,128)(2,1)S(1)}, bf16[512,512]{1,0:T(8,128)(2,1)S(1)}, u32[]{:S(2)}, u32[]{:S(2)}) collective-permute-start(bf16[512,512]{1,0:T(8,128)(2,1)S(1)} %begin.1), channel_id=1, source_target_pairs={{0,1},{1,0},{2,3},{3,2},{4,5},{5,4},{6,7},{7,6},{8,9},{9,8},{10,11... | collective-permute-start | bytes 1572872 | tf_op jit(solution)/shard_map/ppermute | solution.py:23
  72.2 5.5 %collective-permute-start.8 = (bf16[32,32,512]{2,1,0:T(8,128)(2,1)S(1)}, bf16[32,32,512]{2,1,0:T(8,128)(2,1)}, u32[]{:S(2)}, u32[]{:S(2)}) collective-permute-start(bf16[32,32,512]{2,1,0:T(8,128)(2,1)S(1)} %all_to_all.10.columns.own), channel_id=1, source_target_pairs={{0,1},{1,0},{2,3},{3,2},{4,5},{5,4},{6,7},{7,6},{8,9},{9,8},{10,11... | collective-permute-start | bytes 3145736 | tf_op jit(solution)/shard_map/ppermute | solution.py:23
  72.7 21.0 %all-to-all-start.1 = ((bf16[32,16,1024]{2,1,0:T(8,128)(2,1)}), bf16[32,16,1024]{2,1,0:T(8,128)(2,1)S(1)}, u32[]{:S(2)}, u32[]{:S(2)}) async-start(bf16[32,16,1024]{2,1,0:T(8,128)(2,1)} %bitcast.12), calls=%async_computation.1 | async-start | bytes 2097152 | tf_op jit(solution)/shard_map/all_to_all | solution.py:27
  77.7 2.2 %copy-start.2 = (f32[1,1,1024,1024]{3,2,1,0:T(8,128)S(1)}, f32[1,1,1024,1024]{3,2,1,0:T(8,128)}, u32[]{:S(2)}) copy-start(f32[1,1,1024,1024]{3,2,1,0:T(8,128)} %param.7) | copy-start | bytes 12582916
  94.5 14.4 %collective-permute-start.9 = (bf16[8,32,1024]{2,1,0:T(8,128)(2,1)S(1)}, bf16[8,32,1024]{2,1,0:T(8,128)(2,1)S(1)}, u32[]{:S(2)}, u32[]{:S(2)}) collective-permute-start(bf16[8,32,1024]{2,1,0:T(8,128)(2,1)S(1)} %get-tuple-element.53), channel_id=1, source_target_pairs={{0,32},{32,64},{64,96},{96,0},{1,33},{33,65},{65,97},{97,1},{2,34}... | collective-permute-start | bytes 1572872 | tf_op jit(solution)/shard_map/ppermute | solution.py:18
  95.9 13.7 %collective-permute-start.11 = (bf16[8,32,1024]{2,1,0:T(8,128)(2,1)S(1)}, bf16[8,32,1024]{2,1,0:T(8,128)(2,1)S(1)}, u32[]{:S(2)}, u32[]{:S(2)}) collective-permute-start(bf16[8,32,1024]{2,1,0:T(8,128)(2,1)S(1)} %get-tuple-element.54), channel_id=1, source_target_pairs={{0,96},{32,0},{64,32},{96,64},{1,97},{33,1},{65,33},{97,65},{2,98}... | collective-permute-start | bytes 1572872 | tf_op jit(solution)/shard_map/ppermute | solution.py:18
  97.3 22.8 %collective-permute-start.13 = (bf16[8,32,1024]{2,1,0:T(8,128)(2,1)S(1)}, bf16[8,32,1024]{2,1,0:T(8,128)(2,1)S(1)}, u32[]{:S(2)}, u32[]{:S(2)}) collective-permute-start(bf16[8,32,1024]{2,1,0:T(8,128)(2,1)S(1)} %get-tuple-element.54), channel_id=1, source_target_pairs={{0,32},{32,64},{64,96},{96,0},{1,33},{33,65},{65,97},{97,1},{2,34}... | collective-permute-start | bytes 1572872 | tf_op jit(solution)/shard_map/ppermute | solution.py:18
  97.4 22.8 %collective-permute-start.14 = (bf16[8,32,1024]{2,1,0:T(8,128)(2,1)S(1)}, bf16[8,32,1024]{2,1,0:T(8,128)(2,1)S(1)}, u32[]{:S(2)}, u32[]{:S(2)}) collective-permute-start(bf16[8,32,1024]{2,1,0:T(8,128)(2,1)S(1)} %get-tuple-element.53), channel_id=1, source_target_pairs={{0,96},{32,0},{64,32},{96,64},{1,97},{33,1},{65,33},{97,65},{2,98}... | collective-permute-start | bytes 1572872 | tf_op jit(solution)/shard_map/ppermute | solution.py:18
  108.9 22.5 %collective-permute-start.10 = (bf16[8,32,1024]{2,1,0:T(8,128)(2,1)S(1)}, bf16[8,32,1024]{2,1,0:T(8,128)(2,1)S(1)}, u32[]{:S(2)}, u32[]{:S(2)}) collective-permute-start(bf16[8,32,1024]{2,1,0:T(8,128)(2,1)S(1)} %collective-permute-done.9), channel_id=1, source_target_pairs={{0,32},{32,64},{64,96},{96,0},{1,33},{33,65},{65,97},{97,1},{2,34}... | collective-permute-start | bytes 1572872 | tf_op jit(solution)/shard_map/ppermute | solution.py:18
  109.6 21.8 %collective-permute-start.12 = (bf16[8,32,1024]{2,1,0:T(8,128)(2,1)S(1)}, bf16[8,32,1024]{2,1,0:T(8,128)(2,1)S(1)}, u32[]{:S(2)}, u32[]{:S(2)}) collective-permute-start(bf16[8,32,1024]{2,1,0:T(8,128)(2,1)S(1)} %collective-permute-done.11), channel_id=1, source_target_pairs={{0,96},{32,0},{64,32},{96,64},{1,97},{33,1},{65,33},{97,65},{2,98}... | collective-permute-start | bytes 1572872 | tf_op jit(solution)/shard_map/ppermute | solution.py:18
  120.3 11.1 %copy-start.3 = (bf16[64,32,1024]{2,1,0:T(8,128)(2,1)}, bf16[64,32,1024]{2,1,0:T(8,128)(2,1)S(1)}, u32[]{:S(2)}) copy-start(bf16[64,32,1024]{2,1,0:T(8,128)(2,1)S(1)} %constant_dynamic-update-slice_fusion.below) | copy-start | bytes 12582916

commit v7 on v6

--- a/solution.py
+++ b/solution.py
@@ -348,11 +348,8 @@
     near_up = shifted(near[0], "dp", 1)
     near_down = shifted(near[1], "dp", -1)
 
-    sums = lax.optimization_barrier(
-        (added(piece(mine, 1, 0), far_up), added(piece(mine, 3, 1), far_down))
-    )
-    sum_up = shifted(sums[0], "dp", 1)
-    sum_down = shifted(sums[1], "dp", -1)
+    sum_up = shifted(added(piece(mine, 1, 0), far_up), "dp", 1)
+    sum_down = shifted(added(piece(mine, 3, 1), far_down), "dp", -1)
     own, near_up, near_down = lax.optimization_barrier(
         (lax.dynamic_slice_in_dim(mine, replica * group, group, 0), near_up, near_down)
     )

time: 133 us -> 133 us (level)
  no operation moved by 1% of the time
where the time goes in v7:
time: 133 us; the launch traced here: 132 us
  waiting for transfers between devices  57.6 us (43%)
  blocking collectives  25.7 us (19%)
  starting transfers between devices  22.9 us (17%)
  Pallas kernels  15 us (11%)
  local copies, waits for them, and re-layouts  8.22 us (6%)
  other arithmetic  2.12 us (2%)
    ppermute x12, waiting for transfers between devices, shifted(): lax.ppermute(block, axis, [(i, (i + offset) % count) for i in range(count)])  44.9 us
    all_to_all x1, blocking collectives, exchanged(): lax.all_to_all(blocks, 'shard', split_axis=0, concat_axis=0, tiled=True)  25.7 us
    ppermute x12, starting transfers between devices, shifted(): lax.ppermute(block, axis, [(i, (i + offset) % count) for i in range(count)])  16.7 us
    all_to_all x1, waiting for transfers between devices, exchanged(): lax.all_to_all(blocks, 'shard', split_axis=0, concat_axis=0, tiled=True)  8.07 us
    pallas_call x1, Pallas kernels, statistics(): pl.pallas_call(statistics_kernel, grid=(size // tile,), out_shape=jax.Sha...  5.68 us
    ppermute x3, waiting for transfers between devices, other_core(): return lax.ppermute(block, 'shard', [(i, i ^ 1) for i in range(count)])  4.58 us
    all_to_all x1, starting transfers between devices, exchanged(): lax.all_to_all(blocks, 'shard', split_axis=0, concat_axis=0, tiled=True)  3.73 us
  transfers between devices with their start and end apart: 16, of which 9 were waited for; matrix products, arithmetic and copies ran while one was open for 5% of the time, Pallas kernels for 7%

profile of v7, /device:TPU:1, one launch (start us, length us, event | category | flops | bytes accessed | tf_op | source)
XLA Modules:
  0.0 132.4 jit_solution(18299815771744379817)
XLA Ops:
  0.7 1.3 dynamic-slice_bitcast_fusion
  2.0 1.5 %collective-permute-start = (f32[1024,1024]{1,0:T(8,128)}, f32[1024,1024]{1,0:T(8,128)}, u32[]{:S(2)}, u32[]{:S(2)}) collective-permute-start(f32[1024,1024]{1,0:T(8,128)} %bitcast.19), channel_id=1, source_target_pairs={{0,1},{1,0},{2,3},{3,2},{4,5},{5,4},{6,7},{7,6},{8,9},{9,8},{10,11... | collective-permute-start | bytes 12582920 | tf_op jit(solution)/shard_map/ppermute | solution.py:23
  3.5 1.4 %collective-permute-start.1 = (bf16[8,32,1024]{2,1,0:T(8,128)(2,1)S(1)}, bf16[8,32,1024]{2,1,0:T(8,128)(2,1)S(1)}, u32[]{:S(2)}, u32[]{:S(2)}) collective-permute-start(bf16[8,32,1024]{2,1,0:T(8,128)(2,1)S(1)} %get-tuple-element.27), channel_id=1, source_target_pairs={{0,32},{32,64},{64,96},{96,0},{1,33},{33,65},{65,97},{97,1},{2,34}... | collective-permute-start | bytes 1572872 | tf_op jit(solution)/shard_map/ppermute | solution.py:18
  4.9 1.4 %collective-permute-start.3 = (bf16[8,32,1024]{2,1,0:T(8,128)(2,1)S(1)}, bf16[8,32,1024]{2,1,0:T(8,128)(2,1)S(1)}, u32[]{:S(2)}, u32[]{:S(2)}) collective-permute-start(bf16[8,32,1024]{2,1,0:T(8,128)(2,1)S(1)} %get-tuple-element.28), channel_id=1, source_target_pairs={{0,96},{32,0},{64,32},{96,64},{1,97},{33,1},{65,33},{97,65},{2,98}... | collective-permute-start | bytes 1572872 | tf_op jit(solution)/shard_map/ppermute | solution.py:18
  6.3 4.3 %collective-permute-done = f32[1024,1024]{1,0:T(8,128)} collective-permute-done((f32[1024,1024]{1,0:T(8,128)}, f32[1024,1024]{1,0:T(8,128)}, u32[]{:S(2)}, u32[]{:S(2)}) %collective-permute-start) | collective-permute-done | bytes 4194336 | tf_op jit(solution)/shard_map/ppermute | solution.py:23
  10.6 1.3 constant_dynamic-slice_fusion.1
  11.9 1.4 %collective-permute-start.5 = (bf16[8,32,1024]{2,1,0:T(8,128)(2,1)S(1)}, bf16[8,32,1024]{2,1,0:T(8,128)(2,1)S(1)}, u32[]{:S(2)}, u32[]{:S(2)}) collective-permute-start(bf16[8,32,1024]{2,1,0:T(8,128)(2,1)S(1)} %get-tuple-element.31), channel_id=1, source_target_pairs={{0,32},{32,64},{64,96},{96,0},{1,33},{33,65},{65,97},{97,1},{2,34}... | collective-permute-start | bytes 1572872 | tf_op jit(solution)/shard_map/ppermute | solution.py:18
  13.4 1.5 %collective-permute-start.6 = (bf16[8,32,1024]{2,1,0:T(8,128)(2,1)S(1)}, bf16[8,32,1024]{2,1,0:T(8,128)(2,1)S(1)}, u32[]{:S(2)}, u32[]{:S(2)}) collective-permute-start(bf16[8,32,1024]{2,1,0:T(8,128)(2,1)S(1)} %get-tuple-element.32), channel_id=1, source_target_pairs={{0,96},{32,0},{64,32},{96,64},{1,97},{33,1},{65,33},{97,65},{2,98}... | collective-permute-start | bytes 1572872 | tf_op jit(solution)/shard_map/ppermute | solution.py:18
  14.9 3.6 %collective-permute-done.1 = bf16[8,32,1024]{2,1,0:T(8,128)(2,1)S(1)} collective-permute-done((bf16[8,32,1024]{2,1,0:T(8,128)(2,1)S(1)}, bf16[8,32,1024]{2,1,0:T(8,128)(2,1)S(1)}, u32[]{:S(2)}, u32[]{:S(2)}) %collective-permute-start.1) | collective-permute-done | bytes 524320 | tf_op jit(solution)/shard_map/ppermute | solution.py:18
  18.5 1.6 %add_convert_fusion.2 = (bf16[8,32,1024]{2,1,0:T(8,128)(2,1)S(1)}, bf16[8,32,1024]{2,1,0:T(8,128)(2,1)S(1)}) fusion(bf16[8,32,1024]{2,1,0:T(8,128)(2,1)S(1)} %collective-permute-done.3, bf16[64,32,1024]{2,1,0:T(8,128)(2,1)} %bitcast.27, s32[]{:T(128)S(6)} %select_n.87, bf16[8,32,1024]{2,1,0:T(8,128)(2,1)S(1)} %collective-permute-done.1, s32[]{:T(128)S(6)} %select_n.85), kind=kLoop, calls=%fused_computation.2 | loop fusion | flops 2097152 | bytes 3145736 | tf_op jit(solution)/shard_map/convert_element_type | solution.py:34
  21.0 1.8 %collective-permute-start.4 = (bf16[8,32,1024]{2,1,0:T(8,128)(2,1)S(1)}, bf16[8,32,1024]{2,1,0:T(8,128)(2,1)S(1)}, u32[]{:S(2)}, u32[]{:S(2)}) collective-permute-start(bf16[8,32,1024]{2,1,0:T(8,128)(2,1)S(1)} %get-tuple-element.54), channel_id=1, source_target_pairs={{0,96},{32,0},{64,32},{96,64},{1,97},{33,1},{65,33},{97,65},{2,98}... | collective-permute-start | bytes 1572872 | tf_op jit(solution)/shard_map/ppermute | solution.py:18
  22.9 1.3 constant_dynamic-slice_fusion.3
  24.3 5.4 %collective-permute-done.5 = bf16[8,32,1024]{2,1,0:T(8,128)(2,1)S(1)} collective-permute-done((bf16[8,32,1024]{2,1,0:T(8,128)(2,1)S(1)}, bf16[8,32,1024]{2,1,0:T(8,128)(2,1)S(1)}, u32[]{:S(2)}, u32[]{:S(2)}) %collective-permute-start.5) | collective-permute-done | bytes 524320 | tf_op jit(solution)/shard_map/ppermute | solution.py:18
  30.1 2.7 %orient.1 = (bf16[2,512,1024]{2,1,0:T(8,128)(2,1)S(1)}, bf16[2,512,1024]{2,1,0:T(8,128)(2,1)S(1)}) custom-call(s32[1]{0:T(128)} %bitcast.6.core, f32[32,2,16,1024]{3,2,1,0:T(8,128)S(1)} %bitcast.20, f32[2,512,1024]{2,1,0:T(8,128)S(1)} %bitcast.21, f32[32,2,16,1024]{3,2,1,0:T(8,128)} %bitcast.9.partner, f32[2,512,1024]{2,1,0:T(8,128)} %bitcast.10.partner_halves), custom_call_target="tpu_custom_call" | custom-call | flops 1048576 | bytes 12582912 | tf_op jit(solution)/shard_map/orient/pallas_call | solution.py:122
  32.8 8.2 %collective-permute-done.2.sum_low = bf16[8,32,1024]{2,1,0:T(8,128)(2,1)S(1)} collective-permute-done((bf16[8,32,1024]{2,1,0:T(8,128)(2,1)S(1)}, bf16[8,32,1024]{2,1,0:T(8,128)(2,1)S(1)}, u32[]{:S(2)}, u32[]{:S(2)}) %collective-permute-start.2) | collective-permute-done | bytes 524320 | tf_op jit(solution)/shard_map/ppermute | solution.py:18
  40.9 1.3 finish_sum.1
  42.2 25.7 %all_to_all.10.columns.own = bf16[32,32,512]{2,1,0:T(8,128)(2,1)S(1)} all-to-all(bf16[32,32,512]{2,1,0:T(8,128)(2,1)S(1)} %bitcast.24), channel_id=1, replica_groups=mesh['dp'=4,'shard'=32] {'shard'}, dimensions={0} | all-to-all | bytes 2097152 | tf_op jit(solution)/shard_map/all_to_all | solution.py:27
  69.1 1.3 share.1.part
  70.6 1.6 %complete.1 = bf16[512,1024]{1,0:T(8,128)(2,1)} custom-call(f32[512,1024]{1,0:T(8,128)S(1)} %share.1.part, bf16[512,512]{1,0:T(8,128)(2,1)S(1)} %collective-permute-done.7.other, bf16[2,512,1024]{2,1,0:T(8,128)(2,1)S(1)} %get-tuple-element.45.right), custom_call_target="tpu_custom_call" | custom-call | flops 536870912 | bytes 4194304 | tf_op jit(solution)/shard_map/complete/pallas_call | solution.py:207
  72.7 3.7 %all-to-all-start.1 = ((bf16[32,16,1024]{2,1,0:T(8,128)(2,1)}), bf16[32,16,1024]{2,1,0:T(8,128)(2,1)S(1)}, u32[]{:S(2)}, u32[]{:S(2)}) async-start(bf16[32,16,1024]{2,1,0:T(8,128)(2,1)} %bitcast.12), calls=%async_computation.1 | async-start | bytes 2097152 | tf_op jit(solution)/shard_map/all_to_all | solution.py:27
  76.4 1.3 constant_dynamic-slice_fusion.old
  77.8 2.2 %copy-done.2 = f32[1,1,1024,1024]{3,2,1,0:T(8,128)S(1)} copy-done((f32[1,1,1024,1024]{3,2,1,0:T(8,128)S(1)}, f32[1,1,1024,1024]{3,2,1,0:T(8,128)}, u32[]{:S(2)}) %copy-start.2) | copy-done | bytes 4194328
  79.9 5.7 %statistics.1 = f32[1024,1024]{1,0:T(8,128)} custom-call(s32[1]{0:T(128)} %bitcast.6.core, bf16[32,32,512]{2,1,0:T(8,128)(2,1)S(1)} %all_to_all.10.columns.own, bf16[32,32,512]{2,1,0:T(8,128)(2,1)} %collective-permute-done.8.other, f32[1024,1024]{1,0:T(8,128)S(1)} %bitcast.23), custom_call_target="tpu_custom_call" | custom-call | flops 2147483648 | bytes 12582912 | tf_op jit(solution)/shard_map/statistics/pallas_call | solution.py:256
  85.6 8.1 %all-to-all-done.1 = bf16[32,16,1024]{2,1,0:T(8,128)(2,1)S(1)} async-done(((bf16[32,16,1024]{2,1,0:T(8,128)(2,1)}), bf16[32,16,1024]{2,1,0:T(8,128)(2,1)S(1)}, u32[]{:S(2)}, u32[]{:S(2)}) %all-to-all-start.1) | async-done | bytes 1048608 | tf_op jit(solution)/shard_map/all_to_all | solution.py:27
  94.5 1.4 %collective-permute-start.9 = (bf16[8,32,1024]{2,1,0:T(8,128)(2,1)S(1)}, bf16[8,32,1024]{2,1,0:T(8,128)(2,1)S(1)}, u32[]{:S(2)}, u32[]{:S(2)}) collective-permute-start(bf16[8,32,1024]{2,1,0:T(8,128)(2,1)S(1)} %get-tuple-element.49), channel_id=1, source_target_pairs={{0,32},{32,64},{64,96},{96,0},{1,33},{33,65},{65,97},{97,1},{2,34}... | collective-permute-start | bytes 1572872 | tf_op jit(solution)/shard_map/ppermute | solution.py:18
  95.9 1.4 %collective-permute-start.11 = (bf16[8,32,1024]{2,1,0:T(8,128)(2,1)S(1)}, bf16[8,32,1024]{2,1,0:T(8,128)(2,1)S(1)}, u32[]{:S(2)}, u32[]{:S(2)}) collective-permute-start(bf16[8,32,1024]{2,1,0:T(8,128)(2,1)S(1)} %get-tuple-element.50), channel_id=1, source_target_pairs={{0,96},{32,0},{64,32},{96,64},{1,97},{33,1},{65,33},{97,65},{2,98}... | collective-permute-start | bytes 1572872 | tf_op jit(solution)/shard_map/ppermute | solution.py:18
  97.4 2.6 %collective-permute-start.14 = (bf16[8,32,1024]{2,1,0:T(8,128)(2,1)S(1)}, bf16[8,32,1024]{2,1,0:T(8,128)(2,1)S(1)}, u32[]{:S(2)}, u32[]{:S(2)}) collective-permute-start(bf16[8,32,1024]{2,1,0:T(8,128)(2,1)S(1)} %get-tuple-element.49), channel_id=1, source_target_pairs={{0,96},{32,0},{64,32},{96,64},{1,97},{33,1},{65,33},{97,65},{2,98}... | collective-permute-start | bytes 1572872 | tf_op jit(solution)/shard_map/ppermute | solution.py:18
  100.0 8.9 %collective-permute-done.9 = bf16[8,32,1024]{2,1,0:T(8,128)(2,1)S(1)} collective-permute-done((bf16[8,32,1024]{2,1,0:T(8,128)(2,1)S(1)}, bf16[8,32,1024]{2,1,0:T(8,128)(2,1)S(1)}, u32[]{:S(2)}, u32[]{:S(2)}) %collective-permute-start.9) | collective-permute-done | bytes 524320 | tf_op jit(solution)/shard_map/ppermute | solution.py:18
  109.6 2.7 %collective-permute-start.12 = (bf16[8,32,1024]{2,1,0:T(8,128)(2,1)S(1)}, bf16[8,32,1024]{2,1,0:T(8,128)(2,1)S(1)}, u32[]{:S(2)}, u32[]{:S(2)}) collective-permute-start(bf16[8,32,1024]{2,1,0:T(8,128)(2,1)S(1)} %collective-permute-done.11), channel_id=1, source_target_pairs={{0,96},{32,0},{64,32},{96,64},{1,97},{33,1},{65,33},{97,65},{2,98}... | collective-permute-start | bytes 1572872 | tf_op jit(solution)/shard_map/ppermute | solution.py:18
  112.4 7.7 %collective-permute-done.13 = bf16[8,32,1024]{2,1,0:T(8,128)(2,1)S(1)} collective-permute-done((bf16[8,32,1024]{2,1,0:T(8,128)(2,1)S(1)}, bf16[8,32,1024]{2,1,0:T(8,128)(2,1)S(1)}, u32[]{:S(2)}, u32[]{:S(2)}) %collective-permute-start.13) | collective-permute-done | bytes 524320 | tf_op jit(solution)/shard_map/ppermute | solution.py:18
  120.3 11.1 %collective-permute-done.10.low_far = bf16[8,32,1024]{2,1,0:T(8,128)(2,1)S(1)} collective-permute-done((bf16[8,32,1024]{2,1,0:T(8,128)(2,1)S(1)}, bf16[8,32,1024]{2,1,0:T(8,128)(2,1)S(1)}, u32[]{:S(2)}, u32[]{:S(2)}) %collective-permute-start.10) | collective-permute-done | bytes 524320 | tf_op jit(solution)/shard_map/ppermute | solution.py:18
  131.4 1.0 settle.1
  (32 shorter events, 5.2 us)
Async XLA Ops:
  0.6 5.7 %copy-start = (s32[4,16]{1,0:T(4,128)S(1)}, s32[4,16]{1,0:T(4,128)}, u32[]{:S(2)}) copy-start(s32[4,16]{1,0:T(4,128)} %param.9) | copy-start | bytes 772
  2.0 8.6 %collective-permute-start = (f32[1024,1024]{1,0:T(8,128)}, f32[1024,1024]{1,0:T(8,128)}, u32[]{:S(2)}, u32[]{:S(2)}) collective-permute-start(f32[1024,1024]{1,0:T(8,128)} %bitcast.19), channel_id=1, source_target_pairs={{0,1},{1,0},{2,3},{3,2},{4,5},{5,4},{6,7},{7,6},{8,9},{9,8},{10,11... | collective-permute-start | bytes 12582920 | tf_op jit(solution)/shard_map/ppermute | solution.py:23
  3.5 15.0 %collective-permute-start.1 = (bf16[8,32,1024]{2,1,0:T(8,128)(2,1)S(1)}, bf16[8,32,1024]{2,1,0:T(8,128)(2,1)S(1)}, u32[]{:S(2)}, u32[]{:S(2)}) collective-permute-start(bf16[8,32,1024]{2,1,0:T(8,128)(2,1)S(1)} %get-tuple-element.27), channel_id=1, source_target_pairs={{0,32},{32,64},{64,96},{96,0},{1,33},{33,65},{65,97},{97,1},{2,34}... | collective-permute-start | bytes 1572872 | tf_op jit(solution)/shard_map/ppermute | solution.py:18
  4.9 13.6 %collective-permute-start.3 = (bf16[8,32,1024]{2,1,0:T(8,128)(2,1)S(1)}, bf16[8,32,1024]{2,1,0:T(8,128)(2,1)S(1)}, u32[]{:S(2)}, u32[]{:S(2)}) collective-permute-start(bf16[8,32,1024]{2,1,0:T(8,128)(2,1)S(1)} %get-tuple-element.28), channel_id=1, source_target_pairs={{0,96},{32,0},{64,32},{96,64},{1,97},{33,1},{65,33},{97,65},{2,98}... | collective-permute-start | bytes 1572872 | tf_op jit(solution)/shard_map/ppermute | solution.py:18
  11.9 18.2 %copy-start.1 = (f32[1,1,1024,1024]{3,2,1,0:T(8,128)S(1)}, f32[1,1,1024,1024]{3,2,1,0:T(8,128)}, u32[]{:S(2)}) copy-start(f32[1,1,1024,1024]{3,2,1,0:T(8,128)} %param.8) | copy-start | bytes 12582916
  11.9 17.8 %collective-permute-start.5 = (bf16[8,32,1024]{2,1,0:T(8,128)(2,1)S(1)}, bf16[8,32,1024]{2,1,0:T(8,128)(2,1)S(1)}, u32[]{:S(2)}, u32[]{:S(2)}) collective-permute-start(bf16[8,32,1024]{2,1,0:T(8,128)(2,1)S(1)} %get-tuple-element.31), channel_id=1, source_target_pairs={{0,32},{32,64},{64,96},{96,0},{1,33},{33,65},{65,97},{97,1},{2,34}... | collective-permute-start | bytes 1572872 | tf_op jit(solution)/shard_map/ppermute | solution.py:18
  13.4 16.3 %collective-permute-start.6 = (bf16[8,32,1024]{2,1,0:T(8,128)(2,1)S(1)}, bf16[8,32,1024]{2,1,0:T(8,128)(2,1)S(1)}, u32[]{:S(2)}, u32[]{:S(2)}) collective-permute-start(bf16[8,32,1024]{2,1,0:T(8,128)(2,1)S(1)} %get-tuple-element.32), channel_id=1, source_target_pairs={{0,96},{32,0},{64,32},{96,64},{1,97},{33,1},{65,33},{97,65},{2,98}... | collective-permute-start | bytes 1572872 | tf_op jit(solution)/shard_map/ppermute | solution.py:18
  20.1 20.9 %collective-permute-start.2 = (bf16[8,32,1024]{2,1,0:T(8,128)(2,1)S(1)}, bf16[8,32,1024]{2,1,0:T(8,128)(2,1)S(1)}, u32[]{:S(2)}, u32[]{:S(2)}) collective-permute-start(bf16[8,32,1024]{2,1,0:T(8,128)(2,1)S(1)} %get-tuple-element.55), channel_id=1, source_target_pairs={{0,32},{32,64},{64,96},{96,0},{1,33},{33,65},{65,97},{97,1},{2,34}... | collective-permute-start | bytes 1572872 | tf_op jit(solution)/shard_map/ppermute | solution.py:18
  21.0 19.9 %collective-permute-start.4 = (bf16[8,32,1024]{2,1,0:T(8,128)(2,1)S(1)}, bf16[8,32,1024]{2,1,0:T(8,128)(2,1)S(1)}, u32[]{:S(2)}, u32[]{:S(2)}) collective-permute-start(bf16[8,32,1024]{2,1,0:T(8,128)(2,1)S(1)} %get-tuple-element.54), channel_id=1, source_target_pairs={{0,96},{32,0},{64,32},{96,64},{1,97},{33,1},{65,33},{97,65},{2,98}... | collective-permute-start | bytes 1572872 | tf_op jit(solution)/shard_map/ppermute | solution.py:18
  68.6 2.0 %collective-permute-start.7 = (bf16[512,512]{1,0:T(8,128)(2,1)S(1)}, bf16[512,512]{1,0:T(8,128)(2,1)S(1)}, u32[]{:S(2)}, u32[]{:S(2)}) collective-permute-start(bf16[512,512]{1,0:T(8,128)(2,1)S(1)} %begin.1), channel_id=1, source_target_pairs={{0,1},{1,0},{2,3},{3,2},{4,5},{5,4},{6,7},{7,6},{8,9},{9,8},{10,11... | collective-permute-start | bytes 1572872 | tf_op jit(solution)/shard_map/ppermute | solution.py:23
  72.2 5.5 %collective-permute-start.8 = (bf16[32,32,512]{2,1,0:T(8,128)(2,1)S(1)}, bf16[32,32,512]{2,1,0:T(8,128)(2,1)}, u32[]{:S(2)}, u32[]{:S(2)}) collective-permute-start(bf16[32,32,512]{2,1,0:T(8,128)(2,1)S(1)} %all_to_all.10.columns.own), channel_id=1, source_target_pairs={{0,1},{1,0},{2,3},{3,2},{4,5},{5,4},{6,7},{7,6},{8,9},{9,8},{10,11... | collective-permute-start | bytes 3145736 | tf_op jit(solution)/shard_map/ppermute | solution.py:23
  72.7 21.0 %all-to-all-start.1 = ((bf16[32,16,1024]{2,1,0:T(8,128)(2,1)}), bf16[32,16,1024]{2,1,0:T(8,128)(2,1)S(1)}, u32[]{:S(2)}, u32[]{:S(2)}) async-start(bf16[32,16,1024]{2,1,0:T(8,128)(2,1)} %bitcast.12), calls=%async_computation.1 | async-start | bytes 2097152 | tf_op jit(solution)/shard_map/all_to_all | solution.py:27
  77.7 2.2 %copy-start.2 = (f32[1,1,1024,1024]{3,2,1,0:T(8,128)S(1)}, f32[1,1,1024,1024]{3,2,1,0:T(8,128)}, u32[]{:S(2)}) copy-start(f32[1,1,1024,1024]{3,2,1,0:T(8,128)} %param.7) | copy-start | bytes 12582916
  94.5 14.4 %collective-permute-start.9 = (bf16[8,32,1024]{2,1,0:T(8,128)(2,1)S(1)}, bf16[8,32,1024]{2,1,0:T(8,128)(2,1)S(1)}, u32[]{:S(2)}, u32[]{:S(2)}) collective-permute-start(bf16[8,32,1024]{2,1,0:T(8,128)(2,1)S(1)} %get-tuple-element.49), channel_id=1, source_target_pairs={{0,32},{32,64},{64,96},{96,0},{1,33},{33,65},{65,97},{97,1},{2,34}... | collective-permute-start | bytes 1572872 | tf_op jit(solution)/shard_map/ppermute | solution.py:18
  95.9 13.7 %collective-permute-start.11 = (bf16[8,32,1024]{2,1,0:T(8,128)(2,1)S(1)}, bf16[8,32,1024]{2,1,0:T(8,128)(2,1)S(1)}, u32[]{:S(2)}, u32[]{:S(2)}) collective-permute-start(bf16[8,32,1024]{2,1,0:T(8,128)(2,1)S(1)} %get-tuple-element.50), channel_id=1, source_target_pairs={{0,96},{32,0},{64,32},{96,64},{1,97},{33,1},{65,33},{97,65},{2,98}... | collective-permute-start | bytes 1572872 | tf_op jit(solution)/shard_map/ppermute | solution.py:18
  97.3 22.8 %collective-permute-start.13 = (bf16[8,32,1024]{2,1,0:T(8,128)(2,1)S(1)}, bf16[8,32,1024]{2,1,0:T(8,128)(2,1)S(1)}, u32[]{:S(2)}, u32[]{:S(2)}) collective-permute-start(bf16[8,32,1024]{2,1,0:T(8,128)(2,1)S(1)} %get-tuple-element.50), channel_id=1, source_target_pairs={{0,32},{32,64},{64,96},{96,0},{1,33},{33,65},{65,97},{97,1},{2,34}... | collective-permute-start | bytes 1572872 | tf_op jit(solution)/shard_map/ppermute | solution.py:18
  97.4 22.8 %collective-permute-start.14 = (bf16[8,32,1024]{2,1,0:T(8,128)(2,1)S(1)}, bf16[8,32,1024]{2,1,0:T(8,128)(2,1)S(1)}, u32[]{:S(2)}, u32[]{:S(2)}) collective-permute-start(bf16[8,32,1024]{2,1,0:T(8,128)(2,1)S(1)} %get-tuple-element.49), channel_id=1, source_target_pairs={{0,96},{32,0},{64,32},{96,64},{1,97},{33,1},{65,33},{97,65},{2,98}... | collective-permute-start | bytes 1572872 | tf_op jit(solution)/shard_map/ppermute | solution.py:18
  108.9 22.5 %collective-permute-start.10 = (bf16[8,32,1024]{2,1,0:T(8,128)(2,1)S(1)}, bf16[8,32,1024]{2,1,0:T(8,128)(2,1)S(1)}, u32[]{:S(2)}, u32[]{:S(2)}) collective-permute-start(bf16[8,32,1024]{2,1,0:T(8,128)(2,1)S(1)} %collective-permute-done.9), channel_id=1, source_target_pairs={{0,32},{32,64},{64,96},{96,0},{1,33},{33,65},{65,97},{97,1},{2,34}... | collective-permute-start | bytes 1572872 | tf_op jit(solution)/shard_map/ppermute | solution.py:18
  109.6 21.8 %collective-permute-start.12 = (bf16[8,32,1024]{2,1,0:T(8,128)(2,1)S(1)}, bf16[8,32,1024]{2,1,0:T(8,128)(2,1)S(1)}, u32[]{:S(2)}, u32[]{:S(2)}) collective-permute-start(bf16[8,32,1024]{2,1,0:T(8,128)(2,1)S(1)} %collective-permute-done.11), channel_id=1, source_target_pairs={{0,96},{32,0},{64,32},{96,64},{1,97},{33,1},{65,33},{97,65},{2,98}... | collective-permute-start | bytes 1572872 | tf_op jit(solution)/shard_map/ppermute | solution.py:18
  120.3 11.1 %copy-start.3 = (bf16[64,32,1024]{2,1,0:T(8,128)(2,1)}, bf16[64,32,1024]{2,1,0:T(8,128)(2,1)S(1)}, u32[]{:S(2)}) copy-start(bf16[64,32,1024]{2,1,0:T(8,128)(2,1)S(1)} %constant_dynamic-update-slice_fusion.below) | copy-start | bytes 12582916

commit v8 on v6

--- a/solution.py
+++ b/solution.py
@@ -169,14 +169,14 @@
     for low in range(0, size, tile):
         part[:, low : low + tile] = jnp.dot(
             kept[...], right[0, :, low : low + tile], preferred_element_type=f32
-        )
+        ).astype(bf16)
 
 
 def shared(left, columns, right):
     half, size = right.shape[1:]
     return pl.pallas_call(
         share_kernel,
-        out_shape=jax.ShapeDtypeStruct((half, size), f32),
+        out_shape=jax.ShapeDtypeStruct((half, size), bf16),
         in_specs=[whole_in(pltpu.VMEM)] * 3,
         out_specs=whole_in(pltpu.VMEM),
         scratch_shapes=[pltpu.VMEM((half, half), bf16)],
@@ -193,7 +193,7 @@
     for index, low in enumerate(range(0, size, width)):
         columns = slice(low, low + width)
         product = jnp.dot(other[...], right[1, :, columns], preferred_element_type=f32)
-        made[:, columns] = (part[:, columns] + product).astype(bf16)
+        made[:, columns] = (part[:, columns].astype(f32) + product).astype(bf16)
         copies.append(
             pltpu.make_async_copy(made.at[:, columns], update.at[:, columns], sems.at[index])
         )

time: 133 us -> 133 us (level)
  no operation moved by 1% of the time
where the time goes in v8:
time: 133 us; the launch traced here: 132 us
  waiting for transfers between devices  57.6 us (43%)
  blocking collectives  25.7 us (19%)
  starting transfers between devices  22.9 us (17%)
  Pallas kernels  15 us (11%)
  local copies, waits for them, and re-layouts  8.22 us (6%)
  other arithmetic  2.12 us (2%)
    ppermute x12, waiting for transfers between devices, shifted(): lax.ppermute(block, axis, [(i, (i + offset) % count) for i in range(count)])  44.9 us
    all_to_all x1, blocking collectives, exchanged(): lax.all_to_all(blocks, 'shard', split_axis=0, concat_axis=0, tiled=True)  25.7 us
    ppermute x12, starting transfers between devices, shifted(): lax.ppermute(block, axis, [(i, (i + offset) % count) for i in range(count)])  16.7 us
    all_to_all x1, waiting for transfers between devices, exchanged(): lax.all_to_all(blocks, 'shard', split_axis=0, concat_axis=0, tiled=True)  8.06 us
    pallas_call x1, Pallas kernels, statistics(): pl.pallas_call(statistics_kernel, grid=(size // tile,), out_shape=jax.Sha...  5.69 us
    ppermute x3, waiting for transfers between devices, other_core(): return lax.ppermute(block, 'shard', [(i, i ^ 1) for i in range(count)])  4.58 us
    all_to_all x1, starting transfers between devices, exchanged(): lax.all_to_all(blocks, 'shard', split_axis=0, concat_axis=0, tiled=True)  3.73 us
  transfers between devices with their start and end apart: 16, of which 9 were waited for; matrix products, arithmetic and copies ran while one was open for 5% of the time, Pallas kernels for 7%

profile of v8, /device:TPU:1, one launch (start us, length us, event | category | flops | bytes accessed | tf_op | source)
XLA Modules:
  0.0 132.4 jit_solution(6858482859132465012)
XLA Ops:
  0.7 1.3 dynamic-slice_bitcast_fusion
  2.0 1.5 %collective-permute-start = (f32[1024,1024]{1,0:T(8,128)}, f32[1024,1024]{1,0:T(8,128)}, u32[]{:S(2)}, u32[]{:S(2)}) collective-permute-start(f32[1024,1024]{1,0:T(8,128)} %bitcast.19), channel_id=1, source_target_pairs={{0,1},{1,0},{2,3},{3,2},{4,5},{5,4},{6,7},{7,6},{8,9},{9,8},{10,11... | collective-permute-start | bytes 12582920 | tf_op jit(solution)/shard_map/ppermute | solution.py:23
  3.5 1.4 %collective-permute-start.1 = (bf16[8,32,1024]{2,1,0:T(8,128)(2,1)S(1)}, bf16[8,32,1024]{2,1,0:T(8,128)(2,1)S(1)}, u32[]{:S(2)}, u32[]{:S(2)}) collective-permute-start(bf16[8,32,1024]{2,1,0:T(8,128)(2,1)S(1)} %get-tuple-element.29), channel_id=1, source_target_pairs={{0,32},{32,64},{64,96},{96,0},{1,33},{33,65},{65,97},{97,1},{2,34}... | collective-permute-start | bytes 1572872 | tf_op jit(solution)/shard_map/ppermute | solution.py:18
  4.9 1.4 %collective-permute-start.2 = (bf16[8,32,1024]{2,1,0:T(8,128)(2,1)S(1)}, bf16[8,32,1024]{2,1,0:T(8,128)(2,1)S(1)}, u32[]{:S(2)}, u32[]{:S(2)}) collective-permute-start(bf16[8,32,1024]{2,1,0:T(8,128)(2,1)S(1)} %get-tuple-element.30), channel_id=1, source_target_pairs={{0,96},{32,0},{64,32},{96,64},{1,97},{33,1},{65,33},{97,65},{2,98}... | collective-permute-start | bytes 1572872 | tf_op jit(solution)/shard_map/ppermute | solution.py:18
  6.3 4.3 %collective-permute-done = f32[1024,1024]{1,0:T(8,128)} collective-permute-done((f32[1024,1024]{1,0:T(8,128)}, f32[1024,1024]{1,0:T(8,128)}, u32[]{:S(2)}, u32[]{:S(2)}) %collective-permute-start) | collective-permute-done | bytes 4194336 | tf_op jit(solution)/shard_map/ppermute | solution.py:23
  10.6 1.3 constant_dynamic-slice_fusion.1
  11.9 1.4 %collective-permute-start.5 = (bf16[8,32,1024]{2,1,0:T(8,128)(2,1)S(1)}, bf16[8,32,1024]{2,1,0:T(8,128)(2,1)S(1)}, u32[]{:S(2)}, u32[]{:S(2)}) collective-permute-start(bf16[8,32,1024]{2,1,0:T(8,128)(2,1)S(1)} %get-tuple-element.35), channel_id=1, source_target_pairs={{0,32},{32,64},{64,96},{96,0},{1,33},{33,65},{65,97},{97,1},{2,34}... | collective-permute-start | bytes 1572872 | tf_op jit(solution)/shard_map/ppermute | solution.py:18
  13.4 1.5 %collective-permute-start.6 = (bf16[8,32,1024]{2,1,0:T(8,128)(2,1)S(1)}, bf16[8,32,1024]{2,1,0:T(8,128)(2,1)S(1)}, u32[]{:S(2)}, u32[]{:S(2)}) collective-permute-start(bf16[8,32,1024]{2,1,0:T(8,128)(2,1)S(1)} %get-tuple-element.36), channel_id=1, source_target_pairs={{0,96},{32,0},{64,32},{96,64},{1,97},{33,1},{65,33},{97,65},{2,98}... | collective-permute-start | bytes 1572872 | tf_op jit(solution)/shard_map/ppermute | solution.py:18
  14.9 3.6 %collective-permute-done.1 = bf16[8,32,1024]{2,1,0:T(8,128)(2,1)S(1)} collective-permute-done((bf16[8,32,1024]{2,1,0:T(8,128)(2,1)S(1)}, bf16[8,32,1024]{2,1,0:T(8,128)(2,1)S(1)}, u32[]{:S(2)}, u32[]{:S(2)}) %collective-permute-start.1) | collective-permute-done | bytes 524320 | tf_op jit(solution)/shard_map/ppermute | solution.py:18
  18.5 1.6 %add_convert_fusion.2 = (bf16[8,32,1024]{2,1,0:T(8,128)(2,1)S(1)}, bf16[8,32,1024]{2,1,0:T(8,128)(2,1)S(1)}) fusion(bf16[8,32,1024]{2,1,0:T(8,128)(2,1)S(1)} %collective-permute-done.2, bf16[64,32,1024]{2,1,0:T(8,128)(2,1)} %bitcast.27, s32[]{:T(128)S(6)} %select_n.87, bf16[8,32,1024]{2,1,0:T(8,128)(2,1)S(1)} %collective-permute-done.1, s32[]{:T(128)S(6)} %select_n.85), kind=kLoop, calls=%fused_computation.2 | loop fusion | flops 2097152 | bytes 3145736 | tf_op jit(solution)/shard_map/convert_element_type | solution.py:34
  21.0 1.8 %collective-permute-start.4 = (bf16[8,32,1024]{2,1,0:T(8,128)(2,1)S(1)}, bf16[8,32,1024]{2,1,0:T(8,128)(2,1)S(1)}, u32[]{:S(2)}, u32[]{:S(2)}) collective-permute-start(bf16[8,32,1024]{2,1,0:T(8,128)(2,1)S(1)} %get-tuple-element.34), channel_id=1, source_target_pairs={{0,96},{32,0},{64,32},{96,64},{1,97},{33,1},{65,33},{97,65},{2,98}... | collective-permute-start | bytes 1572872 | tf_op jit(solution)/shard_map/ppermute | solution.py:18
  22.9 1.3 constant_dynamic-slice_fusion.3
  24.3 5.4 %collective-permute-done.5 = bf16[8,32,1024]{2,1,0:T(8,128)(2,1)S(1)} collective-permute-done((bf16[8,32,1024]{2,1,0:T(8,128)(2,1)S(1)}, bf16[8,32,1024]{2,1,0:T(8,128)(2,1)S(1)}, u32[]{:S(2)}, u32[]{:S(2)}) %collective-permute-start.5) | collective-permute-done | bytes 524320 | tf_op jit(solution)/shard_map/ppermute | solution.py:18
  30.1 2.7 %orient.1 = (bf16[2,512,1024]{2,1,0:T(8,128)(2,1)S(1)}, bf16[2,512,1024]{2,1,0:T(8,128)(2,1)S(1)}) custom-call(s32[1]{0:T(128)} %bitcast.6.core, f32[32,2,16,1024]{3,2,1,0:T(8,128)S(1)} %bitcast.20, f32[2,512,1024]{2,1,0:T(8,128)S(1)} %bitcast.21, f32[32,2,16,1024]{3,2,1,0:T(8,128)} %bitcast.9.partner, f32[2,512,1024]{2,1,0:T(8,128)} %bitcast.10.partner_halves), custom_call_target="tpu_custom_call" | custom-call | flops 1048576 | bytes 12582912 | tf_op jit(solution)/shard_map/orient/pallas_call | solution.py:122
  32.8 8.2 %collective-permute-done.3.sum_low = bf16[8,32,1024]{2,1,0:T(8,128)(2,1)S(1)} collective-permute-done((bf16[8,32,1024]{2,1,0:T(8,128)(2,1)S(1)}, bf16[8,32,1024]{2,1,0:T(8,128)(2,1)S(1)}, u32[]{:S(2)}, u32[]{:S(2)}) %collective-permute-start.3) | collective-permute-done | bytes 524320 | tf_op jit(solution)/shard_map/ppermute | solution.py:18
  40.9 1.3 finish_sum.1
  42.2 25.7 %all_to_all.10.columns.own = bf16[32,32,512]{2,1,0:T(8,128)(2,1)S(1)} all-to-all(bf16[32,32,512]{2,1,0:T(8,128)(2,1)S(1)} %bitcast.24), channel_id=1, replica_groups=mesh['dp'=4,'shard'=32] {'shard'}, dimensions={0} | all-to-all | bytes 2097152 | tf_op jit(solution)/shard_map/all_to_all | solution.py:27
  69.1 1.2 share.1.part
  70.6 1.6 %complete.1 = bf16[512,1024]{1,0:T(8,128)(2,1)} custom-call(bf16[512,1024]{1,0:T(8,128)(2,1)S(1)} %share.1.part, bf16[512,512]{1,0:T(8,128)(2,1)S(1)} %collective-permute-done.7.other, bf16[2,512,1024]{2,1,0:T(8,128)(2,1)S(1)} %get-tuple-element.49.right), custom_call_target="tpu_custom_call" | custom-call | flops 536870912 | bytes 4194304 | tf_op jit(solution)/shard_map/complete/pallas_call | solution.py:207
  72.7 3.7 %all-to-all-start.1 = ((bf16[32,16,1024]{2,1,0:T(8,128)(2,1)}), bf16[32,16,1024]{2,1,0:T(8,128)(2,1)S(1)}, u32[]{:S(2)}, u32[]{:S(2)}) async-start(bf16[32,16,1024]{2,1,0:T(8,128)(2,1)} %bitcast.12), calls=%async_computation.1 | async-start | bytes 2097152 | tf_op jit(solution)/shard_map/all_to_all | solution.py:27
  76.4 1.3 constant_dynamic-slice_fusion.old
  77.8 2.2 %copy-done.2 = f32[1,1,1024,1024]{3,2,1,0:T(8,128)S(1)} copy-done((f32[1,1,1024,1024]{3,2,1,0:T(8,128)S(1)}, f32[1,1,1024,1024]{3,2,1,0:T(8,128)}, u32[]{:S(2)}) %copy-start.2) | copy-done | bytes 4194328
  79.9 5.7 %statistics.1 = f32[1024,1024]{1,0:T(8,128)} custom-call(s32[1]{0:T(128)} %bitcast.6.core, bf16[32,32,512]{2,1,0:T(8,128)(2,1)S(1)} %all_to_all.10.columns.own, bf16[32,32,512]{2,1,0:T(8,128)(2,1)} %collective-permute-done.8.other, f32[1024,1024]{1,0:T(8,128)S(1)} %bitcast.23), custom_call_target="tpu_custom_call" | custom-call | flops 2147483648 | bytes 12582912 | tf_op jit(solution)/shard_map/statistics/pallas_call | solution.py:256
  85.6 8.1 %all-to-all-done.1 = bf16[32,16,1024]{2,1,0:T(8,128)(2,1)S(1)} async-done(((bf16[32,16,1024]{2,1,0:T(8,128)(2,1)}), bf16[32,16,1024]{2,1,0:T(8,128)(2,1)S(1)}, u32[]{:S(2)}, u32[]{:S(2)}) %all-to-all-start.1) | async-done | bytes 1048608 | tf_op jit(solution)/shard_map/all_to_all | solution.py:27
  94.5 1.4 %collective-permute-start.9 = (bf16[8,32,1024]{2,1,0:T(8,128)(2,1)S(1)}, bf16[8,32,1024]{2,1,0:T(8,128)(2,1)S(1)}, u32[]{:S(2)}, u32[]{:S(2)}) collective-permute-start(bf16[8,32,1024]{2,1,0:T(8,128)(2,1)S(1)} %get-tuple-element.53), channel_id=1, source_target_pairs={{0,32},{32,64},{64,96},{96,0},{1,33},{33,65},{65,97},{97,1},{2,34}... | collective-permute-start | bytes 1572872 | tf_op jit(solution)/shard_map/ppermute | solution.py:18
  95.9 1.4 %collective-permute-start.11 = (bf16[8,32,1024]{2,1,0:T(8,128)(2,1)S(1)}, bf16[8,32,1024]{2,1,0:T(8,128)(2,1)S(1)}, u32[]{:S(2)}, u32[]{:S(2)}) collective-permute-start(bf16[8,32,1024]{2,1,0:T(8,128)(2,1)S(1)} %get-tuple-element.54), channel_id=1, source_target_pairs={{0,96},{32,0},{64,32},{96,64},{1,97},{33,1},{65,33},{97,65},{2,98}... | collective-permute-start | bytes 1572872 | tf_op jit(solution)/shard_map/ppermute | solution.py:18
  97.4 2.6 %collective-permute-start.14 = (bf16[8,32,1024]{2,1,0:T(8,128)(2,1)S(1)}, bf16[8,32,1024]{2,1,0:T(8,128)(2,1)S(1)}, u32[]{:S(2)}, u32[]{:S(2)}) collective-permute-start(bf16[8,32,1024]{2,1,0:T(8,128)(2,1)S(1)} %get-tuple-element.53), channel_id=1, source_target_pairs={{0,96},{32,0},{64,32},{96,64},{1,97},{33,1},{65,33},{97,65},{2,98}... | collective-permute-start | bytes 1572872 | tf_op jit(solution)/shard_map/ppermute | solution.py:18
  100.0 8.9 %collective-permute-done.9 = bf16[8,32,1024]{2,1,0:T(8,128)(2,1)S(1)} collective-permute-done((bf16[8,32,1024]{2,1,0:T(8,128)(2,1)S(1)}, bf16[8,32,1024]{2,1,0:T(8,128)(2,1)S(1)}, u32[]{:S(2)}, u32[]{:S(2)}) %collective-permute-start.9) | collective-permute-done | bytes 524320 | tf_op jit(solution)/shard_map/ppermute | solution.py:18
  109.6 2.7 %collective-permute-start.12 = (bf16[8,32,1024]{2,1,0:T(8,128)(2,1)S(1)}, bf16[8,32,1024]{2,1,0:T(8,128)(2,1)S(1)}, u32[]{:S(2)}, u32[]{:S(2)}) collective-permute-start(bf16[8,32,1024]{2,1,0:T(8,128)(2,1)S(1)} %collective-permute-done.11), channel_id=1, source_target_pairs={{0,96},{32,0},{64,32},{96,64},{1,97},{33,1},{65,33},{97,65},{2,98}... | collective-permute-start | bytes 1572872 | tf_op jit(solution)/shard_map/ppermute | solution.py:18
  112.4 7.7 %collective-permute-done.13 = bf16[8,32,1024]{2,1,0:T(8,128)(2,1)S(1)} collective-permute-done((bf16[8,32,1024]{2,1,0:T(8,128)(2,1)S(1)}, bf16[8,32,1024]{2,1,0:T(8,128)(2,1)S(1)}, u32[]{:S(2)}, u32[]{:S(2)}) %collective-permute-start.13) | collective-permute-done | bytes 524320 | tf_op jit(solution)/shard_map/ppermute | solution.py:18
  120.3 11.1 %collective-permute-done.10.low_far = bf16[8,32,1024]{2,1,0:T(8,128)(2,1)S(1)} collective-permute-done((bf16[8,32,1024]{2,1,0:T(8,128)(2,1)S(1)}, bf16[8,32,1024]{2,1,0:T(8,128)(2,1)S(1)}, u32[]{:S(2)}, u32[]{:S(2)}) %collective-permute-start.10) | collective-permute-done | bytes 524320 | tf_op jit(solution)/shard_map/ppermute | solution.py:18
  131.4 1.0 settle.1
  (32 shorter events, 5.2 us)
Async XLA Ops:
  0.6 5.7 %copy-start = (s32[4,16]{1,0:T(4,128)S(1)}, s32[4,16]{1,0:T(4,128)}, u32[]{:S(2)}) copy-start(s32[4,16]{1,0:T(4,128)} %param.9) | copy-start | bytes 772
  2.0 8.6 %collective-permute-start = (f32[1024,1024]{1,0:T(8,128)}, f32[1024,1024]{1,0:T(8,128)}, u32[]{:S(2)}, u32[]{:S(2)}) collective-permute-start(f32[1024,1024]{1,0:T(8,128)} %bitcast.19), channel_id=1, source_target_pairs={{0,1},{1,0},{2,3},{3,2},{4,5},{5,4},{6,7},{7,6},{8,9},{9,8},{10,11... | collective-permute-start | bytes 12582920 | tf_op jit(solution)/shard_map/ppermute | solution.py:23
  3.5 15.0 %collective-permute-start.1 = (bf16[8,32,1024]{2,1,0:T(8,128)(2,1)S(1)}, bf16[8,32,1024]{2,1,0:T(8,128)(2,1)S(1)}, u32[]{:S(2)}, u32[]{:S(2)}) collective-permute-start(bf16[8,32,1024]{2,1,0:T(8,128)(2,1)S(1)} %get-tuple-element.29), channel_id=1, source_target_pairs={{0,32},{32,64},{64,96},{96,0},{1,33},{33,65},{65,97},{97,1},{2,34}... | collective-permute-start | bytes 1572872 | tf_op jit(solution)/shard_map/ppermute | solution.py:18
  4.9 13.6 %collective-permute-start.2 = (bf16[8,32,1024]{2,1,0:T(8,128)(2,1)S(1)}, bf16[8,32,1024]{2,1,0:T(8,128)(2,1)S(1)}, u32[]{:S(2)}, u32[]{:S(2)}) collective-permute-start(bf16[8,32,1024]{2,1,0:T(8,128)(2,1)S(1)} %get-tuple-element.30), channel_id=1, source_target_pairs={{0,96},{32,0},{64,32},{96,64},{1,97},{33,1},{65,33},{97,65},{2,98}... | collective-permute-start | bytes 1572872 | tf_op jit(solution)/shard_map/ppermute | solution.py:18
  11.9 18.2 %copy-start.1 = (f32[1,1,1024,1024]{3,2,1,0:T(8,128)S(1)}, f32[1,1,1024,1024]{3,2,1,0:T(8,128)}, u32[]{:S(2)}) copy-start(f32[1,1,1024,1024]{3,2,1,0:T(8,128)} %param.8) | copy-start | bytes 12582916
  11.9 17.8 %collective-permute-start.5 = (bf16[8,32,1024]{2,1,0:T(8,128)(2,1)S(1)}, bf16[8,32,1024]{2,1,0:T(8,128)(2,1)S(1)}, u32[]{:S(2)}, u32[]{:S(2)}) collective-permute-start(bf16[8,32,1024]{2,1,0:T(8,128)(2,1)S(1)} %get-tuple-element.35), channel_id=1, source_target_pairs={{0,32},{32,64},{64,96},{96,0},{1,33},{33,65},{65,97},{97,1},{2,34}... | collective-permute-start | bytes 1572872 | tf_op jit(solution)/shard_map/ppermute | solution.py:18
  13.4 16.3 %collective-permute-start.6 = (bf16[8,32,1024]{2,1,0:T(8,128)(2,1)S(1)}, bf16[8,32,1024]{2,1,0:T(8,128)(2,1)S(1)}, u32[]{:S(2)}, u32[]{:S(2)}) collective-permute-start(bf16[8,32,1024]{2,1,0:T(8,128)(2,1)S(1)} %get-tuple-element.36), channel_id=1, source_target_pairs={{0,96},{32,0},{64,32},{96,64},{1,97},{33,1},{65,33},{97,65},{2,98}... | collective-permute-start | bytes 1572872 | tf_op jit(solution)/shard_map/ppermute | solution.py:18
  20.1 20.9 %collective-permute-start.3 = (bf16[8,32,1024]{2,1,0:T(8,128)(2,1)S(1)}, bf16[8,32,1024]{2,1,0:T(8,128)(2,1)S(1)}, u32[]{:S(2)}, u32[]{:S(2)}) collective-permute-start(bf16[8,32,1024]{2,1,0:T(8,128)(2,1)S(1)} %get-tuple-element.33), channel_id=1, source_target_pairs={{0,32},{32,64},{64,96},{96,0},{1,33},{33,65},{65,97},{97,1},{2,34}... | collective-permute-start | bytes 1572872 | tf_op jit(solution)/shard_map/ppermute | solution.py:18
  21.0 19.9 %collective-permute-start.4 = (bf16[8,32,1024]{2,1,0:T(8,128)(2,1)S(1)}, bf16[8,32,1024]{2,1,0:T(8,128)(2,1)S(1)}, u32[]{:S(2)}, u32[]{:S(2)}) collective-permute-start(bf16[8,32,1024]{2,1,0:T(8,128)(2,1)S(1)} %get-tuple-element.34), channel_id=1, source_target_pairs={{0,96},{32,0},{64,32},{96,64},{1,97},{33,1},{65,33},{97,65},{2,98}... | collective-permute-start | bytes 1572872 | tf_op jit(solution)/shard_map/ppermute | solution.py:18
  68.6 2.0 %collective-permute-start.7 = (bf16[512,512]{1,0:T(8,128)(2,1)S(1)}, bf16[512,512]{1,0:T(8,128)(2,1)S(1)}, u32[]{:S(2)}, u32[]{:S(2)}) collective-permute-start(bf16[512,512]{1,0:T(8,128)(2,1)S(1)} %begin.1), channel_id=1, source_target_pairs={{0,1},{1,0},{2,3},{3,2},{4,5},{5,4},{6,7},{7,6},{8,9},{9,8},{10,11... | collective-permute-start | bytes 1572872 | tf_op jit(solution)/shard_map/ppermute | solution.py:23
  72.2 5.5 %collective-permute-start.8 = (bf16[32,32,512]{2,1,0:T(8,128)(2,1)S(1)}, bf16[32,32,512]{2,1,0:T(8,128)(2,1)}, u32[]{:S(2)}, u32[]{:S(2)}) collective-permute-start(bf16[32,32,512]{2,1,0:T(8,128)(2,1)S(1)} %all_to_all.10.columns.own), channel_id=1, source_target_pairs={{0,1},{1,0},{2,3},{3,2},{4,5},{5,4},{6,7},{7,6},{8,9},{9,8},{10,11... | collective-permute-start | bytes 3145736 | tf_op jit(solution)/shard_map/ppermute | solution.py:23
  72.7 21.0 %all-to-all-start.1 = ((bf16[32,16,1024]{2,1,0:T(8,128)(2,1)}), bf16[32,16,1024]{2,1,0:T(8,128)(2,1)S(1)}, u32[]{:S(2)}, u32[]{:S(2)}) async-start(bf16[32,16,1024]{2,1,0:T(8,128)(2,1)} %bitcast.12), calls=%async_computation.1 | async-start | bytes 2097152 | tf_op jit(solution)/shard_map/all_to_all | solution.py:27
  77.7 2.2 %copy-start.2 = (f32[1,1,1024,1024]{3,2,1,0:T(8,128)S(1)}, f32[1,1,1024,1024]{3,2,1,0:T(8,128)}, u32[]{:S(2)}) copy-start(f32[1,1,1024,1024]{3,2,1,0:T(8,128)} %param.7) | copy-start | bytes 12582916
  94.5 14.4 %collective-permute-start.9 = (bf16[8,32,1024]{2,1,0:T(8,128)(2,1)S(1)}, bf16[8,32,1024]{2,1,0:T(8,128)(2,1)S(1)}, u32[]{:S(2)}, u32[]{:S(2)}) collective-permute-start(bf16[8,32,1024]{2,1,0:T(8,128)(2,1)S(1)} %get-tuple-element.53), channel_id=1, source_target_pairs={{0,32},{32,64},{64,96},{96,0},{1,33},{33,65},{65,97},{97,1},{2,34}... | collective-permute-start | bytes 1572872 | tf_op jit(solution)/shard_map/ppermute | solution.py:18
  95.9 13.7 %collective-permute-start.11 = (bf16[8,32,1024]{2,1,0:T(8,128)(2,1)S(1)}, bf16[8,32,1024]{2,1,0:T(8,128)(2,1)S(1)}, u32[]{:S(2)}, u32[]{:S(2)}) collective-permute-start(bf16[8,32,1024]{2,1,0:T(8,128)(2,1)S(1)} %get-tuple-element.54), channel_id=1, source_target_pairs={{0,96},{32,0},{64,32},{96,64},{1,97},{33,1},{65,33},{97,65},{2,98}... | collective-permute-start | bytes 1572872 | tf_op jit(solution)/shard_map/ppermute | solution.py:18
  97.3 22.8 %collective-permute-start.13 = (bf16[8,32,1024]{2,1,0:T(8,128)(2,1)S(1)}, bf16[8,32,1024]{2,1,0:T(8,128)(2,1)S(1)}, u32[]{:S(2)}, u32[]{:S(2)}) collective-permute-start(bf16[8,32,1024]{2,1,0:T(8,128)(2,1)S(1)} %get-tuple-element.54), channel_id=1, source_target_pairs={{0,32},{32,64},{64,96},{96,0},{1,33},{33,65},{65,97},{97,1},{2,34}... | collective-permute-start | bytes 1572872 | tf_op jit(solution)/shard_map/ppermute | solution.py:18
  97.4 22.8 %collective-permute-start.14 = (bf16[8,32,1024]{2,1,0:T(8,128)(2,1)S(1)}, bf16[8,32,1024]{2,1,0:T(8,128)(2,1)S(1)}, u32[]{:S(2)}, u32[]{:S(2)}) collective-permute-start(bf16[8,32,1024]{2,1,0:T(8,128)(2,1)S(1)} %get-tuple-element.53), channel_id=1, source_target_pairs={{0,96},{32,0},{64,32},{96,64},{1,97},{33,1},{65,33},{97,65},{2,98}... | collective-permute-start | bytes 1572872 | tf_op jit(solution)/shard_map/ppermute | solution.py:18
  108.9 22.5 %collective-permute-start.10 = (bf16[8,32,1024]{2,1,0:T(8,128)(2,1)S(1)}, bf16[8,32,1024]{2,1,0:T(8,128)(2,1)S(1)}, u32[]{:S(2)}, u32[]{:S(2)}) collective-permute-start(bf16[8,32,1024]{2,1,0:T(8,128)(2,1)S(1)} %collective-permute-done.9), channel_id=1, source_target_pairs={{0,32},{32,64},{64,96},{96,0},{1,33},{33,65},{65,97},{97,1},{2,34}... | collective-permute-start | bytes 1572872 | tf_op jit(solution)/shard_map/ppermute | solution.py:18
  109.6 21.8 %collective-permute-start.12 = (bf16[8,32,1024]{2,1,0:T(8,128)(2,1)S(1)}, bf16[8,32,1024]{2,1,0:T(8,128)(2,1)S(1)}, u32[]{:S(2)}, u32[]{:S(2)}) collective-permute-start(bf16[8,32,1024]{2,1,0:T(8,128)(2,1)S(1)} %collective-permute-done.11), channel_id=1, source_target_pairs={{0,96},{32,0},{64,32},{96,64},{1,97},{33,1},{65,33},{97,65},{2,98}... | collective-permute-start | bytes 1572872 | tf_op jit(solution)/shard_map/ppermute | solution.py:18
  120.3 11.1 %copy-start.3 = (bf16[64,32,1024]{2,1,0:T(8,128)(2,1)}, bf16[64,32,1024]{2,1,0:T(8,128)(2,1)S(1)}, u32[]{:S(2)}) copy-start(bf16[64,32,1024]{2,1,0:T(8,128)(2,1)S(1)} %constant_dynamic-update-slice_fusion.below) | copy-start | bytes 12582916
